TPU v7x, 256 devices: a whole 4x4x8 slice. The times are simulated.
256 devices in a mesh: dp: 8 (over z), own: 32 (over y, x, core).
Axes of the slice: x: 4, y: 4, z: 8, core: 2. Of those that a mesh axis runs over, the one named last changes fastest.
Arguments:
- partials: bfloat16 [8, 96, 1024, 1024], P('dp', 'own'), may hold values from -0.125 to 0.125
- active_mask: int32 [96], replicated, may hold values from 0 to 1, as said below
- block_owner: int32 [96], replicated, may hold values from 0 to 31, as said below
- left_stats: float32 [64, 1024, 1024], P('own', 'dp'), may hold values from -6 to 6
- right_stats: float32 [64, 1024, 1024], P('own', 'dp'), may hold values from -6 to 6
- left_root: bfloat16 [64, 1024, 1024], P('own', 'dp'), may hold values from -0.4375 to 0.4375
- right_root: bfloat16 [64, 1024, 1024], P('own', 'dp'), may hold values from -0.4375 to 0.4375
Outputs:
- preconditioned: bfloat16 [96, 1024, 1024], P('own', 'dp')
- left_new: float32 [64, 1024, 1024], P('own', 'dp')
- right_new: float32 [64, 1024, 1024], P('own', 'dp')
Inputs may be any that keep to these rules, and one draw needn't show every extreme that they name: `active_mask`: exactly 64 blocks are active. `block_owner`: every owner index owns exactly 3 blocks, and exactly 2 of them are active.
All inputs are finite; a program needn't handle non-finite values.
Results may differ from a plain program's by a relative error of at most 0.022.
Values may be sent and summed in bfloat16 or wider, within the bound.
No kernel may reach another device: no remote copies, remote signals or barrier semaphores. Data moves between devices by JAX's collectives and lax.ppermute only.
A program may use at most 128 MiB of HBM per device.

v0:
```python
import jax
import jax.numpy as jnp
from jax import lax
from jax.sharding import PartitionSpec as P


def slot_table(active_mask, block_owner, active_count, owners):
    block_total = active_mask.shape[0]
    index = jnp.arange(block_total, dtype=jnp.int32)
    live = active_mask == 1
    earlier = (
        (block_owner[:, None] == block_owner[None, :])
        & live[None, :]
        & (index[None, :] < index[:, None])
    )
    slots = jnp.sum(earlier.astype(jnp.int32), axis=1)
    keyed = jnp.where(live, block_owner * active_count + slots, 0)
    targets = jnp.arange(owners * active_count, dtype=jnp.int32)
    hit = live[None, :] & (keyed[None, :] == targets[:, None])
    chosen = jnp.sum(jnp.where(hit, index[None, :], 0), axis=1)
    return (keyed, live, chosen)


def local(partials, active_mask, block_owner, left_stats, right_stats, left_root, right_root):
    local_blocks = partials.shape[1]
    block_width = partials.shape[3]
    active_count = left_stats.shape[0]
    slab_rows = left_stats.shape[1]
    owners = lax.axis_size("own")
    keyed, live, chosen = slot_table(active_mask, block_owner, active_count, owners)
    my_start = lax.axis_index("dp") * slab_rows
    flat_parts = partials[0].reshape(local_blocks, block_width * block_width)
    spread = lax.all_to_all(flat_parts, "own", split_axis=1, concat_axis=0, tiled=True)
    picked = jnp.take(spread, chosen, axis=0)
    arrived = lax.all_to_all(picked, "own", split_axis=0, concat_axis=1, tiled=True)
    terms = arrived.reshape(active_count, block_width, block_width).astype(jnp.float32)
    gradient = lax.psum_scatter(
        terms.astype(jnp.bfloat16), "dp", scatter_dimension=1, tiled=True
    ).astype(jnp.float32)
    piece = lax.all_gather(gradient.astype(jnp.bfloat16), "dp", axis=1, tiled=True).astype(
        jnp.float32
    )
    left_acc = left_stats
    right_acc = right_stats
    left_cols = jnp.einsum("arw,anw->arn", gradient, piece, precision=lax.Precision.HIGHEST)
    old_cols = left_acc
    left_acc = lax.dynamic_update_slice_in_dim(left_acc, old_cols + left_cols, jnp.int32(0), 2)
    mine = lax.dynamic_slice_in_dim(piece, my_start, slab_rows, 2)
    right_acc = right_acc + jnp.einsum("anr,anw->arw", mine, piece, precision=lax.Precision.HIGHEST)
    mixed_acc = jnp.einsum(
        "arn,anw->arw", left_root, piece.astype(jnp.bfloat16), preferred_element_type=jnp.float32
    )
    mixed_half = mixed_acc.astype(jnp.bfloat16)
    result = jnp.einsum(
        "arn,anw->arw",
        mixed_half,
        lax.all_gather(right_root, "dp", axis=1, tiled=True),
        preferred_element_type=jnp.float32,
    ).astype(jnp.bfloat16)
    flat_result = result.reshape(active_count, slab_rows * block_width)
    back = lax.all_to_all(flat_result, "own", split_axis=1, concat_axis=0, tiled=True)
    placed = jnp.take(back, keyed, axis=0)
    placed = jnp.where(live[:, None], placed, jnp.zeros_like(placed))
    returned = lax.all_to_all(placed, "own", split_axis=0, concat_axis=1, tiled=True)
    preconditioned = returned.reshape(local_blocks, slab_rows, block_width)
    return (preconditioned, left_acc, right_acc)


def solution(mesh):
    placed = (
        P("dp", "own", None, None),
        P(),
        P(),
        P("own", "dp", None),
        P("own", "dp", None),
        P("own", "dp", None),
        P("own", "dp", None),
    )
    return jax.shard_map(
        local,
        mesh=mesh,
        in_specs=placed,
        out_specs=(P("own", "dp", None), P("own", "dp", None), P("own", "dp", None)),
        check_vma=False,
    )
```

profile of v0, /device:TPU:1, one launch (start us, length us, event | category | flops | bytes accessed | tf_op | source)
XLA Modules:
  0.0 469.1 jit_solution(13475200040995492762)
XLA Ops:
  7.2 0.0 copy-start
  7.2 10.5 %all_to_all.48 = bf16[3,32,32768]{2,1,0:T(8,128)(2,1)} reshape(bf16[1,3,1024,1024]{3,2,1,0:T(8,128)(2,1)} %param.7) | data formatting | bytes 12582912 | tf_op jit(solution)/shard_map/all_to_all | solution.py:33
  17.7 11.4 %copy.47 = bf16[3,32,32768]{2,0,1:T(4,128)(2,1)} copy(bf16[3,32,32768]{2,1,0:T(8,128)(2,1)} %all_to_all.48) | data formatting | bytes 12582912 | tf_op jit(solution)/shard_map/all_to_all | solution.py:33
  29.1 8.8 %all-to-all-start = ((bf16[3,32,32768]{2,0,1:T(4,128)(2,1)}), bf16[3,32,32768]{2,0,1:T(4,128)(2,1)}, u32[]{:S(2)}, u32[]{:S(2)}) async-start(bf16[3,32,32768]{2,0,1:T(4,128)(2,1)} %copy.47), calls=%async_computation | async-start | bytes 16777216 | tf_op jit(solution)/shard_map/all_to_all | solution.py:33
  37.9 0.2 reduce-scatter.4.cloned.1.call-start
  38.1 0.0 copy-done.5
  38.1 0.0 copy-done.4
  38.1 0.2 convert_reduce_fusion
  38.3 0.1 select_reduce_fusion
  38.4 0.1 reduce_sum.24
  38.6 99.0 %all-to-all-done = bf16[3,32,32768]{2,0,1:T(4,128)(2,1)} async-done(((bf16[3,32,32768]{2,0,1:T(4,128)(2,1)}), bf16[3,32,32768]{2,0,1:T(4,128)(2,1)}, u32[]{:S(2)}, u32[]{:S(2)}) %all-to-all-start) | async-done | bytes 6291488 | tf_op jit(solution)/shard_map/all_to_all | solution.py:33
  137.6 9.0 %all_to_all.51 = bf16[96,32768]{1,0:T(8,128)(2,1)} reshape(bf16[32,3,32768]{2,1,0:T(4,128)(2,1)} %bitcast) | data formatting | bytes 12582912 | tf_op jit(solution)/shard_map/all_to_all | solution.py:33
  146.6 12.3 %gather_fusion = bf16[64,32768]{1,0:T(8,128)(2,1)} fusion(bf16[96,32768]{1,0:T(8,128)(2,1)} %all_to_all.51, s32[1024]{0:T(1024)S(1)} %pad_clamp_fusion.1), kind=kCustom, calls=%fused_computation | custom fusion | bytes 8388864 | tf_op jit(solution)/shard_map/jit(_take)/gather | solution.py:34
  158.9 7.6 %gather.13 = bf16[32,2,32768]{2,1,0:T(2,128)(2,1)} reshape(bf16[64,32768]{1,0:T(8,128)(2,1)} %gather_fusion) | data formatting | bytes 8388608 | tf_op jit(solution)/shard_map/jit(_take)/gather | solution.py:34
  166.6 5.9 %broadcast_select_fusion = bf16[32,2,32768]{2,1,0:T(2,128)(2,1)S(1)} fusion(bf16[32,2,32768]{2,1,0:T(2,128)(2,1)} %gather.13, pred[32,2]{1,0:T(8,128)(4,1)S(1)} %compare_and_fusion), kind=kLoop, calls=%fused_computation.2 | loop fusion | flops 2097152 | bytes 8388672 | tf_op jit(solution)/shard_map/jit(_take)/select_n | solution.py:34
  172.5 60.1 %all_to_all.64 = bf16[32,2,32768]{2,1,0:T(2,128)(2,1)S(1)} all-to-all(bf16[32,2,32768]{2,1,0:T(2,128)(2,1)S(1)} %broadcast_select_fusion), channel_id=1, replica_groups=mesh['dp'=8,'own'=32] {'own'}, dimensions={0} | all-to-all | bytes 8388608 | tf_op jit(solution)/shard_map/all_to_all | solution.py:35
  232.6 3.4 copy.63
  236.0 0.0 reduce-scatter.4.cloned.1.call-update
  236.0 0.0 all-gather.5.cloned.1.call-start
  236.1 0.7 all-gather.5.cloned.1.call-update
  236.8 0.0 all-gather.3.cloned.1.call-start
  236.8 54.5 %reduce-scatter.4.cloned.1.call-done = bf16[128,2048]{1,0:T(8,128)(2,1)} async-done(((bf16[1024,2048]{1,0:T(8,128)(2,1)}), bf16[128,2048]{1,0:T(8,128)(2,1)}) %reduce-scatter.4.cloned.1.call-update) | async-done | bytes 524304
  291.3 1.4 reshape.94
  292.7 1.2 copy.61
  293.9 0.0 all-gather.3.cloned.1.call-update
  293.9 52.6 %all-gather.5.cloned.1.call-done = bf16[2,1024,1024]{2,1,0:T(8,128)(2,1)} async-done(((bf16[2,128,1024]{2,1,0:T(8,128)(2,1)}), bf16[2,1024,1024]{2,1,0:T(8,128)(2,1)}) %all-gather.5.cloned.1.call-update) | async-done | bytes 4194320 | tf_op jit(solution)/shard_map/all_gather | solution.py:57
  346.5 60.6 %all-gather.3.cloned.1.call-done = bf16[2,1024,1024]{1,2,0:T(8,128)(2,1)} async-done(((bf16[2,128,1024]{1,2,0:T(8,128)(2,1)}), bf16[2,1024,1024]{1,2,0:T(8,128)(2,1)}) %all-gather.3.cloned.1.call-update) | async-done | bytes 4194320 | tf_op jit(solution)/shard_map/all_gather | solution.py:40
  407.1 0.0 copy-done
  407.1 5.3 %convolution_convert_fusion = bf16[2,128,1024]{2,1,0:T(8,128)(2,1)S(1)} fusion(bf16[2,1024,1024]{2,1,0:T(8,128)(2,1)} %all-gather.5.cloned.1.call-done, bf16[2,1024,1024]{1,2,0:T(8,128)(2,1)} %all-gather.3.cloned.1.call-done, bf16[2,128,1024]{2,1,0:T(8,128)(2,1)S(1)} %copy-done), kind=kOutput, calls=%fused_computation.5 | convolution fusion | flops 1074266112 | bytes 9437184 | tf_op jit(solution)/shard_map/arn,anw->arw/dot_general | solution.py:54
  412.4 0.3 all_to_all.54
  412.8 1.3 copy.51
  414.1 10.1 %all-to-all-start.2 = ((bf16[2,32,4096]{2,0,1:T(2,128)(2,1)}), bf16[2,32,4096]{2,0,1:T(2,128)(2,1)S(1)}, u32[]{:S(2)}, u32[]{:S(2)}) async-start(bf16[2,32,4096]{2,0,1:T(2,128)(2,1)} %copy.51), calls=%async_computation.2 | async-start | bytes 1048576 | tf_op jit(solution)/shard_map/all_to_all | solution.py:61
  424.2 0.1 broadcast_in_dim.63
  424.3 0.1 broadcast_in_dim.66
  424.5 11.3 %all-to-all-done.2 = bf16[2,32,4096]{2,0,1:T(2,128)(2,1)S(1)} async-done(((bf16[2,32,4096]{2,0,1:T(2,128)(2,1)}), bf16[2,32,4096]{2,0,1:T(2,128)(2,1)S(1)}, u32[]{:S(2)}, u32[]{:S(2)}) %all-to-all-start.2) | async-done | bytes 524320 | tf_op jit(solution)/shard_map/all_to_all | solution.py:61
  435.8 0.2 all_to_all.57
  436.0 1.0 gather_fusion.1
  437.0 0.5 gather.15
  437.5 1.7 select_select_fusion
  439.2 4.2 all-to-all-start.3
  443.4 0.0 copy-start.1
  443.4 5.3 %convolution_add_fusion = f32[2,128,1024]{2,1,0:T(8,128)} fusion(f32[2,128,1024]{2,1,0:T(8,128)} %param.11, bf16[2,1024,1024]{1,2,0:T(8,128)(2,1)} %all-gather.3.cloned.1.call-done, s32[]{:T(128)S(6)} %select_n.56), kind=kOutput, calls=%fused_computation.3 | convolution fusion | flops 537133056 | bytes 6815748 | tf_op jit(solution)/shard_map/anr,anw->arw/dot_general | solution.py:49
  448.7 0.0 copy-done.2
  448.7 0.0 copy-done.3
  448.7 1.8 convolution_add_fusion.1
  450.5 10.2 %all-to-all-done.3 = bf16[32,3,4096]{2,1,0:T(4,128)(2,1)S(1)} async-done(((bf16[32,3,4096]{2,1,0:T(4,128)(2,1)}), bf16[32,3,4096]{2,1,0:T(4,128)(2,1)S(1)}, u32[]{:S(2)}, u32[]{:S(2)}) %all-to-all-start.3) | async-done | bytes 786464 | tf_op jit(solution)/shard_map/all_to_all | solution.py:64
  460.7 0.6 copy.52
  461.3 1.3 reshape.75
  (12 shorter events, 0.1 us)
Async XLA Ops:
  7.2 400.0 %copy-start = (bf16[2,128,1024]{2,1,0:T(8,128)(2,1)S(1)}, bf16[2,128,1024]{2,1,0:T(8,128)(2,1)}, u32[]{:S(2)}) copy-start(bf16[2,128,1024]{2,1,0:T(8,128)(2,1)} %param.12) | copy-start | bytes 1572868
  29.1 9.0 %copy-start.5 = (s32[96]{0:T(128)S(1)}, s32[96]{0:T(128)}, u32[]{:S(2)}) copy-start(s32[96]{0:T(128)} %param.8) | copy-start | bytes 1156
  29.1 9.0 %copy-start.4 = (s32[96]{0:T(128)S(1)}, s32[96]{0:T(128)}, u32[]{:S(2)}) copy-start(s32[96]{0:T(128)} %param.9) | copy-start | bytes 1156
  29.1 108.5 %all-to-all-start = ((bf16[3,32,32768]{2,0,1:T(4,128)(2,1)}), bf16[3,32,32768]{2,0,1:T(4,128)(2,1)}, u32[]{:S(2)}, u32[]{:S(2)}) async-start(bf16[3,32,32768]{2,0,1:T(4,128)(2,1)} %copy.47), calls=%async_computation | async-start | bytes 16777216 | tf_op jit(solution)/shard_map/all_to_all | solution.py:33
  37.9 253.4 %reduce-scatter.4.cloned.1.call-start = ((), (), s32[]{:S(2)}) async-start(), calls=%async_computation.7 | async-start | bytes 4718592
  236.0 110.5 %all-gather.5.cloned.1.call-start = ((), (), s32[]{:S(2)}) async-start(), calls=%async_computation.6 | async-start | bytes 4718592 | tf_op jit(solution)/shard_map/all_gather | solution.py:57
  236.8 170.4 %all-gather.3.cloned.1.call-start = ((), (), s32[]{:S(2)}) async-start(), calls=%async_computation.5 | async-start | bytes 4718592 | tf_op jit(solution)/shard_map/all_gather | solution.py:40
  414.1 21.7 %all-to-all-start.2 = ((bf16[2,32,4096]{2,0,1:T(2,128)(2,1)}), bf16[2,32,4096]{2,0,1:T(2,128)(2,1)S(1)}, u32[]{:S(2)}, u32[]{:S(2)}) async-start(bf16[2,32,4096]{2,0,1:T(2,128)(2,1)} %copy.51), calls=%async_computation.2 | async-start | bytes 1048576 | tf_op jit(solution)/shard_map/all_to_all | solution.py:61
  439.2 9.5 %copy-start.2 = (bf16[2,128,1024]{1,2,0:T(8,128)(2,1)S(1)}, bf16[2,128,1024]{1,2,0:T(8,128)(2,1)}, u32[]{:S(2)}) copy-start(bf16[2,128,1024]{1,2,0:T(8,128)(2,1)} %copy.61) | copy-start | bytes 1572868
  439.2 9.5 %copy-start.3 = (f32[2,128,1024]{2,1,0:T(8,128)S(1)}, f32[2,128,1024]{2,1,0:T(8,128)}, u32[]{:S(2)}) copy-start(f32[2,128,1024]{2,1,0:T(8,128)} %param.10) | copy-start | bytes 3145732
  439.2 21.5 %all-to-all-start.3 = ((bf16[32,3,4096]{2,1,0:T(4,128)(2,1)}), bf16[32,3,4096]{2,1,0:T(4,128)(2,1)S(1)}, u32[]{:S(2)}, u32[]{:S(2)}) async-start(bf16[32,3,4096]{2,1,0:T(4,128)(2,1)} %select_select_fusion), calls=%async_computation.3 | async-start | bytes 2097152 | tf_op jit(solution)/shard_map/all_to_all | solution.py:64
  443.4 5.3 %copy-start.1 = (bf16[2,1024,1024]{1,2,0:T(8,128)(2,1)S(1)}, bf16[2,1024,1024]{1,2,0:T(8,128)(2,1)}, u32[]{:S(2)}) copy-start(bf16[2,1024,1024]{1,2,0:T(8,128)(2,1)} %all-gather.3.cloned.1.call-done) | copy-start | bytes 12582916
Sparse Core Ops, SparseCore 0:
  236.1 55.0 reduce-scatter.3
  293.1 53.3 all-gather.4
  348.8 58.3 all-gather.2
where the time goes:
time: 470 us; the launch traced here: 469 us
  waiting for transfers between devices  289 us (61%)
  local copies, waits for them, and re-layouts  62.5 us (13%)
  blocking collectives  60.1 us (13%)
  starting transfers between devices  23.3 us (5%)
  between operations  13.9 us (3%)
  matrix products  12.3 us (3%)
  other arithmetic  7.96 us (2%)
    all_to_all x1, waiting for transfers between devices, local(): lax.all_to_all(flat_parts, 'own', split_axis=1, concat_axis=0, tiled=True)  99 us
    all_gather x1, waiting for transfers between devices, local(): lax.all_gather(gradient.astype(jnp.bfloat16), 'dp', axis=1, tiled=True)  60.6 us
    all_to_all x1, blocking collectives, local(): lax.all_to_all(picked, 'own', split_axis=0, concat_axis=1, tiled=True)  60.1 us
    unnamed x4, waiting for transfers between devices  55.2 us
    all_gather x1, waiting for transfers between devices, local(): lax.all_gather(right_root, 'dp', axis=1, tiled=True)  52.6 us
    all_to_all x3, local copies, waits for them, and re-layouts, local(): lax.all_to_all(flat_parts, 'own', split_axis=1, concat_axis=0, tiled=True)  30.9 us
    gather x2, local copies, waits for them, and re-layouts, local(): picked = jnp.take(spread, chosen, axis=0)  20 us
    all_to_all x1, waiting for transfers between devices, local(): lax.all_to_all(flat_result, 'own', split_axis=1, concat_axis=0, tiled=True)  11.3 us
  transfers between devices with their start and end apart: 6, of which 6 were waited for; matrix products, arithmetic and copies ran while one was open for 2% of the time, Pallas kernels for 0%

commit v1 on v0

v1 whole, which is shorter than its diff:
```python
import jax
import jax.numpy as jnp
from jax import lax
from jax.experimental import pallas as pl
from jax.experimental.pallas import tpu as pltpu
from jax.sharding import PartitionSpec as P

TILE_ROWS = 16


def slot_table(active_mask, block_owner, active_count, owners):
    block_total = active_mask.shape[0]
    index = jnp.arange(block_total, dtype=jnp.int32)
    live = active_mask == 1
    earlier = (
        (block_owner[:, None] == block_owner[None, :])
        & live[None, :]
        & (index[None, :] < index[:, None])
    )
    slots = jnp.sum(earlier.astype(jnp.int32), axis=1)
    keyed = jnp.where(live, block_owner * active_count + slots, 0)
    targets = jnp.arange(owners * active_count, dtype=jnp.int32)
    hit = live[None, :] & (keyed[None, :] == targets[:, None])
    chosen = jnp.sum(jnp.where(hit, index[None, :], 0), axis=1)
    return (keyed, live, chosen)


def pick_kernel(table_ref, source_ref, out_ref):
    def step(t, carry):
        wanted = table_ref[t]
        block = source_ref[jnp.maximum(wanted, 0)]
        out_ref[t] = jnp.where(wanted >= 0, block, jnp.zeros_like(block))
        return carry

    lax.fori_loop(0, out_ref.shape[0], step, 0, unroll=4)


def pick(source, table):
    count = table.shape[0]
    shape = (count,) + source.shape[1:]
    return pl.pallas_call(
        pick_kernel,
        out_shape=jax.ShapeDtypeStruct(shape, source.dtype),
        in_specs=[
            pl.BlockSpec(memory_space=pltpu.SMEM),
            pl.BlockSpec(memory_space=pltpu.VMEM),
        ],
        out_specs=pl.BlockSpec(memory_space=pltpu.VMEM),
        compiler_params=pltpu.CompilerParams(vmem_limit_bytes=8 * 1024 * 1024),
        cost_estimate=pl.CostEstimate(
            flops=0, bytes_accessed=2 * (source.size + count * source[0].size), transcendentals=0
        ),
    )(table, source)


def to_pieces(slabs, owners):
    count, rows, cols = slabs.shape
    down = rows // TILE_ROWS
    across = owners // down
    split = slabs.reshape(count, down, TILE_ROWS, across, cols // across)
    return split.transpose(1, 3, 0, 2, 4).reshape(owners, count, TILE_ROWS, cols // across)


def from_pieces(pieces, rows, cols):
    owners, count = pieces.shape[:2]
    down = rows // TILE_ROWS
    across = owners // down
    split = pieces.reshape(down, across, count, TILE_ROWS, cols // across)
    return split.transpose(2, 0, 3, 1, 4).reshape(count, rows, cols)


def swap(pieces):
    return lax.all_to_all(pieces, "own", split_axis=0, concat_axis=0, tiled=True)


def local(partials, active_mask, block_owner, left_stats, right_stats, left_root, right_root):
    width = partials.shape[3]
    active_count, rows = left_stats.shape[:2]
    owners = lax.axis_size("own")
    keyed, live, chosen = slot_table(active_mask, block_owner, active_count, owners)
    wanted = jnp.where(live, keyed, -1)
    my_start = lax.axis_index("dp") * rows

    summed = lax.psum_scatter(partials[0], "dp", scatter_dimension=1, tiled=True)
    summed, right_root = lax.optimization_barrier((summed, right_root))
    right_full = lax.all_gather(right_root, "dp", axis=1, tiled=True)

    spread = swap(to_pieces(summed, owners))
    piece = spread.shape[2:]
    picked = pick(spread.reshape((-1,) + piece), chosen)
    arrived = swap(picked.reshape((owners, active_count) + piece))
    gradient = from_pieces(arrived, rows, width)
    full = lax.all_gather(gradient, "dp", axis=1, tiled=True)

    mixed = jnp.einsum(
        "arn,anw->arw", left_root, full, preferred_element_type=jnp.float32
    ).astype(jnp.bfloat16)
    result = jnp.einsum(
        "arn,anw->arw", mixed, right_full, preferred_element_type=jnp.float32
    ).astype(jnp.bfloat16)

    back = swap(to_pieces(result, owners))
    placed = pick(back.reshape((-1,) + piece), wanted)
    returned = swap(placed.reshape((owners, -1) + piece))
    preconditioned = from_pieces(returned, rows, width)

    left_new = left_stats + jnp.einsum(
        "arw,anw->arn", gradient, full, preferred_element_type=jnp.float32
    )
    mine = lax.dynamic_slice_in_dim(full, my_start, rows, 2)
    right_new = right_stats + jnp.einsum(
        "anr,anw->arw", mine, full, preferred_element_type=jnp.float32
    )
    return (preconditioned, left_new, right_new)


def solution(mesh):
    placed = (
        P("dp", "own", None, None),
        P(),
        P(),
        P("own", "dp", None),
        P("own", "dp", None),
        P("own", "dp", None),
        P("own", "dp", None),
    )
    return jax.shard_map(
        local,
        mesh=mesh,
        in_specs=placed,
        out_specs=(P("own", "dp", None), P("own", "dp", None), P("own", "dp", None)),
        check_vma=False,
    )
```

time: 470 us -> 255 us (0.54)
  waiting for transfers between devices: 289 us -> 184 us
  local copies, waits for them, and re-layouts: 62.5 us -> 7.68 us
  blocking collectives: 60.1 us -> 15.2 us
  other arithmetic: 7.96 us -> 0.3 us
    all_to_all x3, waiting for transfers between devices: 121 us -> 32.9 us  [swap(): lax.all_to_all(pieces, 'own', split_axis=0, concat_axis=0, tiled=True)]
    reduce_scatter x0 -> x1, waiting for transfers between devices: none -> 81.6 us  [local(): lax.psum_scatter(partials[0], 'dp', scatter_dimension=1, tiled=True)]
    unnamed x4 -> x3, waiting for transfers between devices: 55.2 us -> 0.71 us
    all_to_all x1, blocking collectives: 60.1 us -> 15.2 us  [swap(): lax.all_to_all(pieces, 'own', split_axis=0, concat_axis=0, tiled=True)]
    all_gather x2, waiting for transfers between devices: 113 us -> 68.8 us  [the longest x1 55.8 us: local(): full = lax.all_gather(gradient, 'dp', axis=1, tiled=True)]
    all_to_all x7 -> x0, local copies, waits for them, and re-layouts: 33.3 us -> none  [the longest x3 30.9 us: local(): lax.all_to_all(flat_parts, 'own', split_axis=1, concat_axis=0, tiled=True)]
    gather x4 -> x0, local copies, waits for them, and re-layouts: 21.5 us -> none  [the longest x2 20 us: local(): picked = jnp.take(spread, chosen, axis=0)]
    select_n x4 -> x1, other arithmetic: 7.63 us -> 0.01 us  [local(): wanted = jnp.where(live, keyed, -1)]
  transfers between devices with their start and end apart: 6 -> 6, of which waited for: 6 -> 6; matrix products, arithmetic and copies ran while one was open for 2% -> 5% of each run, Pallas kernels for 0% -> 0%
where the time goes in v1:
time: 255 us; the launch traced here: 254 us
  waiting for transfers between devices  184 us (72%)
  starting transfers between devices  19.1 us (7%)
  blocking collectives  15.2 us (6%)
  between operations  13.9 us (5%)
  matrix products  11.5 us (5%)
  local copies, waits for them, and re-layouts  7.68 us (3%)
    reduce_scatter x1, waiting for transfers between devices, local(): lax.psum_scatter(partials[0], 'dp', scatter_dimension=1, tiled=True)  81.6 us
    all_gather x1, waiting for transfers between devices, local(): full = lax.all_gather(gradient, 'dp', axis=1, tiled=True)  55.8 us
    all_to_all x3, waiting for transfers between devices, swap(): lax.all_to_all(pieces, 'own', split_axis=0, concat_axis=0, tiled=True)  32.9 us
    all_to_all x3, starting transfers between devices, swap(): lax.all_to_all(pieces, 'own', split_axis=0, concat_axis=0, tiled=True)  19 us
    all_to_all x1, blocking collectives, swap(): lax.all_to_all(pieces, 'own', split_axis=0, concat_axis=0, tiled=True)  15.2 us
    all_gather x1, waiting for transfers between devices, local(): right_full = lax.all_gather(right_root, 'dp', axis=1, tiled=True)  13 us
  transfers between devices with their start and end apart: 6, of which 6 were waited for; matrix products, arithmetic and copies ran while one was open for 5% of the time, Pallas kernels for 0%

profile of v1, /device:TPU:1, one launch (start us, length us, event | category | flops | bytes accessed | tf_op | source)
XLA Modules:
  0.0 254.2 jit_solution(600165867744734807)
XLA Ops:
  7.2 0.0 copy-start
  7.2 0.0 reduce-scatter.2.cloned.1.call-start
  7.2 0.7 reduce-scatter.2.cloned.1.call-update
  7.9 0.0 copy-start.6
  7.9 0.0 copy-start.5
  7.9 0.0 all-gather.5.cloned.1.call-start
  8.0 81.6 %reduce-scatter.2.cloned.1.call-done = bf16[3,128,1024]{2,1,0:T(8,128)(2,1)} async-done(((bf16[3,1024,1024]{2,1,0:T(8,128)(2,1)}), bf16[3,128,1024]{2,1,0:T(8,128)(2,1)}) %reduce-scatter.2.cloned.1.call-update) | async-done | bytes 786448 | tf_op jit(solution)/shard_map/reduce_scatter | solution.py:84
  89.6 0.0 all-gather.5.cloned.1.call-update
  89.6 2.0 reshape.46
  91.5 1.0 copy.15
  92.6 7.5 %all-to-all-start = ((bf16[32,3,16,256]{3,2,1,0:T(8,128)(2,1)}), bf16[32,3,16,256]{3,2,1,0:T(8,128)(2,1)S(1)}, u32[]{:S(2)}, u32[]{:S(2)}) async-start(bf16[32,3,16,256]{3,2,1,0:T(8,128)(2,1)} %bitcast.2), calls=%async_computation.1 | async-start | bytes 1572864 | tf_op jit(solution)/shard_map/all_to_all | solution.py:73
  100.0 0.0 all-gather.3.cloned.1.call-start
  100.1 0.0 copy-done.6
  100.1 0.0 copy-done.5
  100.1 0.2 convert_reduce_fusion
  100.3 0.1 select_reduce_fusion.table_ref
  100.4 13.8 %all-to-all-done = bf16[32,3,16,256]{3,2,1,0:T(8,128)(2,1)S(1)} async-done(((bf16[32,3,16,256]{3,2,1,0:T(8,128)(2,1)}), bf16[32,3,16,256]{3,2,1,0:T(8,128)(2,1)S(1)}, u32[]{:S(2)}, u32[]{:S(2)}) %all-to-all-start) | async-done | bytes 786464 | tf_op jit(solution)/shard_map/all_to_all | solution.py:73
  114.3 0.8 shard_map.94
  115.0 15.2 %all_to_all.20 = bf16[32,2,16,256]{3,2,1,0:T(8,128)(2,1)S(1)} all-to-all(bf16[32,2,16,256]{3,2,1,0:T(8,128)(2,1)S(1)} %bitcast.25), channel_id=1, replica_groups=mesh['dp'=8,'own'=32] {'own'}, dimensions={0} | all-to-all | bytes 1048576 | tf_op jit(solution)/shard_map/all_to_all | solution.py:73
  130.2 0.4 copy.24
  130.6 1.2 reshape.51
  131.8 0.0 all-gather.3.cloned.1.call-update
  131.8 13.0 %all-gather.5.cloned.1.call-done = bf16[2,1024,1024]{2,1,0:T(8,128)(2,1)} async-done(((bf16[2,128,1024]{2,1,0:T(8,128)(2,1)}), bf16[2,1024,1024]{2,1,0:T(8,128)(2,1)}) %all-gather.5.cloned.1.call-update) | async-done | bytes 4194320 | tf_op jit(solution)/shard_map/all_gather | solution.py:86
  144.8 55.8 %all-gather.3.cloned.1.call-done = bf16[2,1024,1024]{2,1,0:T(8,128)(2,1)} async-done(((bf16[2,128,1024]{2,1,0:T(8,128)(2,1)}), bf16[2,1024,1024]{2,1,0:T(8,128)(2,1)}) %all-gather.3.cloned.1.call-update) | async-done | bytes 4194320 | tf_op jit(solution)/shard_map/all_gather | solution.py:93
  200.6 0.0 copy-done
  200.6 4.7 %convolution_convert_fusion.1 = bf16[2,128,1024]{2,1,0:T(8,128)(2,1)S(1)} fusion(bf16[2,1024,1024]{2,1,0:T(8,128)(2,1)} %all-gather.5.cloned.1.call-done, bf16[2,128,1024]{2,1,0:T(8,128)(2,1)S(1)} %copy-done, bf16[2,1024,1024]{2,1,0:T(8,128)(2,1)} %all-gather.3.cloned.1.call-done), kind=kOutput, calls=%fused_computation.3 | convolution fusion | flops 1074266112 | bytes 9437184 | tf_op jit(solution)/shard_map/arn,anw->arw/dot_general | solution.py:98
  205.4 0.0 copy-start.3
  205.4 0.4 reshape.52
  205.8 0.9 copy.17
  206.7 7.5 %all-to-all-start.2 = ((bf16[32,2,16,256]{3,2,1,0:T(8,128)(2,1)}), bf16[32,2,16,256]{3,2,1,0:T(8,128)(2,1)S(1)}, u32[]{:S(2)}, u32[]{:S(2)}) async-start(bf16[32,2,16,256]{3,2,1,0:T(8,128)(2,1)} %bitcast.8), calls=%async_computation.3 | async-start | bytes 1048576 | tf_op jit(solution)/shard_map/all_to_all | solution.py:73
  214.2 11.5 %all-to-all-done.2 = bf16[32,2,16,256]{3,2,1,0:T(8,128)(2,1)S(1)} async-done(((bf16[32,2,16,256]{3,2,1,0:T(8,128)(2,1)}), bf16[32,2,16,256]{3,2,1,0:T(8,128)(2,1)S(1)}, u32[]{:S(2)}, u32[]{:S(2)}) %all-to-all-start.2) | async-done | bytes 524320 | tf_op jit(solution)/shard_map/all_to_all | solution.py:73
  225.8 1.7 shard_map.95
  227.5 4.0 %all-to-all-start.3 = ((bf16[32,3,16,256]{3,2,1,0:T(8,128)(2,1)}), bf16[32,3,16,256]{3,2,1,0:T(8,128)(2,1)S(1)}, u32[]{:S(2)}, u32[]{:S(2)}) async-start(bf16[32,3,16,256]{3,2,1,0:T(8,128)(2,1)} %bitcast.10), calls=%async_computation.4 | async-start | bytes 1572864 | tf_op jit(solution)/shard_map/all_to_all | solution.py:73
  231.5 0.0 copy-done.3
  231.5 0.0 copy-start.1
  231.5 0.0 copy-start.2
  231.5 0.0 copy-start.4
  231.6 4.3 %convolution_add_fusion = f32[2,128,1024]{2,1,0:T(8,128)} fusion(f32[2,128,1024]{2,1,0:T(8,128)S(1)} %copy-done.3, bf16[2,1024,1024]{2,1,0:T(8,128)(2,1)} %all-gather.3.cloned.1.call-done, s32[]{:T(128)S(6)} %select_n.17), kind=kOutput, calls=%fused_computation | convolution fusion | flops 537133056 | bytes 6815748 | tf_op jit(solution)/shard_map/anr,anw->arw/dot_general | solution.py:111
  235.9 0.0 copy-done.1
  235.9 0.0 copy-done.2
  235.9 0.0 copy-done.4
  235.9 2.5 convolution_add_fusion.1
  238.4 7.5 %all-to-all-done.3 = bf16[32,3,16,256]{3,2,1,0:T(8,128)(2,1)S(1)} async-done(((bf16[32,3,16,256]{3,2,1,0:T(8,128)(2,1)}), bf16[32,3,16,256]{3,2,1,0:T(8,128)(2,1)S(1)}, u32[]{:S(2)}, u32[]{:S(2)}) %all-to-all-start.3) | async-done | bytes 786464 | tf_op jit(solution)/shard_map/all_to_all | solution.py:73
  245.9 0.4 copy.23
  246.3 1.4 reshape.57
  (2 shorter events, 0.0 us)
Async XLA Ops:
  7.2 193.5 %copy-start = (bf16[2,128,1024]{2,1,0:T(8,128)(2,1)S(1)}, bf16[2,128,1024]{2,1,0:T(8,128)(2,1)}, u32[]{:S(2)}) copy-start(bf16[2,128,1024]{2,1,0:T(8,128)(2,1)} %param.12) | copy-start | bytes 1572868
  7.2 82.4 %reduce-scatter.2.cloned.1.call-start = ((), (), s32[]{:S(2)}) async-start(), calls=%async_computation.5 | async-start | bytes 7077888 | tf_op jit(solution)/shard_map/reduce_scatter | solution.py:84
  7.9 92.2 %copy-start.6 = (s32[96]{0:T(128)S(1)}, s32[96]{0:T(128)}, u32[]{:S(2)}) copy-start(s32[96]{0:T(128)} %param.8) | copy-start | bytes 1156
  7.9 92.2 %copy-start.5 = (s32[96]{0:T(128)S(1)}, s32[96]{0:T(128)}, u32[]{:S(2)}) copy-start(s32[96]{0:T(128)} %param.9) | copy-start | bytes 1156
  7.9 136.9 %all-gather.5.cloned.1.call-start = ((), (), s32[]{:S(2)}) async-start(), calls=%async_computation.7 | async-start | bytes 4718592 | tf_op jit(solution)/shard_map/all_gather | solution.py:86
  92.6 21.7 %all-to-all-start = ((bf16[32,3,16,256]{3,2,1,0:T(8,128)(2,1)}), bf16[32,3,16,256]{3,2,1,0:T(8,128)(2,1)S(1)}, u32[]{:S(2)}, u32[]{:S(2)}) async-start(bf16[32,3,16,256]{3,2,1,0:T(8,128)(2,1)} %bitcast.2), calls=%async_computation.1 | async-start | bytes 1572864 | tf_op jit(solution)/shard_map/all_to_all | solution.py:73
  100.0 100.6 %all-gather.3.cloned.1.call-start = ((), (), s32[]{:S(2)}) async-start(), calls=%async_computation.6 | async-start | bytes 4718592 | tf_op jit(solution)/shard_map/all_gather | solution.py:93
  205.4 26.1 %copy-start.3 = (f32[2,128,1024]{2,1,0:T(8,128)S(1)}, f32[2,128,1024]{2,1,0:T(8,128)}, u32[]{:S(2)}) copy-start(f32[2,128,1024]{2,1,0:T(8,128)} %param.11) | copy-start | bytes 3145732
  206.7 19.1 %all-to-all-start.2 = ((bf16[32,2,16,256]{3,2,1,0:T(8,128)(2,1)}), bf16[32,2,16,256]{3,2,1,0:T(8,128)(2,1)S(1)}, u32[]{:S(2)}, u32[]{:S(2)}) async-start(bf16[32,2,16,256]{3,2,1,0:T(8,128)(2,1)} %bitcast.8), calls=%async_computation.3 | async-start | bytes 1048576 | tf_op jit(solution)/shard_map/all_to_all | solution.py:73
  227.5 18.4 %all-to-all-start.3 = ((bf16[32,3,16,256]{3,2,1,0:T(8,128)(2,1)}), bf16[32,3,16,256]{3,2,1,0:T(8,128)(2,1)S(1)}, u32[]{:S(2)}, u32[]{:S(2)}) async-start(bf16[32,3,16,256]{3,2,1,0:T(8,128)(2,1)} %bitcast.10), calls=%async_computation.4 | async-start | bytes 1572864 | tf_op jit(solution)/shard_map/all_to_all | solution.py:73
  231.5 4.3 %copy-start.1 = (bf16[2,1024,1024]{2,1,0:T(8,128)(2,1)S(1)}, bf16[2,1024,1024]{2,1,0:T(8,128)(2,1)}, u32[]{:S(2)}) copy-start(bf16[2,1024,1024]{2,1,0:T(8,128)(2,1)} %all-gather.3.cloned.1.call-done) | copy-start | bytes 12582916
  231.5 4.3 %copy-start.2 = (bf16[2,128,1024]{2,1,0:T(8,128)(2,1)S(1)}, bf16[2,128,1024]{2,1,0:T(8,128)(2,1)}, u32[]{:S(2)}) copy-start(bf16[2,128,1024]{2,1,0:T(8,128)(2,1)} %reshape.51) | copy-start | bytes 1572868
  231.5 4.3 %copy-start.4 = (f32[2,128,1024]{2,1,0:T(8,128)S(1)}, f32[2,128,1024]{2,1,0:T(8,128)}, u32[]{:S(2)}) copy-start(f32[2,128,1024]{2,1,0:T(8,128)} %param.10) | copy-start | bytes 3145732
Sparse Core Ops, SparseCore 0:
  10.6 78.9 reduce-scatter.1
  91.4 53.4 all-gather.4
  147.2 53.4 all-gather.2

commit v2 on v1

v2 whole, which is shorter than its diff:
```python
import functools

import jax
import jax.numpy as jnp
from jax import lax
from jax.experimental import pallas as pl
from jax.experimental.pallas import tpu as pltpu
from jax.sharding import PartitionSpec as P

TILE_ROWS = 16
STREAMS = 2
F32 = jnp.float32
BF16 = jnp.bfloat16
MIB = 1024 * 1024
VMEM = pl.BlockSpec(memory_space=pltpu.VMEM)
SMEM = pl.BlockSpec(memory_space=pltpu.SMEM)
HBM = pl.BlockSpec(memory_space=pltpu.HBM)


def slot_table(active_mask, block_owner, active_count, owners):
    block_total = active_mask.shape[0]
    index = jnp.arange(block_total, dtype=jnp.int32)
    live = active_mask == 1
    earlier = (
        (block_owner[:, None] == block_owner[None, :])
        & live[None, :]
        & (index[None, :] < index[:, None])
    )
    slots = jnp.sum(earlier.astype(jnp.int32), axis=1)
    keyed = jnp.where(live, block_owner * active_count + slots, 0)
    targets = jnp.arange(owners * active_count, dtype=jnp.int32)
    hit = live[None, :] & (keyed[None, :] == targets[:, None])
    chosen = jnp.sum(jnp.where(hit, index[None, :], 0), axis=1)
    return (keyed, live, chosen)


def call(kernel, out_shape, in_specs, args, flops=0, scratch=(), limit=16, out_specs=None):
    outs = jax.tree.leaves(out_shape)
    whole = [x for x, spec in zip(args, in_specs) if spec is not HBM]
    moved = sum(x.size * x.dtype.itemsize for x in whole + outs)
    return pl.pallas_call(
        kernel,
        out_shape=out_shape,
        in_specs=in_specs,
        out_specs=out_specs or jax.tree.map(lambda _: VMEM, out_shape),
        scratch_shapes=list(scratch),
        compiler_params=pltpu.CompilerParams(vmem_limit_bytes=limit * MIB),
        cost_estimate=pl.CostEstimate(flops=flops, bytes_accessed=moved, transcendentals=0),
    )(*args)


def pick_kernel(table_ref, source_ref, out_ref):
    def step(t, carry):
        wanted = table_ref[t]
        block = source_ref[jnp.maximum(wanted, 0)]
        out_ref[t] = jnp.where(wanted >= 0, block, jnp.zeros_like(block))
        return carry

    lax.fori_loop(0, out_ref.shape[0], step, 0, unroll=8)


def pick(source, table):
    shape = jax.ShapeDtypeStruct(table.shape + source.shape[1:], source.dtype)
    return call(pick_kernel, shape, [SMEM, VMEM], (table, source))


def put_pieces(out_ref, item, value, first=0):
    rows, cols = value.shape
    narrow = out_ref.shape[3]
    across = cols // narrow
    for i in range(rows // TILE_ROWS):
        for j in range(across):
            out_ref[(first + i) * across + j, item] = value[
                i * TILE_ROWS : (i + 1) * TILE_ROWS, j * narrow : (j + 1) * narrow
            ]


def unpack_kernel(pieces_ref, *out_refs):
    owners, count, tall, narrow = pieces_ref.shape
    for item in range(count):
        if len(out_refs) == 1:
            out_ref = out_refs[0].at[item]
        else:
            out_ref = out_refs[item]
        across = out_ref.shape[1] // narrow
        for i in range(owners // across):
            for j in range(across):
                out_ref[i * tall : (i + 1) * tall, j * narrow : (j + 1) * narrow] = pieces_ref[
                    i * across + j, item
                ]


def add_kernel(got_ref, piece_ref, out_ref):
    out_ref[...] = (got_ref[...].astype(F32) + piece_ref[...].astype(F32)).astype(BF16)


def pack_kernel(own_ref, *rest):
    got, out_ref = rest[:-1], rest[-1]
    count, rows = own_ref.shape[:2]
    part = got[0].shape[1]
    for item in range(count):
        for stream in range(rows // part):
            total = own_ref[item, stream * part : (stream + 1) * part].astype(F32)
            for ref in got[2 * stream : 2 * stream + 2]:
                total = total + ref[item].astype(F32)
            put_pieces(out_ref, item, total.astype(BF16), stream * part // TILE_ROWS)


def hop(value, step, ring):
    return lax.ppermute(value, "dp", [(i, (i + step) % ring) for i in range(ring)])


def chains(count, ring):
    far, near = ring // 2, ring - 1 - ring // 2
    for step in range(far):
        for block in range(count):
            long_way = 1 if block % 2 == 0 else -1
            for way, length in ((long_way, far), (-long_way, near)):
                place = step - (far - length)
                if place >= 0:
                    yield block, way, place, length


def sum_over_ring(blocks, rows, owners):
    count, _, cols = blocks.shape
    ring = lax.axis_size("dp")
    me = lax.axis_index("dp").astype(jnp.int32)
    part = rows // STREAMS
    shape = (count, part, cols)
    order = list(chains(STREAMS, ring))

    def piece(me, stream, way, place, length):
        target = lax.rem(me + way * (length - place) + ring, ring)
        return lax.dynamic_slice(blocks, (0, target * rows + stream * part, 0), shape)

    first = {step[:2]: piece(me, *step) for step in order if step[2] == 0}
    later, first = lax.optimization_barrier((me, first))
    pieces = {step[:3]: piece(later, *step) for step in order if step[2] > 0}
    own = lax.dynamic_slice(blocks, (0, later * rows, 0), (count, rows, cols))
    held = {}
    for stream, way, place, length in order:
        if place == 0:
            value = first[stream, way]
        else:
            value = call(
                add_kernel,
                jax.ShapeDtypeStruct(shape, BF16),
                [VMEM, VMEM],
                (held[stream, way], pieces[stream, way, place]),
            )
        held[stream, way] = hop(value, way, ring)
    got = [held[stream, way] for stream in range(STREAMS) for way in (1, -1)]
    narrow = cols * (rows // TILE_ROWS) // owners
    return call(
        pack_kernel,
        jax.ShapeDtypeStruct((owners, count, TILE_ROWS, narrow), BF16),
        [VMEM] * (1 + len(got)),
        (own, *got),
    )


def columns(me, k, ring, width):
    return pl.ds(pl.multiple_of(lax.rem(me + k, ring) * width, width), width)


def mix_kernel(ring, places, me_ref, root_ref, *rest):
    shards, (old_ref, new_ref) = rest[: len(places)], rest[len(places) :]
    me = me_ref[0]
    rows = root_ref.shape[1]
    for a in range(root_ref.shape[0]):
        total = old_ref[a]
        for (block, k), shard in zip(places, shards):
            if block == a:
                total = total + jnp.dot(
                    root_ref[a, :, columns(me, k, ring, rows)],
                    shard[...],
                    preferred_element_type=F32,
                )
        new_ref[a] = total


def gram_kernel(ring, places, me_ref, *rest):
    shards, rest = rest[: len(places)], rest[len(places) :]
    owned, (left_in, right_in, left_ref, right_ref) = rest[:-4], rest[-4:]
    me = me_ref[0]
    rows = left_ref.shape[1]
    mine = columns(me, 0, ring, rows)
    left_ref[...] = left_in[...]
    for a in range(left_ref.shape[0]):
        total = right_in[a]
        for (block, k), shard in zip(places, shards):
            if block == a:
                cols = columns(me, k, ring, rows)
                left_ref[a, :, cols] = left_ref[a, :, cols] + lax.dot_general(
                    owned[a][...],
                    shard[...],
                    (((1,), (1,)), ((), ())),
                    preferred_element_type=F32,
                )
                total = total + lax.dot_general(
                    shard[:, mine],
                    shard[...],
                    (((0,), (0,)), ((), ())),
                    preferred_element_type=F32,
                )
        right_ref[a] = total


def result_kernel(ring, places, me_ref, root_ref, right_ref, *rest):
    count = len(places)
    shards, (old_ref, out_ref), rest = rest[:count], rest[count : count + 2], rest[count + 2 :]
    kept, sems = rest[:count], rest[count]
    copies = []
    for i in range(count):
        copies.append(pltpu.make_async_copy(shards[i], kept[i], sems.at[i]))
        copies[i].start()
    me = me_ref[0]
    rows = root_ref.shape[1]
    for a in range(root_ref.shape[0]):
        total = old_ref[a]
        for (block, k), shard in zip(places, shards):
            if block == a:
                total = total + jnp.dot(
                    root_ref[a, :, columns(me, k, ring, rows)],
                    shard[...],
                    preferred_element_type=F32,
                )
        result = jnp.dot(total.astype(BF16), right_ref[a], preferred_element_type=F32)
        put_pieces(out_ref, a, result.astype(BF16))
    for copy in copies:
        copy.wait()


def swap(pieces):
    return lax.all_to_all(pieces, "own", split_axis=0, concat_axis=0, tiled=True)


def local(partials, active_mask, block_owner, left_stats, right_stats, left_root, right_root):
    blocks, width = partials.shape[1], partials.shape[3]
    active_count, rows = left_stats.shape[:2]
    owners = lax.axis_size("own")
    ring = lax.axis_size("dp")
    me = lax.axis_index("dp").astype(jnp.int32)[None]
    keyed, live, chosen = slot_table(active_mask, block_owner, active_count, owners)
    wanted = jnp.where(live, keyed, -1)

    summed = sum_over_ring(partials[0], rows, owners)
    summed, right_root = lax.optimization_barrier((summed, right_root))
    right_full = lax.all_gather(right_root, "dp", axis=1, tiled=True)

    spread = swap(summed)
    piece = spread.shape[2:]
    picked = pick(spread.reshape((-1,) + piece), chosen)
    arrived = swap(picked.reshape((owners, active_count) + piece))
    slab = jax.ShapeDtypeStruct((rows, width), BF16)
    gradient = call(unpack_kernel, [slab] * active_count, [VMEM], (arrived,))
    gradient = list(gradient)

    flops = 2 * rows * rows * width
    slabs = jax.ShapeDtypeStruct((active_count, rows, width), F32)
    mixed = jnp.zeros(slabs.shape, F32)
    left_new, right_new = left_stats, right_stats

    def gram(places, shards, left, right):
        return call(
            functools.partial(gram_kernel, ring, places),
            [slabs, slabs],
            [SMEM] + [VMEM] * (len(shards) + active_count + 2),
            (me, *shards, *gradient, left, right),
            flops=2 * flops * len(shards),
        )

    held = {}
    places, shards = [(block, 0) for block in range(active_count)], list(gradient)
    for step in range(ring // 2):
        mixed = call(
            functools.partial(mix_kernel, ring, places),
            slabs,
            [SMEM, VMEM] + [VMEM] * (len(shards) + 1),
            (me, left_root, *shards, mixed),
            flops=flops * len(shards),
        )
        left_new, right_new = gram(places, shards, left_new, right_new)
        places, shards = [], []
        for block, way, place, length in chains(active_count, ring):
            if place == step:
                value = held.get((block, way), gradient[block])
                if step == ring // 2 - 1:
                    value, right_full = lax.optimization_barrier((value, right_full))
                held[block, way] = hop(value, way, ring)
                places.append((block, (-way * (place + 1)) % ring))
                shards.append(held[block, way])
    slab = jax.ShapeDtypeStruct((rows, width), BF16)
    result, *shards = call(
        functools.partial(result_kernel, ring, places),
        [jax.ShapeDtypeStruct((owners, active_count) + piece, BF16)] + [slab] * len(shards),
        [SMEM, VMEM, VMEM] + [VMEM] * (len(shards) + 1),
        (me, left_root, right_full, *shards, mixed),
        flops=flops * (len(shards) + ring * active_count),
        scratch=[pltpu.SemaphoreType.DMA((len(shards),))],
        limit=24,
        out_specs=[VMEM] + [HBM] * len(shards),
    )

    back = swap(result)
    placed = pick(back.reshape((-1,) + piece), wanted)
    returned = swap(placed.reshape((owners, blocks) + piece))
    preconditioned = call(
        unpack_kernel,
        jax.ShapeDtypeStruct((blocks, rows, width), BF16),
        [VMEM],
        (returned,),
    )

    left_new, right_new = gram(places, shards, left_new, right_new)
    return (preconditioned, left_new, right_new)


def solution(mesh):
    placed = (
        P("dp", "own", None, None),
        P(),
        P(),
        P("own", "dp", None),
        P("own", "dp", None),
        P("own", "dp", None),
        P("own", "dp", None),
    )
    return jax.shard_map(
        local,
        mesh=mesh,
        in_specs=placed,
        out_specs=(P("own", "dp", None), P("own", "dp", None), P("own", "dp", None)),
        check_vma=False,
    )
```

time: 255 us -> 219 us (0.86)
  waiting for transfers between devices: 184 us -> 89.3 us
  starting transfers between devices: 19.1 us -> 53.4 us
  blocking collectives: 15.2 us -> 36.1 us
  Pallas kernels: 2.51 us -> 18.1 us
  matrix products: 11.5 us -> 0 us
    reduce_scatter x1 -> x0, waiting for transfers between devices: 81.6 us -> none  [local(): lax.psum_scatter(partials[0], 'dp', scatter_dimension=1, tiled=True)]
    ppermute x0 -> x28, waiting for transfers between devices: none -> 69.1 us  [hop(): lax.ppermute(value, 'dp', [(i, (i + step) % ring) for i in range(ring)])]
    all_gather x1 -> x0, waiting for transfers between devices: 55.8 us -> none  [local(): full = lax.all_gather(gradient, 'dp', axis=1, tiled=True)]
    ppermute x0 -> x28, starting transfers between devices: none -> 40.4 us  [hop(): lax.ppermute(value, 'dp', [(i, (i + step) % ring) for i in range(ring)])]
    all_to_all x1 -> x2, blocking collectives: 15.2 us -> 36.1 us  [swap(): lax.all_to_all(pieces, 'own', split_axis=0, concat_axis=0, tiled=True)]
    pallas_call x2 -> x25, Pallas kernels: 2.51 us -> 18.1 us  [call(): pl.pallas_call(kernel, out_shape=out_shape, in_specs=in_specs, out_specs=...]
    all_gather x1, waiting for transfers between devices: 13 us -> 0.01 us  [local(): right_full = lax.all_gather(right_root, 'dp', axis=1, tiled=True)]
    all_to_all x3 -> x2, waiting for transfers between devices: 32.9 us -> 20.1 us  [swap(): lax.all_to_all(pieces, 'own', split_axis=0, concat_axis=0, tiled=True)]
  transfers between devices with their start and end apart: 6 -> 31, of which waited for: 6 -> 17; matrix products, arithmetic and copies ran while one was open for 5% -> 2% of each run, Pallas kernels for 0% -> 6%
where the time goes in v2:
time: 219 us; the launch traced here: 218 us
  waiting for transfers between devices  89.3 us (41%)
  starting transfers between devices  53.4 us (24%)
  blocking collectives  36.1 us (16%)
  Pallas kernels  18.1 us (8%)
  between operations  14.5 us (7%)
  local copies, waits for them, and re-layouts  6.76 us (3%)
    ppermute x28, waiting for transfers between devices, hop(): lax.ppermute(value, 'dp', [(i, (i + step) % ring) for i in range(ring)])  69.1 us
    ppermute x28, starting transfers between devices, hop(): lax.ppermute(value, 'dp', [(i, (i + step) % ring) for i in range(ring)])  40.4 us
    all_to_all x2, blocking collectives, swap(): lax.all_to_all(pieces, 'own', split_axis=0, concat_axis=0, tiled=True)  36.1 us
    all_to_all x2, waiting for transfers between devices, swap(): lax.all_to_all(pieces, 'own', split_axis=0, concat_axis=0, tiled=True)  20.1 us
    pallas_call x25, Pallas kernels, call(): pl.pallas_call(kernel, out_shape=out_shape, in_specs=in_specs, out_specs=...  18.1 us
    all_to_all x2, starting transfers between devices, swap(): lax.all_to_all(pieces, 'own', split_axis=0, concat_axis=0, tiled=True)  13 us
  transfers between devices with their start and end apart: 31, of which 17 were waited for; matrix products, arithmetic and copies ran while one was open for 2% of the time, Pallas kernels for 6%

profile of v2, /device:TPU:1, one launch (start us, length us, event | category | flops | bytes accessed | tf_op | source)
XLA Modules:
  0.0 218.4 jit_solution(3616085489002022188)
XLA Ops:
  7.2 1.6 dynamic-slice_bitcast_fusion.11
  8.8 6.5 %collective-permute-start.10 = (bf16[3,64,1024]{2,1,0:T(8,128)(2,1)S(1)}, bf16[3,64,1024]{2,1,0:T(8,128)(2,1)S(1)}, u32[]{:S(2)}, u32[]{:S(2)}) collective-permute-start(bf16[3,64,1024]{2,1,0:T(8,128)(2,1)S(1)} %get-tuple-element.33), channel_id=1, source_target_pairs={{0,224},{32,0},{64,32},{96,64},{128,96},{160,128},{192,160},{224,1... | collective-permute-start | bytes 1179656 | tf_op jit(solution)/shard_map/ppermute | solution.py:110
  15.3 2.7 %collective-permute-start.4 = (bf16[3,64,1024]{2,1,0:T(8,128)(2,1)S(1)}, bf16[3,64,1024]{2,1,0:T(8,128)(2,1)S(1)}, u32[]{:S(2)}, u32[]{:S(2)}) collective-permute-start(bf16[3,64,1024]{2,1,0:T(8,128)(2,1)S(1)} %get-tuple-element.31), channel_id=1, source_target_pairs={{0,224},{32,0},{64,32},{96,64},{128,96},{160,128},{192,160},{224,1... | collective-permute-start | bytes 1179656 | tf_op jit(solution)/shard_map/ppermute | solution.py:110
  18.0 2.6 %dynamic-slice_bitcast_fusion.1 = (bf16[3,64,1024]{2,1,0:T(8,128)(2,1)S(1)}, bf16[3,64,1024]{2,1,0:T(8,128)(2,1)S(1)}, bf16[3,64,1024]{2,1,0:T(8,128)(2,1)S(1)},...) fusion(bf16[1,3,1024,1024]{3,2,1,0:T(8,128)(2,1)} %param.7, ...), kind=kLoop, calls=%fused_computation.1 | loop fusion | bytes 7864360 | tf_op jit(solution)/shard_map/dynamic_slice | solution.py:134
  20.6 2.5 %collective-permute-done.10.got_ref = bf16[3,64,1024]{2,1,0:T(8,128)(2,1)S(1)} collective-permute-done((bf16[3,64,1024]{2,1,0:T(8,128)(2,1)S(1)}, bf16[3,64,1024]{2,1,0:T(8,128)(2,1)S(1)}, u32[]{:S(2)}, u32[]{:S(2)}) %collective-permute-start.10) | collective-permute-done | bytes 393248 | tf_op jit(solution)/shard_map/ppermute | solution.py:110
  23.2 3.5 %collective-permute-start.11 = (bf16[3,64,1024]{2,1,0:T(8,128)(2,1)S(1)}, bf16[3,64,1024]{2,1,0:T(8,128)(2,1)S(1)}, u32[]{:S(2)}, u32[]{:S(2)}) collective-permute-start(bf16[3,64,1024]{2,1,0:T(8,128)(2,1)S(1)} %shard_map.101), channel_id=1, source_target_pairs={{0,224},{32,0},{64,32},{96,64},{128,96},{160,128},{192,160},{224,1... | collective-permute-start | bytes 1179656 | tf_op jit(solution)/shard_map/ppermute | solution.py:110
  26.9 7.7 %collective-permute-done.7.got_ref = bf16[3,64,1024]{2,1,0:T(8,128)(2,1)S(1)} collective-permute-done((bf16[3,64,1024]{2,1,0:T(8,128)(2,1)S(1)}, bf16[3,64,1024]{2,1,0:T(8,128)(2,1)S(1)}, u32[]{:S(2)}, u32[]{:S(2)}) %collective-permute-start.7) | collective-permute-done | bytes 393248 | tf_op jit(solution)/shard_map/ppermute | solution.py:110
  34.9 2.7 %collective-permute-start.5 = (bf16[3,64,1024]{2,1,0:T(8,128)(2,1)S(1)}, bf16[3,64,1024]{2,1,0:T(8,128)(2,1)S(1)}, u32[]{:S(2)}, u32[]{:S(2)}) collective-permute-start(bf16[3,64,1024]{2,1,0:T(8,128)(2,1)S(1)} %shard_map.97), channel_id=1, source_target_pairs={{0,224},{32,0},{64,32},{96,64},{128,96},{160,128},{192,160},{224,1... | collective-permute-start | bytes 1179656 | tf_op jit(solution)/shard_map/ppermute | solution.py:110
  37.6 2.3 %collective-permute-done.11.got_ref = bf16[3,64,1024]{2,1,0:T(8,128)(2,1)S(1)} collective-permute-done((bf16[3,64,1024]{2,1,0:T(8,128)(2,1)S(1)}, bf16[3,64,1024]{2,1,0:T(8,128)(2,1)S(1)}, u32[]{:S(2)}, u32[]{:S(2)}) %collective-permute-start.11) | collective-permute-done | bytes 393248 | tf_op jit(solution)/shard_map/ppermute | solution.py:110
  40.0 3.5 %collective-permute-start.12 = (bf16[3,64,1024]{2,1,0:T(8,128)(2,1)S(1)}, bf16[3,64,1024]{2,1,0:T(8,128)(2,1)S(1)}, u32[]{:S(2)}, u32[]{:S(2)}) collective-permute-start(bf16[3,64,1024]{2,1,0:T(8,128)(2,1)S(1)} %shard_map.102), channel_id=1, source_target_pairs={{0,224},{32,0},{64,32},{96,64},{128,96},{160,128},{192,160},{224,1... | collective-permute-start | bytes 1179656 | tf_op jit(solution)/shard_map/ppermute | solution.py:110
  43.7 7.7 %collective-permute-done.8.got_ref = bf16[3,64,1024]{2,1,0:T(8,128)(2,1)S(1)} collective-permute-done((bf16[3,64,1024]{2,1,0:T(8,128)(2,1)S(1)}, bf16[3,64,1024]{2,1,0:T(8,128)(2,1)S(1)}, u32[]{:S(2)}, u32[]{:S(2)}) %collective-permute-start.8) | collective-permute-done | bytes 393248 | tf_op jit(solution)/shard_map/ppermute | solution.py:110
  51.8 2.7 %collective-permute-start.6 = (bf16[3,64,1024]{2,1,0:T(8,128)(2,1)S(1)}, bf16[3,64,1024]{2,1,0:T(8,128)(2,1)S(1)}, u32[]{:S(2)}, u32[]{:S(2)}) collective-permute-start(bf16[3,64,1024]{2,1,0:T(8,128)(2,1)S(1)} %shard_map.98), channel_id=1, source_target_pairs={{0,224},{32,0},{64,32},{96,64},{128,96},{160,128},{192,160},{224,1... | collective-permute-start | bytes 1179656 | tf_op jit(solution)/shard_map/ppermute | solution.py:110
  54.5 2.3 %collective-permute-done.12.got_ref = bf16[3,64,1024]{2,1,0:T(8,128)(2,1)S(1)} collective-permute-done((bf16[3,64,1024]{2,1,0:T(8,128)(2,1)S(1)}, bf16[3,64,1024]{2,1,0:T(8,128)(2,1)S(1)}, u32[]{:S(2)}, u32[]{:S(2)}) %collective-permute-start.12) | collective-permute-done | bytes 393248 | tf_op jit(solution)/shard_map/ppermute | solution.py:110
  56.9 3.5 %collective-permute-start.13 = (bf16[3,64,1024]{2,1,0:T(8,128)(2,1)S(1)}, bf16[3,64,1024]{2,1,0:T(8,128)(2,1)S(1)}, u32[]{:S(2)}, u32[]{:S(2)}) collective-permute-start(bf16[3,64,1024]{2,1,0:T(8,128)(2,1)S(1)} %shard_map.103), channel_id=1, source_target_pairs={{0,224},{32,0},{64,32},{96,64},{128,96},{160,128},{192,160},{224,1... | collective-permute-start | bytes 1179656 | tf_op jit(solution)/shard_map/ppermute | solution.py:110
  61.2 1.2 dynamic-slice_bitcast_fusion.own_ref
  62.4 5.9 %collective-permute-done.9.rest_2_ = bf16[3,64,1024]{2,1,0:T(8,128)(2,1)S(1)} collective-permute-done((bf16[3,64,1024]{2,1,0:T(8,128)(2,1)S(1)}, bf16[3,64,1024]{2,1,0:T(8,128)(2,1)S(1)}, u32[]{:S(2)}, u32[]{:S(2)}) %collective-permute-start.9) | collective-permute-done | bytes 393248 | tf_op jit(solution)/shard_map/ppermute | solution.py:110
  68.3 5.3 %collective-permute-done.13.rest_3_ = bf16[3,64,1024]{2,1,0:T(8,128)(2,1)S(1)} collective-permute-done((bf16[3,64,1024]{2,1,0:T(8,128)(2,1)S(1)}, bf16[3,64,1024]{2,1,0:T(8,128)(2,1)S(1)}, u32[]{:S(2)}, u32[]{:S(2)}) %collective-permute-start.13) | collective-permute-done | bytes 393248 | tf_op jit(solution)/shard_map/ppermute | solution.py:110
  73.6 3.1 %collective-permute-done.3.rest_0_ = bf16[3,64,1024]{2,1,0:T(8,128)(2,1)S(1)} collective-permute-done((bf16[3,64,1024]{2,1,0:T(8,128)(2,1)}, bf16[3,64,1024]{2,1,0:T(8,128)(2,1)S(1)}, u32[]{:S(2)}, u32[]{:S(2)}) %collective-permute-start.3) | collective-permute-done | bytes 393248 | tf_op jit(solution)/shard_map/ppermute | solution.py:110
  76.7 1.2 shard_map.104
  77.9 9.0 %all-to-all-start = ((bf16[32,3,16,256]{3,2,1,0:T(8,128)(2,1)}), bf16[32,3,16,256]{3,2,1,0:T(8,128)(2,1)S(1)}, u32[]{:S(2)}, u32[]{:S(2)}) async-start(bf16[32,3,16,256]{3,2,1,0:T(8,128)(2,1)} %shard_map.104), calls=%async_computation | async-start | bytes 1572864 | tf_op jit(solution)/shard_map/all_to_all | solution.py:235
  87.2 13.9 %all-to-all-done = bf16[32,3,16,256]{3,2,1,0:T(8,128)(2,1)S(1)} async-done(((bf16[32,3,16,256]{3,2,1,0:T(8,128)(2,1)}), bf16[32,3,16,256]{3,2,1,0:T(8,128)(2,1)S(1)}, u32[]{:S(2)}, u32[]{:S(2)}) %all-to-all-start) | async-done | bytes 786464 | tf_op jit(solution)/shard_map/all_to_all | solution.py:235
  101.9 15.2 %all_to_all.20.pieces_ref = bf16[32,2,16,256]{3,2,1,0:T(8,128)(2,1)S(1)} all-to-all(bf16[32,2,16,256]{3,2,1,0:T(8,128)(2,1)S(1)} %bitcast.37), channel_id=1, replica_groups=mesh['dp'=8,'own'=32] {'own'}, dimensions={0} | all-to-all | bytes 1048576 | tf_op jit(solution)/shard_map/all_to_all | solution.py:235
  117.2 2.7 %collective-permute-start.14 = (bf16[128,1024]{1,0:T(8,128)(2,1)S(1)}, bf16[128,1024]{1,0:T(8,128)(2,1)S(1)}, u32[]{:S(2)}, u32[]{:S(2)}) collective-permute-start(bf16[128,1024]{1,0:T(8,128)(2,1)S(1)} %get-tuple-element.35.rest_1_.rest_3_.rest_5_), channel_id=1, source_target_pairs={{0,224},{32,0},{64,32},{96,64},{128,96},{160,128},{192,160},{224,1... | collective-permute-start | bytes 786440 | tf_op jit(solution)/shard_map/ppermute | solution.py:110
  119.9 1.4 collective-permute-start.25
  121.3 10.8 %collective-permute-done.17.rest_0_ = bf16[128,1024]{1,0:T(8,128)(2,1)S(1)} collective-permute-done((bf16[128,1024]{1,0:T(8,128)(2,1)S(1)}, bf16[128,1024]{1,0:T(8,128)(2,1)S(1)}, u32[]{:S(2)}, u32[]{:S(2)}) %collective-permute-start.17) | collective-permute-done | bytes 262176 | tf_op jit(solution)/shard_map/ppermute | solution.py:110
  132.1 2.7 %collective-permute-start.15 = (bf16[128,1024]{1,0:T(8,128)(2,1)S(1)}, bf16[128,1024]{1,0:T(8,128)(2,1)S(1)}, u32[]{:S(2)}, u32[]{:S(2)}) collective-permute-start(bf16[128,1024]{1,0:T(8,128)(2,1)S(1)} %collective-permute-done.14.rest_1_), channel_id=1, source_target_pairs={{0,224},{32,0},{64,32},{96,64},{128,96},{160,128},{192,160},{224,1... | collective-permute-start | bytes 786440 | tf_op jit(solution)/shard_map/ppermute | solution.py:110
  134.9 5.8 %collective-permute-done.22.rest_2_ = bf16[128,1024]{1,0:T(8,128)(2,1)S(1)} collective-permute-done((bf16[128,1024]{1,0:T(8,128)(2,1)S(1)}, bf16[128,1024]{1,0:T(8,128)(2,1)S(1)}, u32[]{:S(2)}, u32[]{:S(2)}) %collective-permute-start.22) | collective-permute-done | bytes 262176 | tf_op jit(solution)/shard_map/ppermute | solution.py:110
  140.7 1.9 collective-permute-start.23
  142.5 5.4 %collective-permute-done.18.rest_0_ = bf16[128,1024]{1,0:T(8,128)(2,1)S(1)} collective-permute-done((bf16[128,1024]{1,0:T(8,128)(2,1)S(1)}, bf16[128,1024]{1,0:T(8,128)(2,1)S(1)}, u32[]{:S(2)}, u32[]{:S(2)}) %collective-permute-start.18) | collective-permute-done | bytes 262176 | tf_op jit(solution)/shard_map/ppermute | solution.py:110
  147.9 2.7 %collective-permute-start.16 = (bf16[128,1024]{1,0:T(8,128)(2,1)S(1)}, bf16[128,1024]{1,0:T(8,128)(2,1)}, u32[]{:S(2)}, u32[]{:S(2)}) collective-permute-start(bf16[128,1024]{1,0:T(8,128)(2,1)S(1)} %collective-permute-done.15.rest_1_), channel_id=1, source_target_pairs={{0,224},{32,0},{64,32},{96,64},{128,96},{160,128},{192,160},{224,1... | collective-permute-start | bytes 786440 | tf_op jit(solution)/shard_map/ppermute | solution.py:110
  150.6 1.3 collective-permute-done.23.rest_2_
  151.9 2.0 collective-permute-start.24
  153.9 5.4 %collective-permute-done.19.rest_0_ = bf16[128,1024]{1,0:T(8,128)(2,1)} collective-permute-done((bf16[128,1024]{1,0:T(8,128)(2,1)S(1)}, bf16[128,1024]{1,0:T(8,128)(2,1)}, u32[]{:S(2)}, u32[]{:S(2)}) %collective-permute-start.19) | collective-permute-done | bytes 262176 | tf_op jit(solution)/shard_map/ppermute | solution.py:110
  159.3 1.1 collective-permute-start.21
  161.6 1.7 shard_map.109.rest_4_
  163.3 1.5 collective-permute-done.27.rest_3_
  164.9 1.6 shard_map.110.rest_2_
  166.5 2.0 collective-permute-done.21.rest_1_
  168.6 1.1 shard_map.111
  169.7 20.9 %all_to_all.21 = bf16[32,2,16,256]{3,2,1,0:T(8,128)(2,1)S(1)} all-to-all(bf16[32,2,16,256]{3,2,1,0:T(8,128)(2,1)S(1)} %get-tuple-element.42), channel_id=1, replica_groups=mesh['dp'=8,'own'=32] {'own'}, dimensions={0} | all-to-all | bytes 1048576 | tf_op jit(solution)/shard_map/all_to_all | solution.py:235
  190.5 1.7 shard_map.112
  192.3 4.0 %all-to-all-start.3 = ((bf16[32,3,16,256]{3,2,1,0:T(8,128)(2,1)}), bf16[32,3,16,256]{3,2,1,0:T(8,128)(2,1)S(1)}, u32[]{:S(2)}, u32[]{:S(2)}) async-start(bf16[32,3,16,256]{3,2,1,0:T(8,128)(2,1)} %bitcast.19), calls=%async_computation.3 | async-start | bytes 1572864 | tf_op jit(solution)/shard_map/all_to_all | solution.py:235
  196.3 1.2 copy-done.3
  198.8 1.8 shard_map.116
  200.7 2.0 shard_map.117
  202.6 1.7 shard_map.118
  204.4 6.3 %all-to-all-done.3.pieces_ref = bf16[32,3,16,256]{3,2,1,0:T(8,128)(2,1)S(1)} async-done(((bf16[32,3,16,256]{3,2,1,0:T(8,128)(2,1)}), bf16[32,3,16,256]{3,2,1,0:T(8,128)(2,1)S(1)}, u32[]{:S(2)}, u32[]{:S(2)}) %all-to-all-start.3) | async-done | bytes 786464 | tf_op jit(solution)/shard_map/all_to_all | solution.py:235
  210.6 0.9 shard_map.113
  (86 shorter events, 5.8 us)
Async XLA Ops:
  7.2 152.1 %all-gather.2.cloned.1.call-start = ((), (), s32[]{:S(2)}) async-start(), calls=%async_computation.4 | async-start | bytes 4718592 | tf_op jit(solution)/shard_map/all_gather | solution.py:249
  8.8 14.3 %collective-permute-start.10 = (bf16[3,64,1024]{2,1,0:T(8,128)(2,1)S(1)}, bf16[3,64,1024]{2,1,0:T(8,128)(2,1)S(1)}, u32[]{:S(2)}, u32[]{:S(2)}) collective-permute-start(bf16[3,64,1024]{2,1,0:T(8,128)(2,1)S(1)} %get-tuple-element.33), channel_id=1, source_target_pairs={{0,224},{32,0},{64,32},{96,64},{128,96},{160,128},{192,160},{224,1... | collective-permute-start | bytes 1179656 | tf_op jit(solution)/shard_map/ppermute | solution.py:110
  15.3 11.4 %collective-permute-start = (bf16[3,64,1024]{2,1,0:T(8,128)(2,1)S(1)}, bf16[3,64,1024]{2,1,0:T(8,128)(2,1)S(1)}, u32[]{:S(2)}, u32[]{:S(2)}) collective-permute-start(bf16[3,64,1024]{2,1,0:T(8,128)(2,1)S(1)} %get-tuple-element.30), channel_id=1, source_target_pairs={{0,32},{32,64},{64,96},{96,128},{128,160},{160,192},{192,224},{224... | collective-permute-start | bytes 1179656 | tf_op jit(solution)/shard_map/ppermute | solution.py:110
  15.3 19.3 %collective-permute-start.7 = (bf16[3,64,1024]{2,1,0:T(8,128)(2,1)S(1)}, bf16[3,64,1024]{2,1,0:T(8,128)(2,1)S(1)}, u32[]{:S(2)}, u32[]{:S(2)}) collective-permute-start(bf16[3,64,1024]{2,1,0:T(8,128)(2,1)S(1)} %get-tuple-element.32), channel_id=1, source_target_pairs={{0,32},{32,64},{64,96},{96,128},{128,160},{160,192},{192,224},{224... | collective-permute-start | bytes 1179656 | tf_op jit(solution)/shard_map/ppermute | solution.py:110
  15.3 19.5 %collective-permute-start.4 = (bf16[3,64,1024]{2,1,0:T(8,128)(2,1)S(1)}, bf16[3,64,1024]{2,1,0:T(8,128)(2,1)S(1)}, u32[]{:S(2)}, u32[]{:S(2)}) collective-permute-start(bf16[3,64,1024]{2,1,0:T(8,128)(2,1)S(1)} %get-tuple-element.31), channel_id=1, source_target_pairs={{0,224},{32,0},{64,32},{96,64},{128,96},{160,128},{192,160},{224,1... | collective-permute-start | bytes 1179656 | tf_op jit(solution)/shard_map/ppermute | solution.py:110
  23.2 16.8 %collective-permute-start.11 = (bf16[3,64,1024]{2,1,0:T(8,128)(2,1)S(1)}, bf16[3,64,1024]{2,1,0:T(8,128)(2,1)S(1)}, u32[]{:S(2)}, u32[]{:S(2)}) collective-permute-start(bf16[3,64,1024]{2,1,0:T(8,128)(2,1)S(1)} %shard_map.101), channel_id=1, source_target_pairs={{0,224},{32,0},{64,32},{96,64},{128,96},{160,128},{192,160},{224,1... | collective-permute-start | bytes 1179656 | tf_op jit(solution)/shard_map/ppermute | solution.py:110
  26.8 16.8 %collective-permute-start.1 = (bf16[3,64,1024]{2,1,0:T(8,128)(2,1)S(1)}, bf16[3,64,1024]{2,1,0:T(8,128)(2,1)S(1)}, u32[]{:S(2)}, u32[]{:S(2)}) collective-permute-start(bf16[3,64,1024]{2,1,0:T(8,128)(2,1)S(1)} %shard_map.94), channel_id=1, source_target_pairs={{0,32},{32,64},{64,96},{96,128},{128,160},{160,192},{192,224},{224... | collective-permute-start | bytes 1179656 | tf_op jit(solution)/shard_map/ppermute | solution.py:110
  34.7 16.8 %collective-permute-start.8 = (bf16[3,64,1024]{2,1,0:T(8,128)(2,1)S(1)}, bf16[3,64,1024]{2,1,0:T(8,128)(2,1)S(1)}, u32[]{:S(2)}, u32[]{:S(2)}) collective-permute-start(bf16[3,64,1024]{2,1,0:T(8,128)(2,1)S(1)} %shard_map.99), channel_id=1, source_target_pairs={{0,32},{32,64},{64,96},{96,128},{128,160},{160,192},{192,224},{224... | collective-permute-start | bytes 1179656 | tf_op jit(solution)/shard_map/ppermute | solution.py:110
  34.9 16.7 %collective-permute-start.5 = (bf16[3,64,1024]{2,1,0:T(8,128)(2,1)S(1)}, bf16[3,64,1024]{2,1,0:T(8,128)(2,1)S(1)}, u32[]{:S(2)}, u32[]{:S(2)}) collective-permute-start(bf16[3,64,1024]{2,1,0:T(8,128)(2,1)S(1)} %shard_map.97), channel_id=1, source_target_pairs={{0,224},{32,0},{64,32},{96,64},{128,96},{160,128},{192,160},{224,1... | collective-permute-start | bytes 1179656 | tf_op jit(solution)/shard_map/ppermute | solution.py:110
  40.0 16.8 %collective-permute-start.12 = (bf16[3,64,1024]{2,1,0:T(8,128)(2,1)S(1)}, bf16[3,64,1024]{2,1,0:T(8,128)(2,1)S(1)}, u32[]{:S(2)}, u32[]{:S(2)}) collective-permute-start(bf16[3,64,1024]{2,1,0:T(8,128)(2,1)S(1)} %shard_map.102), channel_id=1, source_target_pairs={{0,224},{32,0},{64,32},{96,64},{128,96},{160,128},{192,160},{224,1... | collective-permute-start | bytes 1179656 | tf_op jit(solution)/shard_map/ppermute | solution.py:110
  43.5 43.4 %copy-start.17 = (s32[96]{0:T(128)S(1)}, s32[96]{0:T(128)}, u32[]{:S(2)}) copy-start(s32[96]{0:T(128)} %param.8) | copy-start | bytes 1156
  43.5 43.4 %copy-start.16 = (s32[96]{0:T(128)S(1)}, s32[96]{0:T(128)}, u32[]{:S(2)}) copy-start(s32[96]{0:T(128)} %param.9) | copy-start | bytes 1156
  43.6 16.8 %collective-permute-start.2 = (bf16[3,64,1024]{2,1,0:T(8,128)(2,1)S(1)}, bf16[3,64,1024]{2,1,0:T(8,128)(2,1)S(1)}, u32[]{:S(2)}, u32[]{:S(2)}) collective-permute-start(bf16[3,64,1024]{2,1,0:T(8,128)(2,1)S(1)} %shard_map.95), channel_id=1, source_target_pairs={{0,32},{32,64},{64,96},{96,128},{128,160},{160,192},{192,224},{224... | collective-permute-start | bytes 1179656 | tf_op jit(solution)/shard_map/ppermute | solution.py:110
  51.6 16.8 %collective-permute-start.9 = (bf16[3,64,1024]{2,1,0:T(8,128)(2,1)S(1)}, bf16[3,64,1024]{2,1,0:T(8,128)(2,1)S(1)}, u32[]{:S(2)}, u32[]{:S(2)}) collective-permute-start(bf16[3,64,1024]{2,1,0:T(8,128)(2,1)S(1)} %shard_map.100), channel_id=1, source_target_pairs={{0,32},{32,64},{64,96},{96,128},{128,160},{160,192},{192,224},{224... | collective-permute-start | bytes 1179656 | tf_op jit(solution)/shard_map/ppermute | solution.py:110
  51.8 16.6 %collective-permute-start.6 = (bf16[3,64,1024]{2,1,0:T(8,128)(2,1)S(1)}, bf16[3,64,1024]{2,1,0:T(8,128)(2,1)S(1)}, u32[]{:S(2)}, u32[]{:S(2)}) collective-permute-start(bf16[3,64,1024]{2,1,0:T(8,128)(2,1)S(1)} %shard_map.98), channel_id=1, source_target_pairs={{0,224},{32,0},{64,32},{96,64},{128,96},{160,128},{192,160},{224,1... | collective-permute-start | bytes 1179656 | tf_op jit(solution)/shard_map/ppermute | solution.py:110
  56.8 104.1 %copy-start = (bf16[2,128,1024]{2,1,0:T(8,128)(2,1)S(1)}, bf16[2,128,1024]{2,1,0:T(8,128)(2,1)}, u32[]{:S(2)}) copy-start(bf16[2,128,1024]{2,1,0:T(8,128)(2,1)} %root_ref.9) | copy-start | bytes 1572868
  56.9 16.8 %collective-permute-start.13 = (bf16[3,64,1024]{2,1,0:T(8,128)(2,1)S(1)}, bf16[3,64,1024]{2,1,0:T(8,128)(2,1)S(1)}, u32[]{:S(2)}, u32[]{:S(2)}) collective-permute-start(bf16[3,64,1024]{2,1,0:T(8,128)(2,1)S(1)} %shard_map.103), channel_id=1, source_target_pairs={{0,224},{32,0},{64,32},{96,64},{128,96},{160,128},{192,160},{224,1... | collective-permute-start | bytes 1179656 | tf_op jit(solution)/shard_map/ppermute | solution.py:110
  61.2 15.5 %collective-permute-start.3 = (bf16[3,64,1024]{2,1,0:T(8,128)(2,1)}, bf16[3,64,1024]{2,1,0:T(8,128)(2,1)S(1)}, u32[]{:S(2)}, u32[]{:S(2)}) collective-permute-start(bf16[3,64,1024]{2,1,0:T(8,128)(2,1)} %shard_map.96), channel_id=1, source_target_pairs={{0,32},{32,64},{64,96},{96,128},{128,160},{160,192},{192,224},{224... | collective-permute-start | bytes 1179656 | tf_op jit(solution)/shard_map/ppermute | solution.py:110
  77.9 23.2 %all-to-all-start = ((bf16[32,3,16,256]{3,2,1,0:T(8,128)(2,1)}), bf16[32,3,16,256]{3,2,1,0:T(8,128)(2,1)S(1)}, u32[]{:S(2)}, u32[]{:S(2)}) async-start(bf16[32,3,16,256]{3,2,1,0:T(8,128)(2,1)} %shard_map.104), calls=%async_computation | async-start | bytes 1572864 | tf_op jit(solution)/shard_map/all_to_all | solution.py:235
  117.1 15.0 %collective-permute-start.17 = (bf16[128,1024]{1,0:T(8,128)(2,1)S(1)}, bf16[128,1024]{1,0:T(8,128)(2,1)S(1)}, u32[]{:S(2)}, u32[]{:S(2)}) collective-permute-start(bf16[128,1024]{1,0:T(8,128)(2,1)S(1)} %get-tuple-element.36.rest_0_.rest_2_.rest_4_), channel_id=1, source_target_pairs={{0,32},{32,64},{64,96},{96,128},{128,160},{160,192},{192,224},{224... | collective-permute-start | bytes 786440 | tf_op jit(solution)/shard_map/ppermute | solution.py:110
  117.2 14.9 %collective-permute-start.14 = (bf16[128,1024]{1,0:T(8,128)(2,1)S(1)}, bf16[128,1024]{1,0:T(8,128)(2,1)S(1)}, u32[]{:S(2)}, u32[]{:S(2)}) collective-permute-start(bf16[128,1024]{1,0:T(8,128)(2,1)S(1)} %get-tuple-element.35.rest_1_.rest_3_.rest_5_), channel_id=1, source_target_pairs={{0,224},{32,0},{64,32},{96,64},{128,96},{160,128},{192,160},{224,1... | collective-permute-start | bytes 786440 | tf_op jit(solution)/shard_map/ppermute | solution.py:110
  119.9 20.8 %collective-permute-start.22 = (bf16[128,1024]{1,0:T(8,128)(2,1)S(1)}, bf16[128,1024]{1,0:T(8,128)(2,1)S(1)}, u32[]{:S(2)}, u32[]{:S(2)}) collective-permute-start(bf16[128,1024]{1,0:T(8,128)(2,1)S(1)} %get-tuple-element.36.rest_0_.rest_2_.rest_4_), channel_id=1, source_target_pairs={{0,224},{32,0},{64,32},{96,64},{128,96},{160,128},{192,160},{224,1... | collective-permute-start | bytes 786440 | tf_op jit(solution)/shard_map/ppermute | solution.py:110
  119.9 22.6 %collective-permute-start.25 = (bf16[128,1024]{1,0:T(8,128)(2,1)S(1)}, bf16[128,1024]{1,0:T(8,128)(2,1)S(1)}, u32[]{:S(2)}, u32[]{:S(2)}) collective-permute-start(bf16[128,1024]{1,0:T(8,128)(2,1)S(1)} %get-tuple-element.35.rest_1_.rest_3_.rest_5_), channel_id=1, source_target_pairs={{0,32},{32,64},{64,96},{96,128},{128,160},{160,192},{192,224},{224... | collective-permute-start | bytes 786440 | tf_op jit(solution)/shard_map/ppermute | solution.py:110
  132.1 15.8 %collective-permute-start.18 = (bf16[128,1024]{1,0:T(8,128)(2,1)S(1)}, bf16[128,1024]{1,0:T(8,128)(2,1)S(1)}, u32[]{:S(2)}, u32[]{:S(2)}) collective-permute-start(bf16[128,1024]{1,0:T(8,128)(2,1)S(1)} %collective-permute-done.17.rest_0_), channel_id=1, source_target_pairs={{0,32},{32,64},{64,96},{96,128},{128,160},{160,192},{192,224},{224... | collective-permute-start | bytes 786440 | tf_op jit(solution)/shard_map/ppermute | solution.py:110
  132.1 15.8 %collective-permute-start.15 = (bf16[128,1024]{1,0:T(8,128)(2,1)S(1)}, bf16[128,1024]{1,0:T(8,128)(2,1)S(1)}, u32[]{:S(2)}, u32[]{:S(2)}) collective-permute-start(bf16[128,1024]{1,0:T(8,128)(2,1)S(1)} %collective-permute-done.14.rest_1_), channel_id=1, source_target_pairs={{0,224},{32,0},{64,32},{96,64},{128,96},{160,128},{192,160},{224,1... | collective-permute-start | bytes 786440 | tf_op jit(solution)/shard_map/ppermute | solution.py:110
  140.6 25.8 %copy-start.4 = (bf16[128,1024]{1,0:T(8,128)(2,1)}, bf16[128,1024]{1,0:T(8,128)(2,1)S(1)}, u32[]{:S(2)}) copy-start(bf16[128,1024]{1,0:T(8,128)(2,1)S(1)} %collective-permute-done.22.rest_2_) | copy-start | bytes 786436
  140.7 11.2 %collective-permute-start.23 = (bf16[128,1024]{1,0:T(8,128)(2,1)S(1)}, bf16[128,1024]{1,0:T(8,128)(2,1)}, u32[]{:S(2)}, u32[]{:S(2)}) collective-permute-start(bf16[128,1024]{1,0:T(8,128)(2,1)S(1)} %collective-permute-done.22.rest_2_), channel_id=1, source_target_pairs={{0,224},{32,0},{64,32},{96,64},{128,96},{160,128},{192,160},{224,1... | collective-permute-start | bytes 786440 | tf_op jit(solution)/shard_map/ppermute | solution.py:110
  142.5 24.0 %copy-start.6 = (bf16[128,1024]{1,0:T(8,128)(2,1)}, bf16[128,1024]{1,0:T(8,128)(2,1)S(1)}, u32[]{:S(2)}) copy-start(bf16[128,1024]{1,0:T(8,128)(2,1)S(1)} %collective-permute-done.25.rest_3_) | copy-start | bytes 786436
  142.5 11.3 %collective-permute-start.26 = (bf16[128,1024]{1,0:T(8,128)(2,1)S(1)}, bf16[128,1024]{1,0:T(8,128)(2,1)}, u32[]{:S(2)}, u32[]{:S(2)}) collective-permute-start(bf16[128,1024]{1,0:T(8,128)(2,1)S(1)} %collective-permute-done.25.rest_3_), channel_id=1, source_target_pairs={{0,32},{32,64},{64,96},{96,128},{128,160},{160,192},{192,224},{224... | collective-permute-start | bytes 786440 | tf_op jit(solution)/shard_map/ppermute | solution.py:110
  147.9 18.6 %copy-start.8 = (bf16[128,1024]{1,0:T(8,128)(2,1)}, bf16[128,1024]{1,0:T(8,128)(2,1)S(1)}, u32[]{:S(2)}) copy-start(bf16[128,1024]{1,0:T(8,128)(2,1)S(1)} %collective-permute-done.18.rest_0_) | copy-start | bytes 786436
  147.9 11.3 %collective-permute-start.19 = (bf16[128,1024]{1,0:T(8,128)(2,1)S(1)}, bf16[128,1024]{1,0:T(8,128)(2,1)}, u32[]{:S(2)}, u32[]{:S(2)}) collective-permute-start(bf16[128,1024]{1,0:T(8,128)(2,1)S(1)} %collective-permute-done.18.rest_0_), channel_id=1, source_target_pairs={{0,32},{32,64},{64,96},{96,128},{128,160},{160,192},{192,224},{224... | collective-permute-start | bytes 786440 | tf_op jit(solution)/shard_map/ppermute | solution.py:110
  147.9 13.7 %copy-start.10 = (bf16[128,1024]{1,0:T(8,128)(2,1)}, bf16[128,1024]{1,0:T(8,128)(2,1)S(1)}, u32[]{:S(2)}) copy-start(bf16[128,1024]{1,0:T(8,128)(2,1)S(1)} %collective-permute-done.15.rest_1_) | copy-start | bytes 786436
  147.9 11.3 %collective-permute-start.16 = (bf16[128,1024]{1,0:T(8,128)(2,1)S(1)}, bf16[128,1024]{1,0:T(8,128)(2,1)}, u32[]{:S(2)}, u32[]{:S(2)}) collective-permute-start(bf16[128,1024]{1,0:T(8,128)(2,1)S(1)} %collective-permute-done.15.rest_1_), channel_id=1, source_target_pairs={{0,224},{32,0},{64,32},{96,64},{128,96},{160,128},{192,160},{224,1... | collective-permute-start | bytes 786440 | tf_op jit(solution)/shard_map/ppermute | solution.py:110
  151.9 11.4 %collective-permute-start.24 = (bf16[128,1024]{1,0:T(8,128)(2,1)}, bf16[128,1024]{1,0:T(8,128)(2,1)}, u32[]{:S(2)}, u32[]{:S(2)}) collective-permute-start(bf16[128,1024]{1,0:T(8,128)(2,1)} %collective-permute-done.23.rest_2_), channel_id=1, source_target_pairs={{0,224},{32,0},{64,32},{96,64},{128,96},{160,128},{192,160},{224,1... | collective-permute-start | bytes 786440 | tf_op jit(solution)/shard_map/ppermute | solution.py:110
  153.9 11.0 %collective-permute-start.27 = (bf16[128,1024]{1,0:T(8,128)(2,1)}, bf16[128,1024]{1,0:T(8,128)(2,1)}, u32[]{:S(2)}, u32[]{:S(2)}) collective-permute-start(bf16[128,1024]{1,0:T(8,128)(2,1)} %collective-permute-done.26.rest_3_), channel_id=1, source_target_pairs={{0,32},{32,64},{64,96},{96,128},{128,160},{160,192},{192,224},{224... | collective-permute-start | bytes 786440 | tf_op jit(solution)/shard_map/ppermute | solution.py:110
  159.3 9.3 %collective-permute-start.21 = (bf16[128,1024]{1,0:T(8,128)(2,1)}, bf16[128,1024]{1,0:T(8,128)(2,1)S(1)}, u32[]{:S(2)}, u32[]{:S(2)}) collective-permute-start(bf16[128,1024]{1,0:T(8,128)(2,1)} %collective-permute-done.16.rest_1_), channel_id=1, source_target_pairs={{0,224},{32,0},{64,32},{96,64},{128,96},{160,128},{192,160},{224,1... | collective-permute-start | bytes 786440 | tf_op jit(solution)/shard_map/ppermute | solution.py:110
  160.4 8.2 %collective-permute-start.20 = (bf16[128,1024]{1,0:T(8,128)(2,1)}, bf16[128,1024]{1,0:T(8,128)(2,1)S(1)}, u32[]{:S(2)}, u32[]{:S(2)}) collective-permute-start(bf16[128,1024]{1,0:T(8,128)(2,1)} %collective-permute-done.19.rest_0_), channel_id=1, source_target_pairs={{0,32},{32,64},{64,96},{96,128},{128,160},{160,192},{192,224},{224... | collective-permute-start | bytes 786440 | tf_op jit(solution)/shard_map/ppermute | solution.py:110
  161.1 7.4 %copy-start.1 = (bf16[2,1024,1024]{2,1,0:T(8,128)(2,1)S(1)}, bf16[2,1024,1024]{2,1,0:T(8,128)(2,1)}, u32[]{:S(2)}) copy-start(bf16[2,1024,1024]{2,1,0:T(8,128)(2,1)} %all-gather.2.cloned.1.call-done.right_ref) | copy-start | bytes 12582916
  163.3 33.0 %copy-start.2 = (f32[2,128,1024]{2,1,0:T(8,128)S(1)}, f32[2,128,1024]{2,1,0:T(8,128)}, u32[]{:S(2)}) copy-start(f32[2,128,1024]{2,1,0:T(8,128)} %rest_4_.1) | copy-start | bytes 3145732
  169.6 22.6 %copy-start.12 = (bf16[128,1024]{1,0:T(8,128)(2,1)}, bf16[128,1024]{1,0:T(8,128)(2,1)S(1)}, u32[]{:S(2)}) copy-start(bf16[128,1024]{1,0:T(8,128)(2,1)S(1)} %get-tuple-element.43.rest_0_) | copy-start | bytes 786436
  169.6 22.6 %copy-start.14 = (bf16[128,1024]{1,0:T(8,128)(2,1)}, bf16[128,1024]{1,0:T(8,128)(2,1)S(1)}, u32[]{:S(2)}) copy-start(bf16[128,1024]{1,0:T(8,128)(2,1)S(1)} %get-tuple-element.44.rest_1_) | copy-start | bytes 786436
  169.6 28.4 %copy-start.5 = (bf16[128,1024]{1,0:T(8,128)(2,1)S(1)}, bf16[128,1024]{1,0:T(8,128)(2,1)}, u32[]{:S(2)}) copy-start(bf16[128,1024]{1,0:T(8,128)(2,1)} %copy-done.4) | copy-start | bytes 786436
  169.7 28.4 %copy-start.7 = (bf16[128,1024]{1,0:T(8,128)(2,1)S(1)}, bf16[128,1024]{1,0:T(8,128)(2,1)}, u32[]{:S(2)}) copy-start(bf16[128,1024]{1,0:T(8,128)(2,1)} %copy-done.6) | copy-start | bytes 786436
  192.3 18.4 %all-to-all-start.3 = ((bf16[32,3,16,256]{3,2,1,0:T(8,128)(2,1)}), bf16[32,3,16,256]{3,2,1,0:T(8,128)(2,1)S(1)}, u32[]{:S(2)}, u32[]{:S(2)}) async-start(bf16[32,3,16,256]{3,2,1,0:T(8,128)(2,1)} %bitcast.19), calls=%async_computation.3 | async-start | bytes 1572864 | tf_op jit(solution)/shard_map/all_to_all | solution.py:235
  197.5 1.3 copy-start.9
  197.5 1.3 copy-start.11
  198.0 4.6 %copy-start.13 = (bf16[128,1024]{1,0:T(8,128)(2,1)S(1)}, bf16[128,1024]{1,0:T(8,128)(2,1)}, u32[]{:S(2)}) copy-start(bf16[128,1024]{1,0:T(8,128)(2,1)} %copy-done.12) | copy-start | bytes 786436
  198.0 4.6 %copy-start.15 = (bf16[128,1024]{1,0:T(8,128)(2,1)S(1)}, bf16[128,1024]{1,0:T(8,128)(2,1)}, u32[]{:S(2)}) copy-start(bf16[128,1024]{1,0:T(8,128)(2,1)} %copy-done.14) | copy-start | bytes 786436
  (1 other events, 1.2 us)
Sparse Core Ops, SparseCore 0:
  78.0 63.3 all-gather.1

commit v3 on v2

--- a/solution.py
+++ b/solution.py
@@ -94,6 +94,11 @@
     out_ref[...] = (got_ref[...].astype(F32) + piece_ref[...].astype(F32)).astype(BF16)
 
 
+def after_kernel(*refs):
+    source_ref, out_ref = refs[-2:]
+    out_ref[...] = source_ref[...]
+
+
 def pack_kernel(own_ref, *rest):
     got, out_ref = rest[:-1], rest[-1]
     count, rows = own_ref.shape[:2]
@@ -121,7 +126,7 @@
                     yield block, way, place, length
 
 
-def sum_over_ring(blocks, rows, owners):
+def sum_over_ring(blocks, rows, owners, root, tables):
     count, _, cols = blocks.shape
     ring = lax.axis_size("dp")
     me = lax.axis_index("dp").astype(jnp.int32)
@@ -137,7 +142,7 @@
     later, first = lax.optimization_barrier((me, first))
     pieces = {step[:3]: piece(later, *step) for step in order if step[2] > 0}
     own = lax.dynamic_slice(blocks, (0, later * rows, 0), (count, rows, cols))
-    held = {}
+    held, sent = {}, {}
     for stream, way, place, length in order:
         if place == 0:
             value = first[stream, way]
@@ -148,15 +153,21 @@
                 [VMEM, VMEM],
                 (held[stream, way], pieces[stream, way, place]),
             )
+        sent[stream, way] = value
         held[stream, way] = hop(value, way, ring)
+    earlier = [held[key] if key != (0, 1) else sent[key] for key in held]
+    after = jax.ShapeDtypeStruct(root.shape, root.dtype)
+    earlier += tables
+    root = call(after_kernel, after, [HBM] * len(earlier) + [VMEM], (*earlier, root))
     got = [held[stream, way] for stream in range(STREAMS) for way in (1, -1)]
     narrow = cols * (rows // TILE_ROWS) // owners
-    return call(
+    packed = call(
         pack_kernel,
         jax.ShapeDtypeStruct((owners, count, TILE_ROWS, narrow), BF16),
         [VMEM] * (1 + len(got)),
         (own, *got),
     )
+    return packed, root
 
 
 def columns(me, k, ring, width):
@@ -244,8 +255,9 @@
     keyed, live, chosen = slot_table(active_mask, block_owner, active_count, owners)
     wanted = jnp.where(live, keyed, -1)
 
-    summed = sum_over_ring(partials[0], rows, owners)
-    summed, right_root = lax.optimization_barrier((summed, right_root))
+    summed, right_root = sum_over_ring(
+        partials[0], rows, owners, right_root, [chosen, wanted]
+    )
     right_full = lax.all_gather(right_root, "dp", axis=1, tiled=True)
 
     spread = swap(summed)

time: 219 us -> 217 us (level)
  blocking collectives: 36.1 us -> 59 us
  waiting for transfers between devices: 89.3 us -> 67.4 us
  starting transfers between devices: 53.4 us -> 51.2 us
    all_to_all x2 -> x3, blocking collectives: 36.1 us -> 59 us  [swap(): lax.all_to_all(pieces, 'own', split_axis=0, concat_axis=0, tiled=True)]
    all_to_all x2 -> x1, waiting for transfers between devices: 20.1 us -> 6.25 us  [swap(): lax.all_to_all(pieces, 'own', split_axis=0, concat_axis=0, tiled=True)]
    all_to_all x2 -> x1, starting transfers between devices: 13 us -> 4.01 us  [swap(): lax.all_to_all(pieces, 'own', split_axis=0, concat_axis=0, tiled=True)]
    ppermute x28, waiting for transfers between devices: 69.1 us -> 61.2 us  [hop(): lax.ppermute(value, 'dp', [(i, (i + step) % ring) for i in range(ring)])]
    ppermute x28, starting transfers between devices: 40.4 us -> 47.1 us  [hop(): lax.ppermute(value, 'dp', [(i, (i + step) % ring) for i in range(ring)])]
    pallas_call x25 -> x26, Pallas kernels: 18.1 us -> 17.4 us  [call(): pl.pallas_call(kernel, out_shape=out_shape, in_specs=in_specs, out_specs=...]
  transfers between devices with their start and end apart: 31 -> 30, of which waited for: 17 -> 16; matrix products, arithmetic and copies ran while one was open for 2% -> 2% of each run, Pallas kernels for 6% -> 6%
where the time goes in v3:
time: 217 us
  waiting for transfers between devices  67.4 us (31%)
  blocking collectives  59 us (27%)
  starting transfers between devices  51.2 us (24%)
  Pallas kernels  17.4 us (8%)
  between operations  14.5 us (7%)
  local copies, waits for them, and re-layouts  6.8 us (3%)
    ppermute x28, waiting for transfers between devices, hop(): lax.ppermute(value, 'dp', [(i, (i + step) % ring) for i in range(ring)])  61.2 us
    all_to_all x3, blocking collectives, swap(): lax.all_to_all(pieces, 'own', split_axis=0, concat_axis=0, tiled=True)  59 us
    ppermute x28, starting transfers between devices, hop(): lax.ppermute(value, 'dp', [(i, (i + step) % ring) for i in range(ring)])  47.1 us
    pallas_call x26, Pallas kernels, call(): pl.pallas_call(kernel, out_shape=out_shape, in_specs=in_specs, out_specs=...  17.4 us
    all_to_all x1, waiting for transfers between devices, swap(): lax.all_to_all(pieces, 'own', split_axis=0, concat_axis=0, tiled=True)  6.25 us
  transfers between devices with their start and end apart: 30, of which 16 were waited for; matrix products, arithmetic and copies ran while one was open for 2% of the time, Pallas kernels for 6%

profile of v3, /device:TPU:1, one launch (start us, length us, event | category | flops | bytes accessed | tf_op | source)
XLA Modules:
  0.0 216.6 jit_solution(18434442995717020724)
XLA Ops:
  7.2 1.6 dynamic-slice_bitcast_fusion.11
  8.8 6.5 %collective-permute-start.10 = (bf16[3,64,1024]{2,1,0:T(8,128)(2,1)S(1)}, bf16[3,64,1024]{2,1,0:T(8,128)(2,1)S(1)}, u32[]{:S(2)}, u32[]{:S(2)}) collective-permute-start(bf16[3,64,1024]{2,1,0:T(8,128)(2,1)S(1)} %get-tuple-element.31), channel_id=1, source_target_pairs={{0,224},{32,0},{64,32},{96,64},{128,96},{160,128},{192,160},{224,1... | collective-permute-start | bytes 1179656 | tf_op jit(solution)/shard_map/ppermute | solution.py:115
  15.3 2.7 %collective-permute-start.4 = (bf16[3,64,1024]{2,1,0:T(8,128)(2,1)S(1)}, bf16[3,64,1024]{2,1,0:T(8,128)(2,1)S(1)}, u32[]{:S(2)}, u32[]{:S(2)}) collective-permute-start(bf16[3,64,1024]{2,1,0:T(8,128)(2,1)S(1)} %get-tuple-element.29), channel_id=1, source_target_pairs={{0,224},{32,0},{64,32},{96,64},{128,96},{160,128},{192,160},{224,1... | collective-permute-start | bytes 1179656 | tf_op jit(solution)/shard_map/ppermute | solution.py:115
  18.0 2.6 %dynamic-slice_bitcast_fusion.1 = (bf16[3,64,1024]{2,1,0:T(8,128)(2,1)S(1)}, bf16[3,64,1024]{2,1,0:T(8,128)(2,1)S(1)}, bf16[3,64,1024]{2,1,0:T(8,128)(2,1)S(1)},...) fusion(bf16[1,3,1024,1024]{3,2,1,0:T(8,128)(2,1)} %param.7, ...), kind=kLoop, calls=%fused_computation.1 | loop fusion | bytes 7864360 | tf_op jit(solution)/shard_map/dynamic_slice | solution.py:139
  20.6 2.5 %collective-permute-done.10.got_ref = bf16[3,64,1024]{2,1,0:T(8,128)(2,1)S(1)} collective-permute-done((bf16[3,64,1024]{2,1,0:T(8,128)(2,1)S(1)}, bf16[3,64,1024]{2,1,0:T(8,128)(2,1)S(1)}, u32[]{:S(2)}, u32[]{:S(2)}) %collective-permute-start.10) | collective-permute-done | bytes 393248 | tf_op jit(solution)/shard_map/ppermute | solution.py:115
  23.2 3.5 %collective-permute-start.11 = (bf16[3,64,1024]{2,1,0:T(8,128)(2,1)S(1)}, bf16[3,64,1024]{2,1,0:T(8,128)(2,1)S(1)}, u32[]{:S(2)}, u32[]{:S(2)}) collective-permute-start(bf16[3,64,1024]{2,1,0:T(8,128)(2,1)S(1)} %shard_map.101), channel_id=1, source_target_pairs={{0,224},{32,0},{64,32},{96,64},{128,96},{160,128},{192,160},{224,1... | collective-permute-start | bytes 1179656 | tf_op jit(solution)/shard_map/ppermute | solution.py:115
  26.9 4.7 %collective-permute-done.4.got_ref = bf16[3,64,1024]{2,1,0:T(8,128)(2,1)S(1)} collective-permute-done((bf16[3,64,1024]{2,1,0:T(8,128)(2,1)S(1)}, bf16[3,64,1024]{2,1,0:T(8,128)(2,1)S(1)}, u32[]{:S(2)}, u32[]{:S(2)}) %collective-permute-start.4) | collective-permute-done | bytes 393248 | tf_op jit(solution)/shard_map/ppermute | solution.py:115
  31.6 3.5 %collective-permute-start.5 = (bf16[3,64,1024]{2,1,0:T(8,128)(2,1)S(1)}, bf16[3,64,1024]{2,1,0:T(8,128)(2,1)S(1)}, u32[]{:S(2)}, u32[]{:S(2)}) collective-permute-start(bf16[3,64,1024]{2,1,0:T(8,128)(2,1)S(1)} %shard_map.97), channel_id=1, source_target_pairs={{0,224},{32,0},{64,32},{96,64},{128,96},{160,128},{192,160},{224,1... | collective-permute-start | bytes 1179656 | tf_op jit(solution)/shard_map/ppermute | solution.py:115
  35.3 4.7 %collective-permute-done.11.got_ref = bf16[3,64,1024]{2,1,0:T(8,128)(2,1)S(1)} collective-permute-done((bf16[3,64,1024]{2,1,0:T(8,128)(2,1)S(1)}, bf16[3,64,1024]{2,1,0:T(8,128)(2,1)S(1)}, u32[]{:S(2)}, u32[]{:S(2)}) %collective-permute-start.11) | collective-permute-done | bytes 393248 | tf_op jit(solution)/shard_map/ppermute | solution.py:115
  40.0 3.5 %collective-permute-start.12 = (bf16[3,64,1024]{2,1,0:T(8,128)(2,1)S(1)}, bf16[3,64,1024]{2,1,0:T(8,128)(2,1)S(1)}, u32[]{:S(2)}, u32[]{:S(2)}) collective-permute-start(bf16[3,64,1024]{2,1,0:T(8,128)(2,1)S(1)} %shard_map.102), channel_id=1, source_target_pairs={{0,224},{32,0},{64,32},{96,64},{128,96},{160,128},{192,160},{224,1... | collective-permute-start | bytes 1179656 | tf_op jit(solution)/shard_map/ppermute | solution.py:115
  43.7 4.6 %collective-permute-done.5.got_ref = bf16[3,64,1024]{2,1,0:T(8,128)(2,1)S(1)} collective-permute-done((bf16[3,64,1024]{2,1,0:T(8,128)(2,1)S(1)}, bf16[3,64,1024]{2,1,0:T(8,128)(2,1)S(1)}, u32[]{:S(2)}, u32[]{:S(2)}) %collective-permute-start.5) | collective-permute-done | bytes 393248 | tf_op jit(solution)/shard_map/ppermute | solution.py:115
  48.5 3.5 %collective-permute-start.6 = (bf16[3,64,1024]{2,1,0:T(8,128)(2,1)S(1)}, bf16[3,64,1024]{2,1,0:T(8,128)(2,1)S(1)}, u32[]{:S(2)}, u32[]{:S(2)}) collective-permute-start(bf16[3,64,1024]{2,1,0:T(8,128)(2,1)S(1)} %shard_map.98), channel_id=1, source_target_pairs={{0,224},{32,0},{64,32},{96,64},{128,96},{160,128},{192,160},{224,1... | collective-permute-start | bytes 1179656 | tf_op jit(solution)/shard_map/ppermute | solution.py:115
  52.1 4.7 %collective-permute-done.12.got_ref = bf16[3,64,1024]{2,1,0:T(8,128)(2,1)S(1)} collective-permute-done((bf16[3,64,1024]{2,1,0:T(8,128)(2,1)S(1)}, bf16[3,64,1024]{2,1,0:T(8,128)(2,1)S(1)}, u32[]{:S(2)}, u32[]{:S(2)}) %collective-permute-start.12) | collective-permute-done | bytes 393248 | tf_op jit(solution)/shard_map/ppermute | solution.py:115
  56.9 3.5 %collective-permute-start.13 = (bf16[3,64,1024]{2,1,0:T(8,128)(2,1)S(1)}, bf16[3,64,1024]{2,1,0:T(8,128)(2,1)S(1)}, u32[]{:S(2)}, u32[]{:S(2)}) collective-permute-start(bf16[3,64,1024]{2,1,0:T(8,128)(2,1)S(1)} %shard_map.103), channel_id=1, source_target_pairs={{0,224},{32,0},{64,32},{96,64},{128,96},{160,128},{192,160},{224,1... | collective-permute-start | bytes 1179656 | tf_op jit(solution)/shard_map/ppermute | solution.py:115
  60.7 7.6 %collective-permute-done.2.got_ref = bf16[3,64,1024]{2,1,0:T(8,128)(2,1)S(1)} collective-permute-done((bf16[3,64,1024]{2,1,0:T(8,128)(2,1)S(1)}, bf16[3,64,1024]{2,1,0:T(8,128)(2,1)S(1)}, u32[]{:S(2)}, u32[]{:S(2)}) %collective-permute-start.2) | collective-permute-done | bytes 393248 | tf_op jit(solution)/shard_map/ppermute | solution.py:115
  68.4 5.2 %collective-permute-done.13.rest_3_.refs_1_ = bf16[3,64,1024]{2,1,0:T(8,128)(2,1)S(1)} collective-permute-done((bf16[3,64,1024]{2,1,0:T(8,128)(2,1)S(1)}, bf16[3,64,1024]{2,1,0:T(8,128)(2,1)S(1)}, u32[]{:S(2)}, u32[]{:S(2)}) %collective-permute-start.13) | collective-permute-done | bytes 393248 | tf_op jit(solution)/shard_map/ppermute | solution.py:115
  73.6 0.8 shard_map.107
  74.8 1.2 dynamic-slice_bitcast_fusion.own_ref
  76.0 10.1 %collective-permute-done.3.rest_0_ = bf16[3,64,1024]{2,1,0:T(8,128)(2,1)S(1)} collective-permute-done((bf16[3,64,1024]{2,1,0:T(8,128)(2,1)S(1)}, bf16[3,64,1024]{2,1,0:T(8,128)(2,1)S(1)}, u32[]{:S(2)}, u32[]{:S(2)}) %collective-permute-start.3) | collective-permute-done | bytes 393248 | tf_op jit(solution)/shard_map/ppermute | solution.py:115
  86.4 23.3 %all_to_all.20 = bf16[32,3,16,256]{3,2,1,0:T(8,128)(2,1)S(1)} all-to-all(bf16[32,3,16,256]{3,2,1,0:T(8,128)(2,1)S(1)} %shard_map.104), channel_id=1, replica_groups=mesh['dp'=8,'own'=32] {'own'}, dimensions={0} | all-to-all | bytes 1572864 | tf_op jit(solution)/shard_map/all_to_all | solution.py:246
  109.7 0.7 shard_map.105
  110.4 15.2 %all_to_all.21.pieces_ref = bf16[32,2,16,256]{3,2,1,0:T(8,128)(2,1)S(1)} all-to-all(bf16[32,2,16,256]{3,2,1,0:T(8,128)(2,1)S(1)} %bitcast.36), channel_id=1, replica_groups=mesh['dp'=8,'own'=32] {'own'}, dimensions={0} | all-to-all | bytes 1048576 | tf_op jit(solution)/shard_map/all_to_all | solution.py:246
  125.7 2.7 %collective-permute-start.14 = (bf16[128,1024]{1,0:T(8,128)(2,1)S(1)}, bf16[128,1024]{1,0:T(8,128)(2,1)S(1)}, u32[]{:S(2)}, u32[]{:S(2)}) collective-permute-start(bf16[128,1024]{1,0:T(8,128)(2,1)S(1)} %get-tuple-element.32.rest_1_.rest_3_.rest_5_), channel_id=1, source_target_pairs={{0,224},{32,0},{64,32},{96,64},{128,96},{160,128},{192,160},{224,1... | collective-permute-start | bytes 786440 | tf_op jit(solution)/shard_map/ppermute | solution.py:115
  128.7 1.2 collective-permute-start.25
  129.9 4.5 %collective-permute-done.17.rest_0_ = bf16[128,1024]{1,0:T(8,128)(2,1)S(1)} collective-permute-done((bf16[128,1024]{1,0:T(8,128)(2,1)S(1)}, bf16[128,1024]{1,0:T(8,128)(2,1)S(1)}, u32[]{:S(2)}, u32[]{:S(2)}) %collective-permute-start.17) | collective-permute-done | bytes 262176 | tf_op jit(solution)/shard_map/ppermute | solution.py:115
  134.4 2.7 %collective-permute-start.15 = (bf16[128,1024]{1,0:T(8,128)(2,1)S(1)}, bf16[128,1024]{1,0:T(8,128)(2,1)S(1)}, u32[]{:S(2)}, u32[]{:S(2)}) collective-permute-start(bf16[128,1024]{1,0:T(8,128)(2,1)S(1)} %collective-permute-done.14.rest_1_), channel_id=1, source_target_pairs={{0,224},{32,0},{64,32},{96,64},{128,96},{160,128},{192,160},{224,1... | collective-permute-start | bytes 786440 | tf_op jit(solution)/shard_map/ppermute | solution.py:115
  137.1 1.9 collective-permute-done.22.rest_2_
  138.9 3.4 %collective-permute-start.23 = (bf16[128,1024]{1,0:T(8,128)(2,1)S(1)}, bf16[128,1024]{1,0:T(8,128)(2,1)}, u32[]{:S(2)}, u32[]{:S(2)}) collective-permute-start(bf16[128,1024]{1,0:T(8,128)(2,1)S(1)} %collective-permute-done.22.rest_2_), channel_id=1, source_target_pairs={{0,224},{32,0},{64,32},{96,64},{128,96},{160,128},{192,160},{224,1... | collective-permute-start | bytes 786440 | tf_op jit(solution)/shard_map/ppermute | solution.py:115
  142.4 3.2 %collective-permute-done.18.rest_0_ = bf16[128,1024]{1,0:T(8,128)(2,1)S(1)} collective-permute-done((bf16[128,1024]{1,0:T(8,128)(2,1)S(1)}, bf16[128,1024]{1,0:T(8,128)(2,1)S(1)}, u32[]{:S(2)}, u32[]{:S(2)}) %collective-permute-start.18) | collective-permute-done | bytes 262176 | tf_op jit(solution)/shard_map/ppermute | solution.py:115
  145.6 2.7 %collective-permute-start.16 = (bf16[128,1024]{1,0:T(8,128)(2,1)S(1)}, bf16[128,1024]{1,0:T(8,128)(2,1)}, u32[]{:S(2)}, u32[]{:S(2)}) collective-permute-start(bf16[128,1024]{1,0:T(8,128)(2,1)S(1)} %collective-permute-done.15.rest_1_), channel_id=1, source_target_pairs={{0,224},{32,0},{64,32},{96,64},{128,96},{160,128},{192,160},{224,1... | collective-permute-start | bytes 786440 | tf_op jit(solution)/shard_map/ppermute | solution.py:115
  148.3 1.9 collective-permute-done.23.rest_2_
  150.2 3.5 %collective-permute-start.24 = (bf16[128,1024]{1,0:T(8,128)(2,1)}, bf16[128,1024]{1,0:T(8,128)(2,1)}, u32[]{:S(2)}, u32[]{:S(2)}) collective-permute-start(bf16[128,1024]{1,0:T(8,128)(2,1)} %collective-permute-done.23.rest_2_), channel_id=1, source_target_pairs={{0,224},{32,0},{64,32},{96,64},{128,96},{160,128},{192,160},{224,1... | collective-permute-start | bytes 786440 | tf_op jit(solution)/shard_map/ppermute | solution.py:115
  153.7 1.3 collective-permute-done.19.rest_0_
  155.0 0.9 collective-permute-done.16.rest_1_
  155.8 3.5 %collective-permute-start.21 = (bf16[128,1024]{1,0:T(8,128)(2,1)}, bf16[128,1024]{1,0:T(8,128)(2,1)S(1)}, u32[]{:S(2)}, u32[]{:S(2)}) collective-permute-start(bf16[128,1024]{1,0:T(8,128)(2,1)} %collective-permute-done.16.rest_1_), channel_id=1, source_target_pairs={{0,224},{32,0},{64,32},{96,64},{128,96},{160,128},{192,160},{224,1... | collective-permute-start | bytes 786440 | tf_op jit(solution)/shard_map/ppermute | solution.py:115
  160.2 1.7 shard_map.110.rest_4_
  161.9 1.7 shard_map.111.rest_2_
  163.6 3.5 %collective-permute-done.21.rest_1_ = bf16[128,1024]{1,0:T(8,128)(2,1)S(1)} collective-permute-done((bf16[128,1024]{1,0:T(8,128)(2,1)}, bf16[128,1024]{1,0:T(8,128)(2,1)S(1)}, u32[]{:S(2)}, u32[]{:S(2)}) %collective-permute-start.21) | collective-permute-done | bytes 262176 | tf_op jit(solution)/shard_map/ppermute | solution.py:115
  167.1 1.1 shard_map.112
  168.2 20.5 %all_to_all.22 = bf16[32,2,16,256]{3,2,1,0:T(8,128)(2,1)S(1)} all-to-all(bf16[32,2,16,256]{3,2,1,0:T(8,128)(2,1)S(1)} %get-tuple-element.38), channel_id=1, replica_groups=mesh['dp'=8,'own'=32] {'own'}, dimensions={0} | all-to-all | bytes 1048576 | tf_op jit(solution)/shard_map/all_to_all | solution.py:246
  188.8 1.7 shard_map.113
  190.5 4.0 %all-to-all-start.3 = ((bf16[32,3,16,256]{3,2,1,0:T(8,128)(2,1)}), bf16[32,3,16,256]{3,2,1,0:T(8,128)(2,1)S(1)}, u32[]{:S(2)}, u32[]{:S(2)}) async-start(bf16[32,3,16,256]{3,2,1,0:T(8,128)(2,1)} %bitcast.19), calls=%async_computation.3 | async-start | bytes 1572864 | tf_op jit(solution)/shard_map/all_to_all | solution.py:246
  194.5 1.2 copy-done.3
  197.0 1.8 shard_map.117
  198.9 2.0 shard_map.118
  200.9 1.7 shard_map.119
  202.6 6.3 %all-to-all-done.3.pieces_ref = bf16[32,3,16,256]{3,2,1,0:T(8,128)(2,1)S(1)} async-done(((bf16[32,3,16,256]{3,2,1,0:T(8,128)(2,1)}), bf16[32,3,16,256]{3,2,1,0:T(8,128)(2,1)S(1)}, u32[]{:S(2)}, u32[]{:S(2)}) %all-to-all-start.3) | async-done | bytes 786464 | tf_op jit(solution)/shard_map/all_to_all | solution.py:246
  208.8 0.9 shard_map.114
  (88 shorter events, 4.7 us)
Async XLA Ops:
  7.2 147.8 %all-gather.2.cloned.1.call-start = ((), (), s32[]{:S(2)}) async-start(), calls=%async_computation.4 | async-start | bytes 4718592 | tf_op jit(solution)/shard_map/all_gather | solution.py:261
  8.8 14.3 %collective-permute-start.10 = (bf16[3,64,1024]{2,1,0:T(8,128)(2,1)S(1)}, bf16[3,64,1024]{2,1,0:T(8,128)(2,1)S(1)}, u32[]{:S(2)}, u32[]{:S(2)}) collective-permute-start(bf16[3,64,1024]{2,1,0:T(8,128)(2,1)S(1)} %get-tuple-element.31), channel_id=1, source_target_pairs={{0,224},{32,0},{64,32},{96,64},{128,96},{160,128},{192,160},{224,1... | collective-permute-start | bytes 1179656 | tf_op jit(solution)/shard_map/ppermute | solution.py:115
  15.3 11.4 %collective-permute-start.7 = (bf16[3,64,1024]{2,1,0:T(8,128)(2,1)S(1)}, bf16[3,64,1024]{2,1,0:T(8,128)(2,1)S(1)}, u32[]{:S(2)}, u32[]{:S(2)}) collective-permute-start(bf16[3,64,1024]{2,1,0:T(8,128)(2,1)S(1)} %get-tuple-element.30), channel_id=1, source_target_pairs={{0,32},{32,64},{64,96},{96,128},{128,160},{160,192},{192,224},{224... | collective-permute-start | bytes 1179656 | tf_op jit(solution)/shard_map/ppermute | solution.py:115
  15.3 16.2 %collective-permute-start.4 = (bf16[3,64,1024]{2,1,0:T(8,128)(2,1)S(1)}, bf16[3,64,1024]{2,1,0:T(8,128)(2,1)S(1)}, u32[]{:S(2)}, u32[]{:S(2)}) collective-permute-start(bf16[3,64,1024]{2,1,0:T(8,128)(2,1)S(1)} %get-tuple-element.29), channel_id=1, source_target_pairs={{0,224},{32,0},{64,32},{96,64},{128,96},{160,128},{192,160},{224,1... | collective-permute-start | bytes 1179656 | tf_op jit(solution)/shard_map/ppermute | solution.py:115
  18.0 17.1 %collective-permute-start = (bf16[3,64,1024]{2,1,0:T(8,128)(2,1)S(1)}, bf16[3,64,1024]{2,1,0:T(8,128)(2,1)S(1)}, u32[]{:S(2)}, u32[]{:S(2)}) collective-permute-start(bf16[3,64,1024]{2,1,0:T(8,128)(2,1)S(1)} %get-tuple-element.28), channel_id=1, source_target_pairs={{0,32},{32,64},{64,96},{96,128},{128,160},{160,192},{192,224},{224... | collective-permute-start | bytes 1179656 | tf_op jit(solution)/shard_map/ppermute | solution.py:115
  18.0 25.5 %copy-start.18 = (s32[96]{0:T(128)S(1)}, s32[96]{0:T(128)}, u32[]{:S(2)}) copy-start(s32[96]{0:T(128)} %param.8) | copy-start | bytes 1156
  20.6 39.8 %copy-start.17 = (s32[96]{0:T(128)S(1)}, s32[96]{0:T(128)}, u32[]{:S(2)}) copy-start(s32[96]{0:T(128)} %param.9) | copy-start | bytes 1156
  20.6 53.0 %copy-start.12 = (bf16[2,128,1024]{2,1,0:T(8,128)(2,1)S(1)}, bf16[2,128,1024]{2,1,0:T(8,128)(2,1)}, u32[]{:S(2)}) copy-start(bf16[2,128,1024]{2,1,0:T(8,128)(2,1)} %refs_6_.1) | copy-start | bytes 1572868
  23.2 16.8 %collective-permute-start.11 = (bf16[3,64,1024]{2,1,0:T(8,128)(2,1)S(1)}, bf16[3,64,1024]{2,1,0:T(8,128)(2,1)S(1)}, u32[]{:S(2)}, u32[]{:S(2)}) collective-permute-start(bf16[3,64,1024]{2,1,0:T(8,128)(2,1)S(1)} %shard_map.101), channel_id=1, source_target_pairs={{0,224},{32,0},{64,32},{96,64},{128,96},{160,128},{192,160},{224,1... | collective-permute-start | bytes 1179656 | tf_op jit(solution)/shard_map/ppermute | solution.py:115
  26.8 16.8 %collective-permute-start.8 = (bf16[3,64,1024]{2,1,0:T(8,128)(2,1)S(1)}, bf16[3,64,1024]{2,1,0:T(8,128)(2,1)S(1)}, u32[]{:S(2)}, u32[]{:S(2)}) collective-permute-start(bf16[3,64,1024]{2,1,0:T(8,128)(2,1)S(1)} %shard_map.99), channel_id=1, source_target_pairs={{0,32},{32,64},{64,96},{96,128},{128,160},{160,192},{192,224},{224... | collective-permute-start | bytes 1179656 | tf_op jit(solution)/shard_map/ppermute | solution.py:115
  31.6 16.8 %collective-permute-start.5 = (bf16[3,64,1024]{2,1,0:T(8,128)(2,1)S(1)}, bf16[3,64,1024]{2,1,0:T(8,128)(2,1)S(1)}, u32[]{:S(2)}, u32[]{:S(2)}) collective-permute-start(bf16[3,64,1024]{2,1,0:T(8,128)(2,1)S(1)} %shard_map.97), channel_id=1, source_target_pairs={{0,224},{32,0},{64,32},{96,64},{128,96},{160,128},{192,160},{224,1... | collective-permute-start | bytes 1179656 | tf_op jit(solution)/shard_map/ppermute | solution.py:115
  35.2 16.8 %collective-permute-start.1 = (bf16[3,64,1024]{2,1,0:T(8,128)(2,1)S(1)}, bf16[3,64,1024]{2,1,0:T(8,128)(2,1)S(1)}, u32[]{:S(2)}, u32[]{:S(2)}) collective-permute-start(bf16[3,64,1024]{2,1,0:T(8,128)(2,1)S(1)} %shard_map.94), channel_id=1, source_target_pairs={{0,32},{32,64},{64,96},{96,128},{128,160},{160,192},{192,224},{224... | collective-permute-start | bytes 1179656 | tf_op jit(solution)/shard_map/ppermute | solution.py:115
  40.0 16.8 %collective-permute-start.12 = (bf16[3,64,1024]{2,1,0:T(8,128)(2,1)S(1)}, bf16[3,64,1024]{2,1,0:T(8,128)(2,1)S(1)}, u32[]{:S(2)}, u32[]{:S(2)}) collective-permute-start(bf16[3,64,1024]{2,1,0:T(8,128)(2,1)S(1)} %shard_map.102), channel_id=1, source_target_pairs={{0,224},{32,0},{64,32},{96,64},{128,96},{160,128},{192,160},{224,1... | collective-permute-start | bytes 1179656 | tf_op jit(solution)/shard_map/ppermute | solution.py:115
  43.6 24.8 %collective-permute-start.9 = (bf16[3,64,1024]{2,1,0:T(8,128)(2,1)S(1)}, bf16[3,64,1024]{2,1,0:T(8,128)(2,1)S(1)}, u32[]{:S(2)}, u32[]{:S(2)}) collective-permute-start(bf16[3,64,1024]{2,1,0:T(8,128)(2,1)S(1)} %shard_map.100), channel_id=1, source_target_pairs={{0,32},{32,64},{64,96},{96,128},{128,160},{160,192},{192,224},{224... | collective-permute-start | bytes 1179656 | tf_op jit(solution)/shard_map/ppermute | solution.py:115
  48.5 20.0 %collective-permute-start.6 = (bf16[3,64,1024]{2,1,0:T(8,128)(2,1)S(1)}, bf16[3,64,1024]{2,1,0:T(8,128)(2,1)S(1)}, u32[]{:S(2)}, u32[]{:S(2)}) collective-permute-start(bf16[3,64,1024]{2,1,0:T(8,128)(2,1)S(1)} %shard_map.98), channel_id=1, source_target_pairs={{0,224},{32,0},{64,32},{96,64},{128,96},{160,128},{192,160},{224,1... | collective-permute-start | bytes 1179656 | tf_op jit(solution)/shard_map/ppermute | solution.py:115
  52.0 16.3 %collective-permute-start.2 = (bf16[3,64,1024]{2,1,0:T(8,128)(2,1)S(1)}, bf16[3,64,1024]{2,1,0:T(8,128)(2,1)S(1)}, u32[]{:S(2)}, u32[]{:S(2)}) collective-permute-start(bf16[3,64,1024]{2,1,0:T(8,128)(2,1)S(1)} %shard_map.95), channel_id=1, source_target_pairs={{0,32},{32,64},{64,96},{96,128},{128,160},{160,192},{192,224},{224... | collective-permute-start | bytes 1179656 | tf_op jit(solution)/shard_map/ppermute | solution.py:115
  56.9 16.8 %collective-permute-start.13 = (bf16[3,64,1024]{2,1,0:T(8,128)(2,1)S(1)}, bf16[3,64,1024]{2,1,0:T(8,128)(2,1)S(1)}, u32[]{:S(2)}, u32[]{:S(2)}) collective-permute-start(bf16[3,64,1024]{2,1,0:T(8,128)(2,1)S(1)} %shard_map.103), channel_id=1, source_target_pairs={{0,224},{32,0},{64,32},{96,64},{128,96},{160,128},{192,160},{224,1... | collective-permute-start | bytes 1179656 | tf_op jit(solution)/shard_map/ppermute | solution.py:115
  73.6 85.8 %copy-start = (bf16[2,128,1024]{2,1,0:T(8,128)(2,1)S(1)}, bf16[2,128,1024]{2,1,0:T(8,128)(2,1)}, u32[]{:S(2)}) copy-start(bf16[2,128,1024]{2,1,0:T(8,128)(2,1)} %root_ref.9) | copy-start | bytes 1572868
  74.5 11.5 %collective-permute-start.3 = (bf16[3,64,1024]{2,1,0:T(8,128)(2,1)S(1)}, bf16[3,64,1024]{2,1,0:T(8,128)(2,1)S(1)}, u32[]{:S(2)}, u32[]{:S(2)}) collective-permute-start(bf16[3,64,1024]{2,1,0:T(8,128)(2,1)S(1)} %shard_map.96.refs_0_), channel_id=1, source_target_pairs={{0,32},{32,64},{64,96},{96,128},{128,160},{160,192},{192,224},{224... | collective-permute-start | bytes 1179656 | tf_op jit(solution)/shard_map/ppermute | solution.py:115
  125.7 8.7 %collective-permute-start.17 = (bf16[128,1024]{1,0:T(8,128)(2,1)S(1)}, bf16[128,1024]{1,0:T(8,128)(2,1)S(1)}, u32[]{:S(2)}, u32[]{:S(2)}) collective-permute-start(bf16[128,1024]{1,0:T(8,128)(2,1)S(1)} %get-tuple-element.33.rest_0_.rest_2_.rest_4_), channel_id=1, source_target_pairs={{0,32},{32,64},{64,96},{96,128},{128,160},{160,192},{192,224},{224... | collective-permute-start | bytes 786440 | tf_op jit(solution)/shard_map/ppermute | solution.py:115
  125.7 8.6 %collective-permute-start.14 = (bf16[128,1024]{1,0:T(8,128)(2,1)S(1)}, bf16[128,1024]{1,0:T(8,128)(2,1)S(1)}, u32[]{:S(2)}, u32[]{:S(2)}) collective-permute-start(bf16[128,1024]{1,0:T(8,128)(2,1)S(1)} %get-tuple-element.32.rest_1_.rest_3_.rest_5_), channel_id=1, source_target_pairs={{0,224},{32,0},{64,32},{96,64},{128,96},{160,128},{192,160},{224,1... | collective-permute-start | bytes 786440 | tf_op jit(solution)/shard_map/ppermute | solution.py:115
  128.4 10.5 %collective-permute-start.22 = (bf16[128,1024]{1,0:T(8,128)(2,1)S(1)}, bf16[128,1024]{1,0:T(8,128)(2,1)S(1)}, u32[]{:S(2)}, u32[]{:S(2)}) collective-permute-start(bf16[128,1024]{1,0:T(8,128)(2,1)S(1)} %get-tuple-element.33.rest_0_.rest_2_.rest_4_), channel_id=1, source_target_pairs={{0,224},{32,0},{64,32},{96,64},{128,96},{160,128},{192,160},{224,1... | collective-permute-start | bytes 786440 | tf_op jit(solution)/shard_map/ppermute | solution.py:115
  128.7 13.7 %collective-permute-start.25 = (bf16[128,1024]{1,0:T(8,128)(2,1)S(1)}, bf16[128,1024]{1,0:T(8,128)(2,1)S(1)}, u32[]{:S(2)}, u32[]{:S(2)}) collective-permute-start(bf16[128,1024]{1,0:T(8,128)(2,1)S(1)} %get-tuple-element.32.rest_1_.rest_3_.rest_5_), channel_id=1, source_target_pairs={{0,32},{32,64},{64,96},{96,128},{128,160},{160,192},{192,224},{224... | collective-permute-start | bytes 786440 | tf_op jit(solution)/shard_map/ppermute | solution.py:115
  134.4 11.2 %collective-permute-start.18 = (bf16[128,1024]{1,0:T(8,128)(2,1)S(1)}, bf16[128,1024]{1,0:T(8,128)(2,1)S(1)}, u32[]{:S(2)}, u32[]{:S(2)}) collective-permute-start(bf16[128,1024]{1,0:T(8,128)(2,1)S(1)} %collective-permute-done.17.rest_0_), channel_id=1, source_target_pairs={{0,32},{32,64},{64,96},{96,128},{128,160},{160,192},{192,224},{224... | collective-permute-start | bytes 786440 | tf_op jit(solution)/shard_map/ppermute | solution.py:115
  134.4 11.2 %collective-permute-start.15 = (bf16[128,1024]{1,0:T(8,128)(2,1)S(1)}, bf16[128,1024]{1,0:T(8,128)(2,1)S(1)}, u32[]{:S(2)}, u32[]{:S(2)}) collective-permute-start(bf16[128,1024]{1,0:T(8,128)(2,1)S(1)} %collective-permute-done.14.rest_1_), channel_id=1, source_target_pairs={{0,224},{32,0},{64,32},{96,64},{128,96},{160,128},{192,160},{224,1... | collective-permute-start | bytes 786440 | tf_op jit(solution)/shard_map/ppermute | solution.py:115
  138.9 24.7 %copy-start.4 = (bf16[128,1024]{1,0:T(8,128)(2,1)}, bf16[128,1024]{1,0:T(8,128)(2,1)S(1)}, u32[]{:S(2)}) copy-start(bf16[128,1024]{1,0:T(8,128)(2,1)S(1)} %collective-permute-done.22.rest_2_) | copy-start | bytes 786436
  138.9 11.3 %collective-permute-start.23 = (bf16[128,1024]{1,0:T(8,128)(2,1)S(1)}, bf16[128,1024]{1,0:T(8,128)(2,1)}, u32[]{:S(2)}, u32[]{:S(2)}) collective-permute-start(bf16[128,1024]{1,0:T(8,128)(2,1)S(1)} %collective-permute-done.22.rest_2_), channel_id=1, source_target_pairs={{0,224},{32,0},{64,32},{96,64},{128,96},{160,128},{192,160},{224,1... | collective-permute-start | bytes 786440 | tf_op jit(solution)/shard_map/ppermute | solution.py:115
  142.4 21.3 %copy-start.6 = (bf16[128,1024]{1,0:T(8,128)(2,1)}, bf16[128,1024]{1,0:T(8,128)(2,1)S(1)}, u32[]{:S(2)}) copy-start(bf16[128,1024]{1,0:T(8,128)(2,1)S(1)} %collective-permute-done.25.rest_3_) | copy-start | bytes 786436
  142.4 11.3 %collective-permute-start.26 = (bf16[128,1024]{1,0:T(8,128)(2,1)S(1)}, bf16[128,1024]{1,0:T(8,128)(2,1)}, u32[]{:S(2)}, u32[]{:S(2)}) collective-permute-start(bf16[128,1024]{1,0:T(8,128)(2,1)S(1)} %collective-permute-done.25.rest_3_), channel_id=1, source_target_pairs={{0,32},{32,64},{64,96},{96,128},{128,160},{160,192},{192,224},{224... | collective-permute-start | bytes 786440 | tf_op jit(solution)/shard_map/ppermute | solution.py:115
  145.6 18.0 %copy-start.8 = (bf16[128,1024]{1,0:T(8,128)(2,1)}, bf16[128,1024]{1,0:T(8,128)(2,1)S(1)}, u32[]{:S(2)}) copy-start(bf16[128,1024]{1,0:T(8,128)(2,1)S(1)} %collective-permute-done.18.rest_0_) | copy-start | bytes 786436
  145.6 9.3 %collective-permute-start.19 = (bf16[128,1024]{1,0:T(8,128)(2,1)S(1)}, bf16[128,1024]{1,0:T(8,128)(2,1)}, u32[]{:S(2)}, u32[]{:S(2)}) collective-permute-start(bf16[128,1024]{1,0:T(8,128)(2,1)S(1)} %collective-permute-done.18.rest_0_), channel_id=1, source_target_pairs={{0,32},{32,64},{64,96},{96,128},{128,160},{160,192},{192,224},{224... | collective-permute-start | bytes 786440 | tf_op jit(solution)/shard_map/ppermute | solution.py:115
  145.6 14.6 %copy-start.10 = (bf16[128,1024]{1,0:T(8,128)(2,1)}, bf16[128,1024]{1,0:T(8,128)(2,1)S(1)}, u32[]{:S(2)}) copy-start(bf16[128,1024]{1,0:T(8,128)(2,1)S(1)} %collective-permute-done.15.rest_1_) | copy-start | bytes 786436
  145.6 10.2 %collective-permute-start.16 = (bf16[128,1024]{1,0:T(8,128)(2,1)S(1)}, bf16[128,1024]{1,0:T(8,128)(2,1)}, u32[]{:S(2)}, u32[]{:S(2)}) collective-permute-start(bf16[128,1024]{1,0:T(8,128)(2,1)S(1)} %collective-permute-done.15.rest_1_), channel_id=1, source_target_pairs={{0,224},{32,0},{64,32},{96,64},{128,96},{160,128},{192,160},{224,1... | collective-permute-start | bytes 786440 | tf_op jit(solution)/shard_map/ppermute | solution.py:115
  150.2 11.7 %collective-permute-start.24 = (bf16[128,1024]{1,0:T(8,128)(2,1)}, bf16[128,1024]{1,0:T(8,128)(2,1)}, u32[]{:S(2)}, u32[]{:S(2)}) collective-permute-start(bf16[128,1024]{1,0:T(8,128)(2,1)} %collective-permute-done.23.rest_2_), channel_id=1, source_target_pairs={{0,224},{32,0},{64,32},{96,64},{128,96},{160,128},{192,160},{224,1... | collective-permute-start | bytes 786440 | tf_op jit(solution)/shard_map/ppermute | solution.py:115
  153.7 8.2 %collective-permute-start.27 = (bf16[128,1024]{1,0:T(8,128)(2,1)}, bf16[128,1024]{1,0:T(8,128)(2,1)}, u32[]{:S(2)}, u32[]{:S(2)}) collective-permute-start(bf16[128,1024]{1,0:T(8,128)(2,1)} %collective-permute-done.26.rest_3_), channel_id=1, source_target_pairs={{0,32},{32,64},{64,96},{96,128},{128,160},{160,192},{192,224},{224... | collective-permute-start | bytes 786440 | tf_op jit(solution)/shard_map/ppermute | solution.py:115
  155.8 11.3 %collective-permute-start.21 = (bf16[128,1024]{1,0:T(8,128)(2,1)}, bf16[128,1024]{1,0:T(8,128)(2,1)S(1)}, u32[]{:S(2)}, u32[]{:S(2)}) collective-permute-start(bf16[128,1024]{1,0:T(8,128)(2,1)} %collective-permute-done.16.rest_1_), channel_id=1, source_target_pairs={{0,224},{32,0},{64,32},{96,64},{128,96},{160,128},{192,160},{224,1... | collective-permute-start | bytes 786440 | tf_op jit(solution)/shard_map/ppermute | solution.py:115
  159.3 7.8 %collective-permute-start.20 = (bf16[128,1024]{1,0:T(8,128)(2,1)}, bf16[128,1024]{1,0:T(8,128)(2,1)S(1)}, u32[]{:S(2)}, u32[]{:S(2)}) collective-permute-start(bf16[128,1024]{1,0:T(8,128)(2,1)} %collective-permute-done.19.rest_0_), channel_id=1, source_target_pairs={{0,32},{32,64},{64,96},{96,128},{128,160},{160,192},{192,224},{224... | collective-permute-start | bytes 786440 | tf_op jit(solution)/shard_map/ppermute | solution.py:115
  159.7 7.4 %copy-start.1 = (bf16[2,1024,1024]{2,1,0:T(8,128)(2,1)S(1)}, bf16[2,1024,1024]{2,1,0:T(8,128)(2,1)}, u32[]{:S(2)}) copy-start(bf16[2,1024,1024]{2,1,0:T(8,128)(2,1)} %all-gather.2.cloned.1.call-done.right_ref) | copy-start | bytes 12582916
  161.9 32.6 %copy-start.2 = (f32[2,128,1024]{2,1,0:T(8,128)S(1)}, f32[2,128,1024]{2,1,0:T(8,128)}, u32[]{:S(2)}) copy-start(f32[2,128,1024]{2,1,0:T(8,128)} %rest_4_.1) | copy-start | bytes 3145732
  168.2 22.3 %copy-start.13 = (bf16[128,1024]{1,0:T(8,128)(2,1)}, bf16[128,1024]{1,0:T(8,128)(2,1)S(1)}, u32[]{:S(2)}) copy-start(bf16[128,1024]{1,0:T(8,128)(2,1)S(1)} %get-tuple-element.39.rest_0_) | copy-start | bytes 786436
  168.2 22.3 %copy-start.15 = (bf16[128,1024]{1,0:T(8,128)(2,1)}, bf16[128,1024]{1,0:T(8,128)(2,1)S(1)}, u32[]{:S(2)}) copy-start(bf16[128,1024]{1,0:T(8,128)(2,1)S(1)} %get-tuple-element.40.rest_1_) | copy-start | bytes 786436
  168.2 28.0 %copy-start.5 = (bf16[128,1024]{1,0:T(8,128)(2,1)S(1)}, bf16[128,1024]{1,0:T(8,128)(2,1)}, u32[]{:S(2)}) copy-start(bf16[128,1024]{1,0:T(8,128)(2,1)} %copy-done.4) | copy-start | bytes 786436
  168.2 28.0 %copy-start.7 = (bf16[128,1024]{1,0:T(8,128)(2,1)S(1)}, bf16[128,1024]{1,0:T(8,128)(2,1)}, u32[]{:S(2)}) copy-start(bf16[128,1024]{1,0:T(8,128)(2,1)} %copy-done.6) | copy-start | bytes 786436
  190.5 18.4 %all-to-all-start.3 = ((bf16[32,3,16,256]{3,2,1,0:T(8,128)(2,1)}), bf16[32,3,16,256]{3,2,1,0:T(8,128)(2,1)S(1)}, u32[]{:S(2)}, u32[]{:S(2)}) async-start(bf16[32,3,16,256]{3,2,1,0:T(8,128)(2,1)} %bitcast.19), calls=%async_computation.3 | async-start | bytes 1572864 | tf_op jit(solution)/shard_map/all_to_all | solution.py:246
  195.7 1.3 copy-start.9
  195.7 1.3 copy-start.11
  196.2 4.6 %copy-start.14 = (bf16[128,1024]{1,0:T(8,128)(2,1)S(1)}, bf16[128,1024]{1,0:T(8,128)(2,1)}, u32[]{:S(2)}) copy-start(bf16[128,1024]{1,0:T(8,128)(2,1)} %copy-done.13) | copy-start | bytes 786436
  196.2 4.6 %copy-start.16 = (bf16[128,1024]{1,0:T(8,128)(2,1)S(1)}, bf16[128,1024]{1,0:T(8,128)(2,1)}, u32[]{:S(2)}) copy-start(bf16[128,1024]{1,0:T(8,128)(2,1)} %copy-done.15) | copy-start | bytes 786436
  (1 other events, 1.2 us)
Sparse Core Ops, SparseCore 0:
  74.6 55.2 all-gather.1

commit v4 on v3

--- a/solution.py
+++ b/solution.py
@@ -8,7 +8,6 @@
 from jax.sharding import PartitionSpec as P
 
 TILE_ROWS = 16
-STREAMS = 2
 F32 = jnp.float32
 BF16 = jnp.bfloat16
 MIB = 1024 * 1024
@@ -101,14 +100,11 @@
 
 def pack_kernel(own_ref, *rest):
     got, out_ref = rest[:-1], rest[-1]
-    count, rows = own_ref.shape[:2]
-    part = got[0].shape[1]
-    for item in range(count):
-        for stream in range(rows // part):
-            total = own_ref[item, stream * part : (stream + 1) * part].astype(F32)
-            for ref in got[2 * stream : 2 * stream + 2]:
-                total = total + ref[item].astype(F32)
-            put_pieces(out_ref, item, total.astype(BF16), stream * part // TILE_ROWS)
+    for item in range(own_ref.shape[0]):
+        total = own_ref[item].astype(F32)
+        for ref in got[2 * item : 2 * item + 2]:
+            total = total + ref[0].astype(F32)
+        put_pieces(out_ref, item, total.astype(BF16))
 
 
 def hop(value, step, ring):
@@ -130,13 +126,12 @@
     count, _, cols = blocks.shape
     ring = lax.axis_size("dp")
     me = lax.axis_index("dp").astype(jnp.int32)
-    part = rows // STREAMS
-    shape = (count, part, cols)
-    order = list(chains(STREAMS, ring))
+    shape = (1, rows, cols)
+    order = list(chains(count, ring))
 
     def piece(me, stream, way, place, length):
         target = lax.rem(me + way * (length - place) + ring, ring)
-        return lax.dynamic_slice(blocks, (0, target * rows + stream * part, 0), shape)
+        return lax.dynamic_slice(blocks, (stream, target * rows, 0), shape)
 
     first = {step[:2]: piece(me, *step) for step in order if step[2] == 0}
     later, first = lax.optimization_barrier((me, first))
@@ -159,7 +154,7 @@
     after = jax.ShapeDtypeStruct(root.shape, root.dtype)
     earlier += tables
     root = call(after_kernel, after, [HBM] * len(earlier) + [VMEM], (*earlier, root))
-    got = [held[stream, way] for stream in range(STREAMS) for way in (1, -1)]
+    got = [held[stream, way] for stream in range(count) for way in (1, -1)]
     narrow = cols * (rows // TILE_ROWS) // owners
     packed = call(
         pack_kernel,

time: 217 us -> 216 us (level)
  starting transfers between devices: 51.2 us -> 40.1 us
  waiting for transfers between devices: 67.4 us -> 76.8 us
    ppermute x28 -> x35, starting transfers between devices: 47.1 us -> 36 us  [hop(): lax.ppermute(value, 'dp', [(i, (i + step) % ring) for i in range(ring)])]
    ppermute x28 -> x35, waiting for transfers between devices: 61.2 us -> 70.5 us  [hop(): lax.ppermute(value, 'dp', [(i, (i + step) % ring) for i in range(ring)])]
    pallas_call x26 -> x31, Pallas kernels: 17.4 us -> 17.3 us  [call(): pl.pallas_call(kernel, out_shape=out_shape, in_specs=in_specs, out_specs=...]
  transfers between devices with their start and end apart: 30 -> 37, of which waited for: 16 -> 20; matrix products, arithmetic and copies ran while one was open for 2% -> 2% of each run, Pallas kernels for 6% -> 6%
where the time goes in v4:
time: 216 us; the launch traced here: 215 us
  waiting for transfers between devices  76.8 us (36%)
  blocking collectives  59.3 us (27%)
  starting transfers between devices  40.1 us (19%)
  Pallas kernels  17.3 us (8%)
  between operations  14.6 us (7%)
  local copies, waits for them, and re-layouts  6.82 us (3%)
    ppermute x35, waiting for transfers between devices, hop(): lax.ppermute(value, 'dp', [(i, (i + step) % ring) for i in range(ring)])  70.5 us
    all_to_all x3, blocking collectives, swap(): lax.all_to_all(pieces, 'own', split_axis=0, concat_axis=0, tiled=True)  59.3 us
    ppermute x35, starting transfers between devices, hop(): lax.ppermute(value, 'dp', [(i, (i + step) % ring) for i in range(ring)])  36 us
    pallas_call x31, Pallas kernels, call(): pl.pallas_call(kernel, out_shape=out_shape, in_specs=in_specs, out_specs=...  17.3 us
    all_to_all x1, waiting for transfers between devices, swap(): lax.all_to_all(pieces, 'own', split_axis=0, concat_axis=0, tiled=True)  6.25 us
  transfers between devices with their start and end apart: 37, of which 20 were waited for; matrix products, arithmetic and copies ran while one was open for 2% of the time, Pallas kernels for 6%

profile of v4, /device:TPU:1, one launch (start us, length us, event | category | flops | bytes accessed | tf_op | source)
XLA Modules:
  0.0 215.2 jit_solution(9251965695660645896)
XLA Ops:
  7.2 1.5 dynamic-slice_bitcast_fusion.16
  8.7 2.5 %collective-permute-start.14 = (bf16[1,128,1024]{2,1,0:T(8,128)(2,1)S(1)}, bf16[1,128,1024]{2,1,0:T(8,128)(2,1)S(1)}, u32[]{:S(2)}, u32[]{:S(2)}) collective-permute-start(bf16[1,128,1024]{2,1,0:T(8,128)(2,1)S(1)} %get-tuple-element.34), channel_id=1, source_target_pairs={{0,32},{32,64},{64,96},{96,128},{128,160},{160,192},{192,224},{224... | collective-permute-start | bytes 786440 | tf_op jit(solution)/shard_map/ppermute | solution.py:111
  11.3 4.0 %collective-permute-start.10 = (bf16[1,128,1024]{2,1,0:T(8,128)(2,1)S(1)}, bf16[1,128,1024]{2,1,0:T(8,128)(2,1)S(1)}, u32[]{:S(2)}, u32[]{:S(2)}) collective-permute-start(bf16[1,128,1024]{2,1,0:T(8,128)(2,1)S(1)} %get-tuple-element.33), channel_id=1, source_target_pairs={{0,224},{32,0},{64,32},{96,64},{128,96},{160,128},{192,160},{224,1... | collective-permute-start | bytes 786440 | tf_op jit(solution)/shard_map/ppermute | solution.py:111
  15.3 2.7 %collective-permute-start.18 = (bf16[1,128,1024]{2,1,0:T(8,128)(2,1)S(1)}, bf16[1,128,1024]{2,1,0:T(8,128)(2,1)S(1)}, u32[]{:S(2)}, u32[]{:S(2)}) collective-permute-start(bf16[1,128,1024]{2,1,0:T(8,128)(2,1)S(1)} %get-tuple-element.35), channel_id=1, source_target_pairs={{0,224},{32,0},{64,32},{96,64},{128,96},{160,128},{192,160},{224,1... | collective-permute-start | bytes 786440 | tf_op jit(solution)/shard_map/ppermute | solution.py:111
  18.0 2.7 %dynamic-slice_bitcast_fusion.1 = (bf16[1,128,1024]{2,1,0:T(8,128)(2,1)S(1)}, bf16[1,128,1024]{2,1,0:T(8,128)(2,1)S(1)}, bf16[1,128,1024]{2,1,0:T(8,128)(2,1)S(1...) fusion(bf16[1,3,1024,1024]{3,2,1,0:T(8,128)(2,1)} %param.7, ...), kind=kLoop, calls=%fused_computation.1 | loop fusion | bytes 7864344 | tf_op jit(solution)/shard_map/dynamic_slice | solution.py:134
  21.2 2.3 %collective-permute-start.4 = (bf16[1,128,1024]{2,1,0:T(8,128)(2,1)S(1)}, bf16[1,128,1024]{2,1,0:T(8,128)(2,1)S(1)}, u32[]{:S(2)}, u32[]{:S(2)}) collective-permute-start(bf16[1,128,1024]{2,1,0:T(8,128)(2,1)S(1)} %get-tuple-element.31), channel_id=1, source_target_pairs={{0,224},{32,0},{64,32},{96,64},{128,96},{160,128},{192,160},{224,1... | collective-permute-start | bytes 786440 | tf_op jit(solution)/shard_map/ppermute | solution.py:111
  23.7 3.1 %collective-permute-done.got_ref = bf16[1,128,1024]{2,1,0:T(8,128)(2,1)S(1)} collective-permute-done((bf16[1,128,1024]{2,1,0:T(8,128)(2,1)S(1)}, bf16[1,128,1024]{2,1,0:T(8,128)(2,1)S(1)}, u32[]{:S(2)}, u32[]{:S(2)}) %collective-permute-start) | collective-permute-done | bytes 262176 | tf_op jit(solution)/shard_map/ppermute | solution.py:111
  26.8 1.1 collective-permute-start.11
  28.5 3.9 %collective-permute-done.7.got_ref = bf16[1,128,1024]{2,1,0:T(8,128)(2,1)S(1)} collective-permute-done((bf16[1,128,1024]{2,1,0:T(8,128)(2,1)S(1)}, bf16[1,128,1024]{2,1,0:T(8,128)(2,1)S(1)}, u32[]{:S(2)}, u32[]{:S(2)}) %collective-permute-start.7) | collective-permute-done | bytes 262176 | tf_op jit(solution)/shard_map/ppermute | solution.py:111
  32.5 1.1 collective-permute-start.19
  34.2 3.9 %collective-permute-done.15.got_ref = bf16[1,128,1024]{2,1,0:T(8,128)(2,1)S(1)} collective-permute-done((bf16[1,128,1024]{2,1,0:T(8,128)(2,1)S(1)}, bf16[1,128,1024]{2,1,0:T(8,128)(2,1)S(1)}, u32[]{:S(2)}, u32[]{:S(2)}) %collective-permute-start.15) | collective-permute-done | bytes 262176 | tf_op jit(solution)/shard_map/ppermute | solution.py:111
  38.1 1.1 collective-permute-start.5
  39.8 3.9 %collective-permute-done.1.got_ref = bf16[1,128,1024]{2,1,0:T(8,128)(2,1)S(1)} collective-permute-done((bf16[1,128,1024]{2,1,0:T(8,128)(2,1)S(1)}, bf16[1,128,1024]{2,1,0:T(8,128)(2,1)S(1)}, u32[]{:S(2)}, u32[]{:S(2)}) %collective-permute-start.1) | collective-permute-done | bytes 262176 | tf_op jit(solution)/shard_map/ppermute | solution.py:111
  43.7 1.1 collective-permute-start.12
  45.8 3.6 %collective-permute-done.8.got_ref = bf16[1,128,1024]{2,1,0:T(8,128)(2,1)S(1)} collective-permute-done((bf16[1,128,1024]{2,1,0:T(8,128)(2,1)S(1)}, bf16[1,128,1024]{2,1,0:T(8,128)(2,1)S(1)}, u32[]{:S(2)}, u32[]{:S(2)}) %collective-permute-start.8) | collective-permute-done | bytes 262176 | tf_op jit(solution)/shard_map/ppermute | solution.py:111
  49.3 1.1 collective-permute-start.20
  51.0 3.9 %collective-permute-done.16.got_ref = bf16[1,128,1024]{2,1,0:T(8,128)(2,1)S(1)} collective-permute-done((bf16[1,128,1024]{2,1,0:T(8,128)(2,1)S(1)}, bf16[1,128,1024]{2,1,0:T(8,128)(2,1)S(1)}, u32[]{:S(2)}, u32[]{:S(2)}) %collective-permute-start.16) | collective-permute-done | bytes 262176 | tf_op jit(solution)/shard_map/ppermute | solution.py:111
  54.9 1.1 collective-permute-start.6
  56.6 3.9 %collective-permute-done.2.got_ref = bf16[1,128,1024]{2,1,0:T(8,128)(2,1)S(1)} collective-permute-done((bf16[1,128,1024]{2,1,0:T(8,128)(2,1)S(1)}, bf16[1,128,1024]{2,1,0:T(8,128)(2,1)S(1)}, u32[]{:S(2)}, u32[]{:S(2)}) %collective-permute-start.2) | collective-permute-done | bytes 262176 | tf_op jit(solution)/shard_map/ppermute | solution.py:111
  60.6 1.1 collective-permute-start.13
  61.9 4.3 %collective-permute-done.9.rest_2_.refs_4_ = bf16[1,128,1024]{2,1,0:T(8,128)(2,1)S(1)} collective-permute-done((bf16[1,128,1024]{2,1,0:T(8,128)(2,1)S(1)}, bf16[1,128,1024]{2,1,0:T(8,128)(2,1)S(1)}, u32[]{:S(2)}, u32[]{:S(2)}) %collective-permute-start.9) | collective-permute-done | bytes 262176 | tf_op jit(solution)/shard_map/ppermute | solution.py:111
  66.2 5.6 %collective-permute-done.17.rest_4_.refs_2_ = bf16[1,128,1024]{2,1,0:T(8,128)(2,1)S(1)} collective-permute-done((bf16[1,128,1024]{2,1,0:T(8,128)(2,1)S(1)}, bf16[1,128,1024]{2,1,0:T(8,128)(2,1)S(1)}, u32[]{:S(2)}, u32[]{:S(2)}) %collective-permute-start.17) | collective-permute-done | bytes 262176 | tf_op jit(solution)/shard_map/ppermute | solution.py:111
  72.8 1.2 dynamic-slice_bitcast_fusion.own_ref
  73.9 6.6 %collective-permute-done.3.rest_0_ = bf16[1,128,1024]{2,1,0:T(8,128)(2,1)S(1)} collective-permute-done((bf16[1,128,1024]{2,1,0:T(8,128)(2,1)S(1)}, bf16[1,128,1024]{2,1,0:T(8,128)(2,1)S(1)}, u32[]{:S(2)}, u32[]{:S(2)}) %collective-permute-start.3) | collective-permute-done | bytes 262176 | tf_op jit(solution)/shard_map/ppermute | solution.py:111
  80.8 23.3 %all_to_all.20 = bf16[32,3,16,256]{3,2,1,0:T(8,128)(2,1)S(1)} all-to-all(bf16[32,3,16,256]{3,2,1,0:T(8,128)(2,1)S(1)} %shard_map.109), channel_id=1, replica_groups=mesh['dp'=8,'own'=32] {'own'}, dimensions={0} | all-to-all | bytes 1572864 | tf_op jit(solution)/shard_map/all_to_all | solution.py:241
  104.8 15.2 %all_to_all.21.pieces_ref = bf16[32,2,16,256]{3,2,1,0:T(8,128)(2,1)S(1)} all-to-all(bf16[32,2,16,256]{3,2,1,0:T(8,128)(2,1)S(1)} %bitcast.50), channel_id=1, replica_groups=mesh['dp'=8,'own'=32] {'own'}, dimensions={0} | all-to-all | bytes 1048576 | tf_op jit(solution)/shard_map/all_to_all | solution.py:241
  120.2 2.7 %collective-permute-start.21 = (bf16[128,1024]{1,0:T(8,128)(2,1)S(1)}, bf16[128,1024]{1,0:T(8,128)(2,1)S(1)}, u32[]{:S(2)}, u32[]{:S(2)}) collective-permute-start(bf16[128,1024]{1,0:T(8,128)(2,1)S(1)} %get-tuple-element.36.rest_1_.rest_3_.rest_5_), channel_id=1, source_target_pairs={{0,224},{32,0},{64,32},{96,64},{128,96},{160,128},{192,160},{224,1... | collective-permute-start | bytes 786440 | tf_op jit(solution)/shard_map/ppermute | solution.py:111
  122.9 1.4 collective-permute-start.32
  124.3 9.2 %collective-permute-done.24.rest_0_ = bf16[128,1024]{1,0:T(8,128)(2,1)S(1)} collective-permute-done((bf16[128,1024]{1,0:T(8,128)(2,1)S(1)}, bf16[128,1024]{1,0:T(8,128)(2,1)S(1)}, u32[]{:S(2)}, u32[]{:S(2)}) %collective-permute-start.24) | collective-permute-done | bytes 262176 | tf_op jit(solution)/shard_map/ppermute | solution.py:111
  133.5 2.7 %collective-permute-start.22 = (bf16[128,1024]{1,0:T(8,128)(2,1)S(1)}, bf16[128,1024]{1,0:T(8,128)(2,1)S(1)}, u32[]{:S(2)}, u32[]{:S(2)}) collective-permute-start(bf16[128,1024]{1,0:T(8,128)(2,1)S(1)} %collective-permute-done.21.rest_1_), channel_id=1, source_target_pairs={{0,224},{32,0},{64,32},{96,64},{128,96},{160,128},{192,160},{224,1... | collective-permute-start | bytes 786440 | tf_op jit(solution)/shard_map/ppermute | solution.py:111
  136.2 1.2 collective-permute-done.29.rest_2_
  137.4 1.8 collective-permute-start.30
  139.2 5.5 %collective-permute-done.25.rest_0_ = bf16[128,1024]{1,0:T(8,128)(2,1)S(1)} collective-permute-done((bf16[128,1024]{1,0:T(8,128)(2,1)S(1)}, bf16[128,1024]{1,0:T(8,128)(2,1)S(1)}, u32[]{:S(2)}, u32[]{:S(2)}) %collective-permute-start.25) | collective-permute-done | bytes 262176 | tf_op jit(solution)/shard_map/ppermute | solution.py:111
  144.7 2.7 %collective-permute-start.23 = (bf16[128,1024]{1,0:T(8,128)(2,1)S(1)}, bf16[128,1024]{1,0:T(8,128)(2,1)}, u32[]{:S(2)}, u32[]{:S(2)}) collective-permute-start(bf16[128,1024]{1,0:T(8,128)(2,1)S(1)} %collective-permute-done.22.rest_1_), channel_id=1, source_target_pairs={{0,224},{32,0},{64,32},{96,64},{128,96},{160,128},{192,160},{224,1... | collective-permute-start | bytes 786440 | tf_op jit(solution)/shard_map/ppermute | solution.py:111
  147.4 1.3 collective-permute-done.30.rest_2_
  150.5 5.6 %collective-permute-done.26.rest_0_ = bf16[128,1024]{1,0:T(8,128)(2,1)} collective-permute-done((bf16[128,1024]{1,0:T(8,128)(2,1)S(1)}, bf16[128,1024]{1,0:T(8,128)(2,1)}, u32[]{:S(2)}, u32[]{:S(2)}) %collective-permute-start.26) | collective-permute-done | bytes 262176 | tf_op jit(solution)/shard_map/ppermute | solution.py:111
  158.4 1.7 shard_map.115.rest_4_
  160.1 1.3 collective-permute-done.34.rest_3_
  161.5 1.6 shard_map.116.rest_2_
  163.1 2.2 %collective-permute-done.28.rest_1_ = bf16[128,1024]{1,0:T(8,128)(2,1)S(1)} collective-permute-done((bf16[128,1024]{1,0:T(8,128)(2,1)}, bf16[128,1024]{1,0:T(8,128)(2,1)S(1)}, u32[]{:S(2)}, u32[]{:S(2)}) %collective-permute-start.28) | collective-permute-done | bytes 262176 | tf_op jit(solution)/shard_map/ppermute | solution.py:111
  166.5 20.9 %all_to_all.22 = bf16[32,2,16,256]{3,2,1,0:T(8,128)(2,1)S(1)} all-to-all(bf16[32,2,16,256]{3,2,1,0:T(8,128)(2,1)S(1)} %get-tuple-element.42), channel_id=1, replica_groups=mesh['dp'=8,'own'=32] {'own'}, dimensions={0} | all-to-all | bytes 1048576 | tf_op jit(solution)/shard_map/all_to_all | solution.py:241
  187.3 1.7 shard_map.118
  189.1 4.0 %all-to-all-start.3 = ((bf16[32,3,16,256]{3,2,1,0:T(8,128)(2,1)}), bf16[32,3,16,256]{3,2,1,0:T(8,128)(2,1)S(1)}, u32[]{:S(2)}, u32[]{:S(2)}) async-start(bf16[32,3,16,256]{3,2,1,0:T(8,128)(2,1)} %bitcast.26), calls=%async_computation.3 | async-start | bytes 1572864 | tf_op jit(solution)/shard_map/all_to_all | solution.py:241
  193.1 1.2 copy-done.3
  195.6 1.8 shard_map.122
  197.5 2.0 shard_map.123
  199.5 1.7 shard_map.124
  201.2 6.2 %all-to-all-done.3.pieces_ref = bf16[32,3,16,256]{3,2,1,0:T(8,128)(2,1)S(1)} async-done(((bf16[32,3,16,256]{3,2,1,0:T(8,128)(2,1)}), bf16[32,3,16,256]{3,2,1,0:T(8,128)(2,1)S(1)}, u32[]{:S(2)}, u32[]{:S(2)}) %all-to-all-start.3) | async-done | bytes 786464 | tf_op jit(solution)/shard_map/all_to_all | solution.py:241
  (107 shorter events, 14.0 us)
Async XLA Ops:
  7.2 148.9 %all-gather.2.cloned.1.call-start = ((), (), s32[]{:S(2)}) async-start(), calls=%async_computation.4 | async-start | bytes 4718592 | tf_op jit(solution)/shard_map/all_gather | solution.py:256
  8.7 12.5 %collective-permute-start.14 = (bf16[1,128,1024]{2,1,0:T(8,128)(2,1)S(1)}, bf16[1,128,1024]{2,1,0:T(8,128)(2,1)S(1)}, u32[]{:S(2)}, u32[]{:S(2)}) collective-permute-start(bf16[1,128,1024]{2,1,0:T(8,128)(2,1)S(1)} %get-tuple-element.34), channel_id=1, source_target_pairs={{0,32},{32,64},{64,96},{96,128},{128,160},{160,192},{192,224},{224... | collective-permute-start | bytes 786440 | tf_op jit(solution)/shard_map/ppermute | solution.py:111
  11.3 12.3 %collective-permute-start.10 = (bf16[1,128,1024]{2,1,0:T(8,128)(2,1)S(1)}, bf16[1,128,1024]{2,1,0:T(8,128)(2,1)S(1)}, u32[]{:S(2)}, u32[]{:S(2)}) collective-permute-start(bf16[1,128,1024]{2,1,0:T(8,128)(2,1)S(1)} %get-tuple-element.33), channel_id=1, source_target_pairs={{0,224},{32,0},{64,32},{96,64},{128,96},{160,128},{192,160},{224,1... | collective-permute-start | bytes 786440 | tf_op jit(solution)/shard_map/ppermute | solution.py:111
  15.3 11.6 %collective-permute-start = (bf16[1,128,1024]{2,1,0:T(8,128)(2,1)S(1)}, bf16[1,128,1024]{2,1,0:T(8,128)(2,1)S(1)}, u32[]{:S(2)}, u32[]{:S(2)}) collective-permute-start(bf16[1,128,1024]{2,1,0:T(8,128)(2,1)S(1)} %get-tuple-element.30), channel_id=1, source_target_pairs={{0,32},{32,64},{64,96},{96,128},{128,160},{160,192},{192,224},{224... | collective-permute-start | bytes 786440 | tf_op jit(solution)/shard_map/ppermute | solution.py:111
  15.3 12.8 %collective-permute-start.18 = (bf16[1,128,1024]{2,1,0:T(8,128)(2,1)S(1)}, bf16[1,128,1024]{2,1,0:T(8,128)(2,1)S(1)}, u32[]{:S(2)}, u32[]{:S(2)}) collective-permute-start(bf16[1,128,1024]{2,1,0:T(8,128)(2,1)S(1)} %get-tuple-element.35), channel_id=1, source_target_pairs={{0,224},{32,0},{64,32},{96,64},{128,96},{160,128},{192,160},{224,1... | collective-permute-start | bytes 786440 | tf_op jit(solution)/shard_map/ppermute | solution.py:111
  18.0 14.5 %collective-permute-start.7 = (bf16[1,128,1024]{2,1,0:T(8,128)(2,1)S(1)}, bf16[1,128,1024]{2,1,0:T(8,128)(2,1)S(1)}, u32[]{:S(2)}, u32[]{:S(2)}) collective-permute-start(bf16[1,128,1024]{2,1,0:T(8,128)(2,1)S(1)} %get-tuple-element.32), channel_id=1, source_target_pairs={{0,32},{32,64},{64,96},{96,128},{128,160},{160,192},{192,224},{224... | collective-permute-start | bytes 786440 | tf_op jit(solution)/shard_map/ppermute | solution.py:111
  18.0 27.5 %copy-start.18 = (s32[96]{0:T(128)S(1)}, s32[96]{0:T(128)}, u32[]{:S(2)}) copy-start(s32[96]{0:T(128)} %param.8) | copy-start | bytes 1156
  18.0 27.5 %copy-start.17 = (s32[96]{0:T(128)S(1)}, s32[96]{0:T(128)}, u32[]{:S(2)}) copy-start(s32[96]{0:T(128)} %param.9) | copy-start | bytes 1156
  20.7 51.1 %copy-start.12 = (bf16[2,128,1024]{2,1,0:T(8,128)(2,1)S(1)}, bf16[2,128,1024]{2,1,0:T(8,128)(2,1)}, u32[]{:S(2)}) copy-start(bf16[2,128,1024]{2,1,0:T(8,128)(2,1)} %refs_8_.1) | copy-start | bytes 1572868
  21.2 12.4 %collective-permute-start.4 = (bf16[1,128,1024]{2,1,0:T(8,128)(2,1)S(1)}, bf16[1,128,1024]{2,1,0:T(8,128)(2,1)S(1)}, u32[]{:S(2)}, u32[]{:S(2)}) collective-permute-start(bf16[1,128,1024]{2,1,0:T(8,128)(2,1)S(1)} %get-tuple-element.31), channel_id=1, source_target_pairs={{0,224},{32,0},{64,32},{96,64},{128,96},{160,128},{192,160},{224,1... | collective-permute-start | bytes 786440 | tf_op jit(solution)/shard_map/ppermute | solution.py:111
  23.6 14.5 %collective-permute-start.15 = (bf16[1,128,1024]{2,1,0:T(8,128)(2,1)S(1)}, bf16[1,128,1024]{2,1,0:T(8,128)(2,1)S(1)}, u32[]{:S(2)}, u32[]{:S(2)}) collective-permute-start(bf16[1,128,1024]{2,1,0:T(8,128)(2,1)S(1)} %shard_map.104), channel_id=1, source_target_pairs={{0,32},{32,64},{64,96},{96,128},{128,160},{160,192},{192,224},{224... | collective-permute-start | bytes 786440 | tf_op jit(solution)/shard_map/ppermute | solution.py:111
  26.8 12.4 %collective-permute-start.11 = (bf16[1,128,1024]{2,1,0:T(8,128)(2,1)S(1)}, bf16[1,128,1024]{2,1,0:T(8,128)(2,1)S(1)}, u32[]{:S(2)}, u32[]{:S(2)}) collective-permute-start(bf16[1,128,1024]{2,1,0:T(8,128)(2,1)S(1)} %shard_map.101), channel_id=1, source_target_pairs={{0,224},{32,0},{64,32},{96,64},{128,96},{160,128},{192,160},{224,1... | collective-permute-start | bytes 786440 | tf_op jit(solution)/shard_map/ppermute | solution.py:111
  28.1 15.6 %collective-permute-start.1 = (bf16[1,128,1024]{2,1,0:T(8,128)(2,1)S(1)}, bf16[1,128,1024]{2,1,0:T(8,128)(2,1)S(1)}, u32[]{:S(2)}, u32[]{:S(2)}) collective-permute-start(bf16[1,128,1024]{2,1,0:T(8,128)(2,1)S(1)} %shard_map.94), channel_id=1, source_target_pairs={{0,32},{32,64},{64,96},{96,128},{128,160},{160,192},{192,224},{224... | collective-permute-start | bytes 786440 | tf_op jit(solution)/shard_map/ppermute | solution.py:111
  32.5 12.4 %collective-permute-start.19 = (bf16[1,128,1024]{2,1,0:T(8,128)(2,1)S(1)}, bf16[1,128,1024]{2,1,0:T(8,128)(2,1)S(1)}, u32[]{:S(2)}, u32[]{:S(2)}) collective-permute-start(bf16[1,128,1024]{2,1,0:T(8,128)(2,1)S(1)} %shard_map.107), channel_id=1, source_target_pairs={{0,224},{32,0},{64,32},{96,64},{128,96},{160,128},{192,160},{224,1... | collective-permute-start | bytes 786440 | tf_op jit(solution)/shard_map/ppermute | solution.py:111
  33.7 15.6 %collective-permute-start.8 = (bf16[1,128,1024]{2,1,0:T(8,128)(2,1)S(1)}, bf16[1,128,1024]{2,1,0:T(8,128)(2,1)S(1)}, u32[]{:S(2)}, u32[]{:S(2)}) collective-permute-start(bf16[1,128,1024]{2,1,0:T(8,128)(2,1)S(1)} %shard_map.99), channel_id=1, source_target_pairs={{0,32},{32,64},{64,96},{96,128},{128,160},{160,192},{192,224},{224... | collective-permute-start | bytes 786440 | tf_op jit(solution)/shard_map/ppermute | solution.py:111
  38.1 12.4 %collective-permute-start.5 = (bf16[1,128,1024]{2,1,0:T(8,128)(2,1)S(1)}, bf16[1,128,1024]{2,1,0:T(8,128)(2,1)S(1)}, u32[]{:S(2)}, u32[]{:S(2)}) collective-permute-start(bf16[1,128,1024]{2,1,0:T(8,128)(2,1)S(1)} %shard_map.97), channel_id=1, source_target_pairs={{0,224},{32,0},{64,32},{96,64},{128,96},{160,128},{192,160},{224,1... | collective-permute-start | bytes 786440 | tf_op jit(solution)/shard_map/ppermute | solution.py:111
  39.3 15.6 %collective-permute-start.16 = (bf16[1,128,1024]{2,1,0:T(8,128)(2,1)S(1)}, bf16[1,128,1024]{2,1,0:T(8,128)(2,1)S(1)}, u32[]{:S(2)}, u32[]{:S(2)}) collective-permute-start(bf16[1,128,1024]{2,1,0:T(8,128)(2,1)S(1)} %shard_map.105), channel_id=1, source_target_pairs={{0,32},{32,64},{64,96},{96,128},{128,160},{160,192},{192,224},{224... | collective-permute-start | bytes 786440 | tf_op jit(solution)/shard_map/ppermute | solution.py:111
  43.7 12.4 %collective-permute-start.12 = (bf16[1,128,1024]{2,1,0:T(8,128)(2,1)S(1)}, bf16[1,128,1024]{2,1,0:T(8,128)(2,1)S(1)}, u32[]{:S(2)}, u32[]{:S(2)}) collective-permute-start(bf16[1,128,1024]{2,1,0:T(8,128)(2,1)S(1)} %shard_map.102), channel_id=1, source_target_pairs={{0,224},{32,0},{64,32},{96,64},{128,96},{160,128},{192,160},{224,1... | collective-permute-start | bytes 786440 | tf_op jit(solution)/shard_map/ppermute | solution.py:111
  44.9 15.6 %collective-permute-start.2 = (bf16[1,128,1024]{2,1,0:T(8,128)(2,1)S(1)}, bf16[1,128,1024]{2,1,0:T(8,128)(2,1)S(1)}, u32[]{:S(2)}, u32[]{:S(2)}) collective-permute-start(bf16[1,128,1024]{2,1,0:T(8,128)(2,1)S(1)} %shard_map.95), channel_id=1, source_target_pairs={{0,32},{32,64},{64,96},{96,128},{128,160},{160,192},{192,224},{224... | collective-permute-start | bytes 786440 | tf_op jit(solution)/shard_map/ppermute | solution.py:111
  49.3 12.6 %collective-permute-start.20 = (bf16[1,128,1024]{2,1,0:T(8,128)(2,1)S(1)}, bf16[1,128,1024]{2,1,0:T(8,128)(2,1)S(1)}, u32[]{:S(2)}, u32[]{:S(2)}) collective-permute-start(bf16[1,128,1024]{2,1,0:T(8,128)(2,1)S(1)} %shard_map.108), channel_id=1, source_target_pairs={{0,224},{32,0},{64,32},{96,64},{128,96},{160,128},{192,160},{224,1... | collective-permute-start | bytes 786440 | tf_op jit(solution)/shard_map/ppermute | solution.py:111
  50.5 15.6 %collective-permute-start.9 = (bf16[1,128,1024]{2,1,0:T(8,128)(2,1)S(1)}, bf16[1,128,1024]{2,1,0:T(8,128)(2,1)S(1)}, u32[]{:S(2)}, u32[]{:S(2)}) collective-permute-start(bf16[1,128,1024]{2,1,0:T(8,128)(2,1)S(1)} %shard_map.100), channel_id=1, source_target_pairs={{0,32},{32,64},{64,96},{96,128},{128,160},{160,192},{192,224},{224... | collective-permute-start | bytes 786440 | tf_op jit(solution)/shard_map/ppermute | solution.py:111
  54.9 11.2 %collective-permute-start.6 = (bf16[1,128,1024]{2,1,0:T(8,128)(2,1)S(1)}, bf16[1,128,1024]{2,1,0:T(8,128)(2,1)S(1)}, u32[]{:S(2)}, u32[]{:S(2)}) collective-permute-start(bf16[1,128,1024]{2,1,0:T(8,128)(2,1)S(1)} %shard_map.98), channel_id=1, source_target_pairs={{0,224},{32,0},{64,32},{96,64},{128,96},{160,128},{192,160},{224,1... | collective-permute-start | bytes 786440 | tf_op jit(solution)/shard_map/ppermute | solution.py:111
  56.2 15.6 %collective-permute-start.17 = (bf16[1,128,1024]{2,1,0:T(8,128)(2,1)S(1)}, bf16[1,128,1024]{2,1,0:T(8,128)(2,1)S(1)}, u32[]{:S(2)}, u32[]{:S(2)}) collective-permute-start(bf16[1,128,1024]{2,1,0:T(8,128)(2,1)S(1)} %shard_map.106), channel_id=1, source_target_pairs={{0,32},{32,64},{64,96},{96,128},{128,160},{160,192},{192,224},{224... | collective-permute-start | bytes 786440 | tf_op jit(solution)/shard_map/ppermute | solution.py:111
  60.6 11.2 %collective-permute-start.13 = (bf16[1,128,1024]{2,1,0:T(8,128)(2,1)S(1)}, bf16[1,128,1024]{2,1,0:T(8,128)(2,1)S(1)}, u32[]{:S(2)}, u32[]{:S(2)}) collective-permute-start(bf16[1,128,1024]{2,1,0:T(8,128)(2,1)S(1)} %shard_map.103), channel_id=1, source_target_pairs={{0,224},{32,0},{64,32},{96,64},{128,96},{160,128},{192,160},{224,1... | collective-permute-start | bytes 786440 | tf_op jit(solution)/shard_map/ppermute | solution.py:111
  71.8 85.9 %copy-start = (bf16[2,128,1024]{2,1,0:T(8,128)(2,1)S(1)}, bf16[2,128,1024]{2,1,0:T(8,128)(2,1)}, u32[]{:S(2)}) copy-start(bf16[2,128,1024]{2,1,0:T(8,128)(2,1)} %root_ref.9) | copy-start | bytes 1572868
  72.7 7.9 %collective-permute-start.3 = (bf16[1,128,1024]{2,1,0:T(8,128)(2,1)S(1)}, bf16[1,128,1024]{2,1,0:T(8,128)(2,1)S(1)}, u32[]{:S(2)}, u32[]{:S(2)}) collective-permute-start(bf16[1,128,1024]{2,1,0:T(8,128)(2,1)S(1)} %shard_map.96.refs_0_), channel_id=1, source_target_pairs={{0,32},{32,64},{64,96},{96,128},{128,160},{160,192},{192,224},{224... | collective-permute-start | bytes 786440 | tf_op jit(solution)/shard_map/ppermute | solution.py:111
  120.1 13.4 %collective-permute-start.24 = (bf16[128,1024]{1,0:T(8,128)(2,1)S(1)}, bf16[128,1024]{1,0:T(8,128)(2,1)S(1)}, u32[]{:S(2)}, u32[]{:S(2)}) collective-permute-start(bf16[128,1024]{1,0:T(8,128)(2,1)S(1)} %get-tuple-element.37.rest_0_.rest_2_.rest_4_), channel_id=1, source_target_pairs={{0,32},{32,64},{64,96},{96,128},{128,160},{160,192},{192,224},{224... | collective-permute-start | bytes 786440 | tf_op jit(solution)/shard_map/ppermute | solution.py:111
  120.2 13.3 %collective-permute-start.21 = (bf16[128,1024]{1,0:T(8,128)(2,1)S(1)}, bf16[128,1024]{1,0:T(8,128)(2,1)S(1)}, u32[]{:S(2)}, u32[]{:S(2)}) collective-permute-start(bf16[128,1024]{1,0:T(8,128)(2,1)S(1)} %get-tuple-element.36.rest_1_.rest_3_.rest_5_), channel_id=1, source_target_pairs={{0,224},{32,0},{64,32},{96,64},{128,96},{160,128},{192,160},{224,1... | collective-permute-start | bytes 786440 | tf_op jit(solution)/shard_map/ppermute | solution.py:111
  122.8 14.5 %collective-permute-start.29 = (bf16[128,1024]{1,0:T(8,128)(2,1)S(1)}, bf16[128,1024]{1,0:T(8,128)(2,1)S(1)}, u32[]{:S(2)}, u32[]{:S(2)}) collective-permute-start(bf16[128,1024]{1,0:T(8,128)(2,1)S(1)} %get-tuple-element.37.rest_0_.rest_2_.rest_4_), channel_id=1, source_target_pairs={{0,224},{32,0},{64,32},{96,64},{128,96},{160,128},{192,160},{224,1... | collective-permute-start | bytes 786440 | tf_op jit(solution)/shard_map/ppermute | solution.py:111
  122.9 16.3 %collective-permute-start.32 = (bf16[128,1024]{1,0:T(8,128)(2,1)S(1)}, bf16[128,1024]{1,0:T(8,128)(2,1)S(1)}, u32[]{:S(2)}, u32[]{:S(2)}) collective-permute-start(bf16[128,1024]{1,0:T(8,128)(2,1)S(1)} %get-tuple-element.36.rest_1_.rest_3_.rest_5_), channel_id=1, source_target_pairs={{0,32},{32,64},{64,96},{96,128},{128,160},{160,192},{192,224},{224... | collective-permute-start | bytes 786440 | tf_op jit(solution)/shard_map/ppermute | solution.py:111
  133.5 11.2 %collective-permute-start.25 = (bf16[128,1024]{1,0:T(8,128)(2,1)S(1)}, bf16[128,1024]{1,0:T(8,128)(2,1)S(1)}, u32[]{:S(2)}, u32[]{:S(2)}) collective-permute-start(bf16[128,1024]{1,0:T(8,128)(2,1)S(1)} %collective-permute-done.24.rest_0_), channel_id=1, source_target_pairs={{0,32},{32,64},{64,96},{96,128},{128,160},{160,192},{192,224},{224... | collective-permute-start | bytes 786440 | tf_op jit(solution)/shard_map/ppermute | solution.py:111
  133.5 11.2 %collective-permute-start.22 = (bf16[128,1024]{1,0:T(8,128)(2,1)S(1)}, bf16[128,1024]{1,0:T(8,128)(2,1)S(1)}, u32[]{:S(2)}, u32[]{:S(2)}) collective-permute-start(bf16[128,1024]{1,0:T(8,128)(2,1)S(1)} %collective-permute-done.21.rest_1_), channel_id=1, source_target_pairs={{0,224},{32,0},{64,32},{96,64},{128,96},{160,128},{192,160},{224,1... | collective-permute-start | bytes 786440 | tf_op jit(solution)/shard_map/ppermute | solution.py:111
  137.4 25.7 %copy-start.4 = (bf16[128,1024]{1,0:T(8,128)(2,1)}, bf16[128,1024]{1,0:T(8,128)(2,1)S(1)}, u32[]{:S(2)}) copy-start(bf16[128,1024]{1,0:T(8,128)(2,1)S(1)} %collective-permute-done.29.rest_2_) | copy-start | bytes 786436
  137.4 11.3 %collective-permute-start.30 = (bf16[128,1024]{1,0:T(8,128)(2,1)S(1)}, bf16[128,1024]{1,0:T(8,128)(2,1)}, u32[]{:S(2)}, u32[]{:S(2)}) collective-permute-start(bf16[128,1024]{1,0:T(8,128)(2,1)S(1)} %collective-permute-done.29.rest_2_), channel_id=1, source_target_pairs={{0,224},{32,0},{64,32},{96,64},{128,96},{160,128},{192,160},{224,1... | collective-permute-start | bytes 786440 | tf_op jit(solution)/shard_map/ppermute | solution.py:111
  139.2 23.9 %copy-start.6 = (bf16[128,1024]{1,0:T(8,128)(2,1)}, bf16[128,1024]{1,0:T(8,128)(2,1)S(1)}, u32[]{:S(2)}) copy-start(bf16[128,1024]{1,0:T(8,128)(2,1)S(1)} %collective-permute-done.32.rest_3_) | copy-start | bytes 786436
  139.2 11.3 %collective-permute-start.33 = (bf16[128,1024]{1,0:T(8,128)(2,1)S(1)}, bf16[128,1024]{1,0:T(8,128)(2,1)}, u32[]{:S(2)}, u32[]{:S(2)}) collective-permute-start(bf16[128,1024]{1,0:T(8,128)(2,1)S(1)} %collective-permute-done.32.rest_3_), channel_id=1, source_target_pairs={{0,32},{32,64},{64,96},{96,128},{128,160},{160,192},{192,224},{224... | collective-permute-start | bytes 786440 | tf_op jit(solution)/shard_map/ppermute | solution.py:111
  144.7 11.3 %collective-permute-start.26 = (bf16[128,1024]{1,0:T(8,128)(2,1)S(1)}, bf16[128,1024]{1,0:T(8,128)(2,1)}, u32[]{:S(2)}, u32[]{:S(2)}) collective-permute-start(bf16[128,1024]{1,0:T(8,128)(2,1)S(1)} %collective-permute-done.25.rest_0_), channel_id=1, source_target_pairs={{0,32},{32,64},{64,96},{96,128},{128,160},{160,192},{192,224},{224... | collective-permute-start | bytes 786440 | tf_op jit(solution)/shard_map/ppermute | solution.py:111
  144.7 11.3 %collective-permute-start.23 = (bf16[128,1024]{1,0:T(8,128)(2,1)S(1)}, bf16[128,1024]{1,0:T(8,128)(2,1)}, u32[]{:S(2)}, u32[]{:S(2)}) collective-permute-start(bf16[128,1024]{1,0:T(8,128)(2,1)S(1)} %collective-permute-done.22.rest_1_), channel_id=1, source_target_pairs={{0,224},{32,0},{64,32},{96,64},{128,96},{160,128},{192,160},{224,1... | collective-permute-start | bytes 786440 | tf_op jit(solution)/shard_map/ppermute | solution.py:111
  148.7 11.4 %collective-permute-start.31 = (bf16[128,1024]{1,0:T(8,128)(2,1)}, bf16[128,1024]{1,0:T(8,128)(2,1)}, u32[]{:S(2)}, u32[]{:S(2)}) collective-permute-start(bf16[128,1024]{1,0:T(8,128)(2,1)} %collective-permute-done.30.rest_2_), channel_id=1, source_target_pairs={{0,224},{32,0},{64,32},{96,64},{128,96},{160,128},{192,160},{224,1... | collective-permute-start | bytes 786440 | tf_op jit(solution)/shard_map/ppermute | solution.py:111
  150.4 11.0 %collective-permute-start.34 = (bf16[128,1024]{1,0:T(8,128)(2,1)}, bf16[128,1024]{1,0:T(8,128)(2,1)}, u32[]{:S(2)}, u32[]{:S(2)}) collective-permute-start(bf16[128,1024]{1,0:T(8,128)(2,1)} %collective-permute-done.33.rest_3_), channel_id=1, source_target_pairs={{0,32},{32,64},{64,96},{96,128},{128,160},{160,192},{192,224},{224... | collective-permute-start | bytes 786440 | tf_op jit(solution)/shard_map/ppermute | solution.py:111
  156.1 9.3 %collective-permute-start.28 = (bf16[128,1024]{1,0:T(8,128)(2,1)}, bf16[128,1024]{1,0:T(8,128)(2,1)S(1)}, u32[]{:S(2)}, u32[]{:S(2)}) collective-permute-start(bf16[128,1024]{1,0:T(8,128)(2,1)} %collective-permute-done.23.rest_1_), channel_id=1, source_target_pairs={{0,224},{32,0},{64,32},{96,64},{128,96},{160,128},{192,160},{224,1... | collective-permute-start | bytes 786440 | tf_op jit(solution)/shard_map/ppermute | solution.py:111
  157.2 8.2 %collective-permute-start.27 = (bf16[128,1024]{1,0:T(8,128)(2,1)}, bf16[128,1024]{1,0:T(8,128)(2,1)S(1)}, u32[]{:S(2)}, u32[]{:S(2)}) collective-permute-start(bf16[128,1024]{1,0:T(8,128)(2,1)} %collective-permute-done.26.rest_0_), channel_id=1, source_target_pairs={{0,32},{32,64},{64,96},{96,128},{128,160},{160,192},{192,224},{224... | collective-permute-start | bytes 786440 | tf_op jit(solution)/shard_map/ppermute | solution.py:111
  160.1 33.0 %copy-start.2 = (f32[2,128,1024]{2,1,0:T(8,128)S(1)}, f32[2,128,1024]{2,1,0:T(8,128)}, u32[]{:S(2)}) copy-start(f32[2,128,1024]{2,1,0:T(8,128)} %rest_4_.1) | copy-start | bytes 3145732
  166.4 22.6 %copy-start.13 = (bf16[128,1024]{1,0:T(8,128)(2,1)}, bf16[128,1024]{1,0:T(8,128)(2,1)S(1)}, u32[]{:S(2)}) copy-start(bf16[128,1024]{1,0:T(8,128)(2,1)S(1)} %get-tuple-element.43.rest_0_) | copy-start | bytes 786436
  166.5 22.6 %copy-start.15 = (bf16[128,1024]{1,0:T(8,128)(2,1)}, bf16[128,1024]{1,0:T(8,128)(2,1)S(1)}, u32[]{:S(2)}) copy-start(bf16[128,1024]{1,0:T(8,128)(2,1)S(1)} %get-tuple-element.44.rest_1_) | copy-start | bytes 786436
  166.5 28.4 %copy-start.5 = (bf16[128,1024]{1,0:T(8,128)(2,1)S(1)}, bf16[128,1024]{1,0:T(8,128)(2,1)}, u32[]{:S(2)}) copy-start(bf16[128,1024]{1,0:T(8,128)(2,1)} %copy-done.4) | copy-start | bytes 786436
  166.5 28.4 %copy-start.7 = (bf16[128,1024]{1,0:T(8,128)(2,1)S(1)}, bf16[128,1024]{1,0:T(8,128)(2,1)}, u32[]{:S(2)}) copy-start(bf16[128,1024]{1,0:T(8,128)(2,1)} %copy-done.6) | copy-start | bytes 786436
  189.1 18.4 %all-to-all-start.3 = ((bf16[32,3,16,256]{3,2,1,0:T(8,128)(2,1)}), bf16[32,3,16,256]{3,2,1,0:T(8,128)(2,1)S(1)}, u32[]{:S(2)}, u32[]{:S(2)}) async-start(bf16[32,3,16,256]{3,2,1,0:T(8,128)(2,1)} %bitcast.26), calls=%async_computation.3 | async-start | bytes 1572864 | tf_op jit(solution)/shard_map/all_to_all | solution.py:241
  (8 other events, 52.6 us)
Sparse Core Ops, SparseCore 0:
  72.8 59.3 all-gather.1

commit v5 on v4

--- a/solution.py
+++ b/solution.py
@@ -150,7 +150,7 @@
             )
         sent[stream, way] = value
         held[stream, way] = hop(value, way, ring)
-    earlier = [held[key] if key != (0, 1) else sent[key] for key in held]
+    earlier = [held[key] if key not in ((0, 1), (1, -1)) else sent[key] for key in held]
     after = jax.ShapeDtypeStruct(root.shape, root.dtype)
     earlier += tables
     root = call(after_kernel, after, [HBM] * len(earlier) + [VMEM], (*earlier, root))
@@ -231,7 +231,8 @@
                     shard[...],
                     preferred_element_type=F32,
                 )
-        result = jnp.dot(total.astype(BF16), right_ref[a], preferred_element_type=F32)
+        factor = right_ref[:, a].reshape(ring * rows, right_ref.shape[3])
+        result = jnp.dot(total.astype(BF16), factor, preferred_element_type=F32)
         put_pieces(out_ref, a, result.astype(BF16))
     for copy in copies:
         copy.wait()
@@ -253,7 +254,7 @@
     summed, right_root = sum_over_ring(
         partials[0], rows, owners, right_root, [chosen, wanted]
     )
-    right_full = lax.all_gather(right_root, "dp", axis=1, tiled=True)
+    right_full = lax.all_gather(right_root, "dp", axis=0)
 
     spread = swap(summed)
     piece = spread.shape[2:]

time: 216 us -> 215 us (level)
  waiting for transfers between devices: 76.8 us -> 73.6 us
  starting transfers between devices: 40.1 us -> 42.3 us
    ppermute x35, waiting for transfers between devices: 70.5 us -> 67.4 us  [hop(): lax.ppermute(value, 'dp', [(i, (i + step) % ring) for i in range(ring)])]
    ppermute x35, starting transfers between devices: 36 us -> 38.3 us  [hop(): lax.ppermute(value, 'dp', [(i, (i + step) % ring) for i in range(ring)])]
  transfers between devices with their start and end apart: 37 -> 37, of which waited for: 20 -> 22; matrix products, arithmetic and copies ran while one was open for 2% -> 2% of each run, Pallas kernels for 6% -> 6%
where the time goes in v5:
time: 215 us
  waiting for transfers between devices  73.6 us (34%)
  blocking collectives  59.9 us (28%)
  starting transfers between devices  42.3 us (20%)
  Pallas kernels  17.3 us (8%)
  between operations  14.6 us (7%)
  local copies, waits for them, and re-layouts  6.81 us (3%)
    ppermute x35, waiting for transfers between devices, hop(): lax.ppermute(value, 'dp', [(i, (i + step) % ring) for i in range(ring)])  67.4 us
    all_to_all x3, blocking collectives, swap(): lax.all_to_all(pieces, 'own', split_axis=0, concat_axis=0, tiled=True)  59.9 us
    ppermute x35, starting transfers between devices, hop(): lax.ppermute(value, 'dp', [(i, (i + step) % ring) for i in range(ring)])  38.3 us
    pallas_call x31, Pallas kernels, call(): pl.pallas_call(kernel, out_shape=out_shape, in_specs=in_specs, out_specs=...  17.3 us
    all_to_all x1, waiting for transfers between devices, swap(): lax.all_to_all(pieces, 'own', split_axis=0, concat_axis=0, tiled=True)  6.25 us
  transfers between devices with their start and end apart: 37, of which 22 were waited for; matrix products, arithmetic and copies ran while one was open for 2% of the time, Pallas kernels for 6%

profile of v5, /device:TPU:1, one launch (start us, length us, event | category | flops | bytes accessed | tf_op | source)
XLA Modules:
  0.0 214.9 jit_solution(7730128558152508410)
XLA Ops:
  7.2 1.5 dynamic-slice_bitcast_fusion.16
  8.7 2.5 %collective-permute-start.14 = (bf16[1,128,1024]{2,1,0:T(8,128)(2,1)S(1)}, bf16[1,128,1024]{2,1,0:T(8,128)(2,1)S(1)}, u32[]{:S(2)}, u32[]{:S(2)}) collective-permute-start(bf16[1,128,1024]{2,1,0:T(8,128)(2,1)S(1)} %get-tuple-element.34), channel_id=1, source_target_pairs={{0,32},{32,64},{64,96},{96,128},{128,160},{160,192},{192,224},{224... | collective-permute-start | bytes 786440 | tf_op jit(solution)/shard_map/ppermute | solution.py:111
  11.3 4.0 %collective-permute-start.10 = (bf16[1,128,1024]{2,1,0:T(8,128)(2,1)S(1)}, bf16[1,128,1024]{2,1,0:T(8,128)(2,1)S(1)}, u32[]{:S(2)}, u32[]{:S(2)}) collective-permute-start(bf16[1,128,1024]{2,1,0:T(8,128)(2,1)S(1)} %get-tuple-element.33), channel_id=1, source_target_pairs={{0,224},{32,0},{64,32},{96,64},{128,96},{160,128},{192,160},{224,1... | collective-permute-start | bytes 786440 | tf_op jit(solution)/shard_map/ppermute | solution.py:111
  15.3 1.4 collective-permute-start.18
  16.8 2.6 %collective-permute-start.4 = (bf16[1,128,1024]{2,1,0:T(8,128)(2,1)S(1)}, bf16[1,128,1024]{2,1,0:T(8,128)(2,1)S(1)}, u32[]{:S(2)}, u32[]{:S(2)}) collective-permute-start(bf16[1,128,1024]{2,1,0:T(8,128)(2,1)S(1)} %get-tuple-element.31), channel_id=1, source_target_pairs={{0,224},{32,0},{64,32},{96,64},{128,96},{160,128},{192,160},{224,1... | collective-permute-start | bytes 786440 | tf_op jit(solution)/shard_map/ppermute | solution.py:111
  19.3 2.7 %dynamic-slice_bitcast_fusion.1 = (bf16[1,128,1024]{2,1,0:T(8,128)(2,1)S(1)}, bf16[1,128,1024]{2,1,0:T(8,128)(2,1)S(1)}, bf16[1,128,1024]{2,1,0:T(8,128)(2,1)S(1...) fusion(bf16[1,3,1024,1024]{3,2,1,0:T(8,128)(2,1)} %param.7, ...), kind=kLoop, calls=%fused_computation.1 | loop fusion | bytes 7864344 | tf_op jit(solution)/shard_map/dynamic_slice | solution.py:134
  22.5 3.4 %collective-permute-done.18.got_ref = bf16[1,128,1024]{2,1,0:T(8,128)(2,1)S(1)} collective-permute-done((bf16[1,128,1024]{2,1,0:T(8,128)(2,1)S(1)}, bf16[1,128,1024]{2,1,0:T(8,128)(2,1)S(1)}, u32[]{:S(2)}, u32[]{:S(2)}) %collective-permute-start.18) | collective-permute-done | bytes 262176 | tf_op jit(solution)/shard_map/ppermute | solution.py:111
  25.9 3.4 %collective-permute-start.11 = (bf16[1,128,1024]{2,1,0:T(8,128)(2,1)S(1)}, bf16[1,128,1024]{2,1,0:T(8,128)(2,1)S(1)}, u32[]{:S(2)}, u32[]{:S(2)}) collective-permute-start(bf16[1,128,1024]{2,1,0:T(8,128)(2,1)S(1)} %shard_map.101), channel_id=1, source_target_pairs={{0,224},{32,0},{64,32},{96,64},{128,96},{160,128},{192,160},{224,1... | collective-permute-start | bytes 786440 | tf_op jit(solution)/shard_map/ppermute | solution.py:111
  29.5 2.0 collective-permute-done.4.got_ref
  32.3 2.8 %collective-permute-start.5 = (bf16[1,128,1024]{2,1,0:T(8,128)(2,1)S(1)}, bf16[1,128,1024]{2,1,0:T(8,128)(2,1)S(1)}, u32[]{:S(2)}, u32[]{:S(2)}) collective-permute-start(bf16[1,128,1024]{2,1,0:T(8,128)(2,1)S(1)} %shard_map.97), channel_id=1, source_target_pairs={{0,224},{32,0},{64,32},{96,64},{128,96},{160,128},{192,160},{224,1... | collective-permute-start | bytes 786440 | tf_op jit(solution)/shard_map/ppermute | solution.py:111
  35.1 2.8 %collective-permute-done.15.got_ref = bf16[1,128,1024]{2,1,0:T(8,128)(2,1)S(1)} collective-permute-done((bf16[1,128,1024]{2,1,0:T(8,128)(2,1)S(1)}, bf16[1,128,1024]{2,1,0:T(8,128)(2,1)S(1)}, u32[]{:S(2)}, u32[]{:S(2)}) %collective-permute-start.15) | collective-permute-done | bytes 262176 | tf_op jit(solution)/shard_map/ppermute | solution.py:111
  38.1 4.6 %collective-permute-done.19.got_ref = bf16[1,128,1024]{2,1,0:T(8,128)(2,1)S(1)} collective-permute-done((bf16[1,128,1024]{2,1,0:T(8,128)(2,1)S(1)}, bf16[1,128,1024]{2,1,0:T(8,128)(2,1)S(1)}, u32[]{:S(2)}, u32[]{:S(2)}) %collective-permute-start.19) | collective-permute-done | bytes 262176 | tf_op jit(solution)/shard_map/ppermute | solution.py:111
  42.7 3.4 %collective-permute-start.12 = (bf16[1,128,1024]{2,1,0:T(8,128)(2,1)S(1)}, bf16[1,128,1024]{2,1,0:T(8,128)(2,1)S(1)}, u32[]{:S(2)}, u32[]{:S(2)}) collective-permute-start(bf16[1,128,1024]{2,1,0:T(8,128)(2,1)S(1)} %shard_map.102), channel_id=1, source_target_pairs={{0,224},{32,0},{64,32},{96,64},{128,96},{160,128},{192,160},{224,1... | collective-permute-start | bytes 786440 | tf_op jit(solution)/shard_map/ppermute | solution.py:111
  46.6 1.8 collective-permute-done.5.got_ref
  49.1 2.8 %collective-permute-start.6 = (bf16[1,128,1024]{2,1,0:T(8,128)(2,1)S(1)}, bf16[1,128,1024]{2,1,0:T(8,128)(2,1)S(1)}, u32[]{:S(2)}, u32[]{:S(2)}) collective-permute-start(bf16[1,128,1024]{2,1,0:T(8,128)(2,1)S(1)} %shard_map.98), channel_id=1, source_target_pairs={{0,224},{32,0},{64,32},{96,64},{128,96},{160,128},{192,160},{224,1... | collective-permute-start | bytes 786440 | tf_op jit(solution)/shard_map/ppermute | solution.py:111
  52.0 2.8 %collective-permute-done.16.got_ref = bf16[1,128,1024]{2,1,0:T(8,128)(2,1)S(1)} collective-permute-done((bf16[1,128,1024]{2,1,0:T(8,128)(2,1)S(1)}, bf16[1,128,1024]{2,1,0:T(8,128)(2,1)S(1)}, u32[]{:S(2)}, u32[]{:S(2)}) %collective-permute-start.16) | collective-permute-done | bytes 262176 | tf_op jit(solution)/shard_map/ppermute | solution.py:111
  55.1 10.9 %collective-permute-done.2.got_ref = bf16[1,128,1024]{2,1,0:T(8,128)(2,1)S(1)} collective-permute-done((bf16[1,128,1024]{2,1,0:T(8,128)(2,1)S(1)}, bf16[1,128,1024]{2,1,0:T(8,128)(2,1)S(1)}, u32[]{:S(2)}, u32[]{:S(2)}) %collective-permute-start.2) | collective-permute-done | bytes 262176 | tf_op jit(solution)/shard_map/ppermute | solution.py:111
  66.1 5.5 %collective-permute-done.17.rest_4_.refs_2_ = bf16[1,128,1024]{2,1,0:T(8,128)(2,1)S(1)} collective-permute-done((bf16[1,128,1024]{2,1,0:T(8,128)(2,1)S(1)}, bf16[1,128,1024]{2,1,0:T(8,128)(2,1)S(1)}, u32[]{:S(2)}, u32[]{:S(2)}) %collective-permute-start.17) | collective-permute-done | bytes 262176 | tf_op jit(solution)/shard_map/ppermute | solution.py:111
  72.5 1.4 collective-permute-start.13
  74.0 1.2 dynamic-slice_bitcast_fusion.own_ref
  75.2 3.7 %collective-permute-done.13.rest_3_ = bf16[1,128,1024]{2,1,0:T(8,128)(2,1)S(1)} collective-permute-done((bf16[1,128,1024]{2,1,0:T(8,128)(2,1)S(1)}, bf16[1,128,1024]{2,1,0:T(8,128)(2,1)S(1)}, u32[]{:S(2)}, u32[]{:S(2)}) %collective-permute-start.13) | collective-permute-done | bytes 262176 | tf_op jit(solution)/shard_map/ppermute | solution.py:111
  78.9 2.1 collective-permute-done.3.rest_0_
  81.4 23.9 %all_to_all.20 = bf16[32,3,16,256]{3,2,1,0:T(8,128)(2,1)S(1)} all-to-all(bf16[32,3,16,256]{3,2,1,0:T(8,128)(2,1)S(1)} %shard_map.109), channel_id=1, replica_groups=mesh['dp'=8,'own'=32] {'own'}, dimensions={0} | all-to-all | bytes 1572864 | tf_op jit(solution)/shard_map/all_to_all | solution.py:242
  106.0 15.2 %all_to_all.21.pieces_ref = bf16[32,2,16,256]{3,2,1,0:T(8,128)(2,1)S(1)} all-to-all(bf16[32,2,16,256]{3,2,1,0:T(8,128)(2,1)S(1)} %bitcast.52), channel_id=1, replica_groups=mesh['dp'=8,'own'=32] {'own'}, dimensions={0} | all-to-all | bytes 1048576 | tf_op jit(solution)/shard_map/all_to_all | solution.py:242
  121.3 2.7 %collective-permute-start.21 = (bf16[128,1024]{1,0:T(8,128)(2,1)S(1)}, bf16[128,1024]{1,0:T(8,128)(2,1)S(1)}, u32[]{:S(2)}, u32[]{:S(2)}) collective-permute-start(bf16[128,1024]{1,0:T(8,128)(2,1)S(1)} %get-tuple-element.36.rest_1_.rest_3_.rest_5_), channel_id=1, source_target_pairs={{0,224},{32,0},{64,32},{96,64},{128,96},{160,128},{192,160},{224,1... | collective-permute-start | bytes 786440 | tf_op jit(solution)/shard_map/ppermute | solution.py:111
  124.0 1.4 collective-permute-start.32
  125.4 7.8 %collective-permute-done.24.rest_0_ = bf16[128,1024]{1,0:T(8,128)(2,1)S(1)} collective-permute-done((bf16[128,1024]{1,0:T(8,128)(2,1)S(1)}, bf16[128,1024]{1,0:T(8,128)(2,1)S(1)}, u32[]{:S(2)}, u32[]{:S(2)}) %collective-permute-start.24) | collective-permute-done | bytes 262176 | tf_op jit(solution)/shard_map/ppermute | solution.py:111
  133.2 2.7 %collective-permute-start.22 = (bf16[128,1024]{1,0:T(8,128)(2,1)S(1)}, bf16[128,1024]{1,0:T(8,128)(2,1)S(1)}, u32[]{:S(2)}, u32[]{:S(2)}) collective-permute-start(bf16[128,1024]{1,0:T(8,128)(2,1)S(1)} %collective-permute-done.21.rest_1_), channel_id=1, source_target_pairs={{0,224},{32,0},{64,32},{96,64},{128,96},{160,128},{192,160},{224,1... | collective-permute-start | bytes 786440 | tf_op jit(solution)/shard_map/ppermute | solution.py:111
  135.9 1.2 collective-permute-done.29.rest_2_
  137.1 1.2 collective-permute-start.30
  138.8 5.6 %collective-permute-done.25.rest_0_ = bf16[128,1024]{1,0:T(8,128)(2,1)S(1)} collective-permute-done((bf16[128,1024]{1,0:T(8,128)(2,1)S(1)}, bf16[128,1024]{1,0:T(8,128)(2,1)S(1)}, u32[]{:S(2)}, u32[]{:S(2)}) %collective-permute-start.25) | collective-permute-done | bytes 262176 | tf_op jit(solution)/shard_map/ppermute | solution.py:111
  144.5 2.7 %collective-permute-start.23 = (bf16[128,1024]{1,0:T(8,128)(2,1)S(1)}, bf16[128,1024]{1,0:T(8,128)(2,1)}, u32[]{:S(2)}, u32[]{:S(2)}) collective-permute-start(bf16[128,1024]{1,0:T(8,128)(2,1)S(1)} %collective-permute-done.22.rest_1_), channel_id=1, source_target_pairs={{0,224},{32,0},{64,32},{96,64},{128,96},{160,128},{192,160},{224,1... | collective-permute-start | bytes 786440 | tf_op jit(solution)/shard_map/ppermute | solution.py:111
  147.1 1.3 collective-permute-done.30.rest_2_
  150.2 5.6 %collective-permute-done.26.rest_0_ = bf16[128,1024]{1,0:T(8,128)(2,1)} collective-permute-done((bf16[128,1024]{1,0:T(8,128)(2,1)S(1)}, bf16[128,1024]{1,0:T(8,128)(2,1)}, u32[]{:S(2)}, u32[]{:S(2)}) %collective-permute-start.26) | collective-permute-done | bytes 262176 | tf_op jit(solution)/shard_map/ppermute | solution.py:111
  155.8 1.1 collective-permute-start.28
  158.1 1.7 shard_map.115.rest_4_
  159.8 1.4 collective-permute-done.34.rest_3_
  161.2 1.6 shard_map.116.rest_2_
  162.8 2.2 %collective-permute-done.28.rest_1_ = bf16[128,1024]{1,0:T(8,128)(2,1)S(1)} collective-permute-done((bf16[128,1024]{1,0:T(8,128)(2,1)}, bf16[128,1024]{1,0:T(8,128)(2,1)S(1)}, u32[]{:S(2)}, u32[]{:S(2)}) %collective-permute-start.28) | collective-permute-done | bytes 262176 | tf_op jit(solution)/shard_map/ppermute | solution.py:111
  165.1 1.1 shard_map.117
  166.2 20.9 %all_to_all.22 = bf16[32,2,16,256]{3,2,1,0:T(8,128)(2,1)S(1)} all-to-all(bf16[32,2,16,256]{3,2,1,0:T(8,128)(2,1)S(1)} %get-tuple-element.42), channel_id=1, replica_groups=mesh['dp'=8,'own'=32] {'own'}, dimensions={0} | all-to-all | bytes 1048576 | tf_op jit(solution)/shard_map/all_to_all | solution.py:242
  187.1 1.7 shard_map.118
  188.8 4.0 %all-to-all-start.3 = ((bf16[32,3,16,256]{3,2,1,0:T(8,128)(2,1)}), bf16[32,3,16,256]{3,2,1,0:T(8,128)(2,1)S(1)}, u32[]{:S(2)}, u32[]{:S(2)}) async-start(bf16[32,3,16,256]{3,2,1,0:T(8,128)(2,1)} %bitcast.27), calls=%async_computation.3 | async-start | bytes 1572864 | tf_op jit(solution)/shard_map/all_to_all | solution.py:242
  192.8 1.2 copy-done.3
  195.3 1.8 shard_map.122
  197.2 2.0 shard_map.123
  199.2 1.7 shard_map.124
  200.9 6.2 %all-to-all-done.3.pieces_ref = bf16[32,3,16,256]{3,2,1,0:T(8,128)(2,1)S(1)} async-done(((bf16[32,3,16,256]{3,2,1,0:T(8,128)(2,1)}), bf16[32,3,16,256]{3,2,1,0:T(8,128)(2,1)S(1)}, u32[]{:S(2)}, u32[]{:S(2)}) %all-to-all-start.3) | async-done | bytes 786464 | tf_op jit(solution)/shard_map/all_to_all | solution.py:242
  (107 shorter events, 11.2 us)
Async XLA Ops:
  7.2 148.6 %all-gather.3.cloned.1.call-start = ((), (), s32[]{:S(2)}) async-start(), calls=%async_computation.4 | async-start | bytes 4718592 | tf_op jit(solution)/shard_map/all_gather | solution.py:257
  8.7 13.4 %collective-permute-start.14 = (bf16[1,128,1024]{2,1,0:T(8,128)(2,1)S(1)}, bf16[1,128,1024]{2,1,0:T(8,128)(2,1)S(1)}, u32[]{:S(2)}, u32[]{:S(2)}) collective-permute-start(bf16[1,128,1024]{2,1,0:T(8,128)(2,1)S(1)} %get-tuple-element.34), channel_id=1, source_target_pairs={{0,32},{32,64},{64,96},{96,128},{128,160},{160,192},{192,224},{224... | collective-permute-start | bytes 786440 | tf_op jit(solution)/shard_map/ppermute | solution.py:111
  11.3 11.0 %collective-permute-start.10 = (bf16[1,128,1024]{2,1,0:T(8,128)(2,1)S(1)}, bf16[1,128,1024]{2,1,0:T(8,128)(2,1)S(1)}, u32[]{:S(2)}, u32[]{:S(2)}) collective-permute-start(bf16[1,128,1024]{2,1,0:T(8,128)(2,1)S(1)} %get-tuple-element.33), channel_id=1, source_target_pairs={{0,224},{32,0},{64,32},{96,64},{128,96},{160,128},{192,160},{224,1... | collective-permute-start | bytes 786440 | tf_op jit(solution)/shard_map/ppermute | solution.py:111
  15.3 10.6 %collective-permute-start.18 = (bf16[1,128,1024]{2,1,0:T(8,128)(2,1)S(1)}, bf16[1,128,1024]{2,1,0:T(8,128)(2,1)S(1)}, u32[]{:S(2)}, u32[]{:S(2)}) collective-permute-start(bf16[1,128,1024]{2,1,0:T(8,128)(2,1)S(1)} %get-tuple-element.35), channel_id=1, source_target_pairs={{0,224},{32,0},{64,32},{96,64},{128,96},{160,128},{192,160},{224,1... | collective-permute-start | bytes 786440 | tf_op jit(solution)/shard_map/ppermute | solution.py:111
  16.7 12.7 %collective-permute-start.7 = (bf16[1,128,1024]{2,1,0:T(8,128)(2,1)S(1)}, bf16[1,128,1024]{2,1,0:T(8,128)(2,1)S(1)}, u32[]{:S(2)}, u32[]{:S(2)}) collective-permute-start(bf16[1,128,1024]{2,1,0:T(8,128)(2,1)S(1)} %get-tuple-element.32), channel_id=1, source_target_pairs={{0,32},{32,64},{64,96},{96,128},{128,160},{160,192},{192,224},{224... | collective-permute-start | bytes 786440 | tf_op jit(solution)/shard_map/ppermute | solution.py:111
  16.8 14.7 %collective-permute-start.4 = (bf16[1,128,1024]{2,1,0:T(8,128)(2,1)S(1)}, bf16[1,128,1024]{2,1,0:T(8,128)(2,1)S(1)}, u32[]{:S(2)}, u32[]{:S(2)}) collective-permute-start(bf16[1,128,1024]{2,1,0:T(8,128)(2,1)S(1)} %get-tuple-element.31), channel_id=1, source_target_pairs={{0,224},{32,0},{64,32},{96,64},{128,96},{160,128},{192,160},{224,1... | collective-permute-start | bytes 786440 | tf_op jit(solution)/shard_map/ppermute | solution.py:111
  19.3 26.8 %copy-start.18 = (s32[96]{0:T(128)S(1)}, s32[96]{0:T(128)}, u32[]{:S(2)}) copy-start(s32[96]{0:T(128)} %param.8) | copy-start | bytes 1156
  19.3 26.8 %copy-start.17 = (s32[96]{0:T(128)S(1)}, s32[96]{0:T(128)}, u32[]{:S(2)}) copy-start(s32[96]{0:T(128)} %param.9) | copy-start | bytes 1156
  22.1 49.5 %copy-start.12 = (bf16[2,128,1024]{2,1,0:T(8,128)(2,1)S(1)}, bf16[2,128,1024]{2,1,0:T(8,128)(2,1)}, u32[]{:S(2)}) copy-start(bf16[2,128,1024]{2,1,0:T(8,128)(2,1)} %refs_8_.1) | copy-start | bytes 1572868
  22.1 10.2 %collective-permute-start = (bf16[1,128,1024]{2,1,0:T(8,128)(2,1)S(1)}, bf16[1,128,1024]{2,1,0:T(8,128)(2,1)S(1)}, u32[]{:S(2)}, u32[]{:S(2)}) collective-permute-start(bf16[1,128,1024]{2,1,0:T(8,128)(2,1)S(1)} %get-tuple-element.30), channel_id=1, source_target_pairs={{0,32},{32,64},{64,96},{96,128},{128,160},{160,192},{192,224},{224... | collective-permute-start | bytes 786440 | tf_op jit(solution)/shard_map/ppermute | solution.py:111
  22.3 15.6 %collective-permute-start.15 = (bf16[1,128,1024]{2,1,0:T(8,128)(2,1)S(1)}, bf16[1,128,1024]{2,1,0:T(8,128)(2,1)S(1)}, u32[]{:S(2)}, u32[]{:S(2)}) collective-permute-start(bf16[1,128,1024]{2,1,0:T(8,128)(2,1)S(1)} %shard_map.104), channel_id=1, source_target_pairs={{0,32},{32,64},{64,96},{96,128},{128,160},{160,192},{192,224},{224... | collective-permute-start | bytes 786440 | tf_op jit(solution)/shard_map/ppermute | solution.py:111
  25.9 12.1 %collective-permute-start.11 = (bf16[1,128,1024]{2,1,0:T(8,128)(2,1)S(1)}, bf16[1,128,1024]{2,1,0:T(8,128)(2,1)S(1)}, u32[]{:S(2)}, u32[]{:S(2)}) collective-permute-start(bf16[1,128,1024]{2,1,0:T(8,128)(2,1)S(1)} %shard_map.101), channel_id=1, source_target_pairs={{0,224},{32,0},{64,32},{96,64},{128,96},{160,128},{192,160},{224,1... | collective-permute-start | bytes 786440 | tf_op jit(solution)/shard_map/ppermute | solution.py:111
  29.4 13.4 %collective-permute-start.19 = (bf16[1,128,1024]{2,1,0:T(8,128)(2,1)S(1)}, bf16[1,128,1024]{2,1,0:T(8,128)(2,1)S(1)}, u32[]{:S(2)}, u32[]{:S(2)}) collective-permute-start(bf16[1,128,1024]{2,1,0:T(8,128)(2,1)S(1)} %shard_map.107), channel_id=1, source_target_pairs={{0,224},{32,0},{64,32},{96,64},{128,96},{160,128},{192,160},{224,1... | collective-permute-start | bytes 786440 | tf_op jit(solution)/shard_map/ppermute | solution.py:111
  31.5 14.9 %collective-permute-start.8 = (bf16[1,128,1024]{2,1,0:T(8,128)(2,1)S(1)}, bf16[1,128,1024]{2,1,0:T(8,128)(2,1)S(1)}, u32[]{:S(2)}, u32[]{:S(2)}) collective-permute-start(bf16[1,128,1024]{2,1,0:T(8,128)(2,1)S(1)} %shard_map.99), channel_id=1, source_target_pairs={{0,32},{32,64},{64,96},{96,128},{128,160},{160,192},{192,224},{224... | collective-permute-start | bytes 786440 | tf_op jit(solution)/shard_map/ppermute | solution.py:111
  32.3 16.1 %collective-permute-start.5 = (bf16[1,128,1024]{2,1,0:T(8,128)(2,1)S(1)}, bf16[1,128,1024]{2,1,0:T(8,128)(2,1)S(1)}, u32[]{:S(2)}, u32[]{:S(2)}) collective-permute-start(bf16[1,128,1024]{2,1,0:T(8,128)(2,1)S(1)} %shard_map.97), channel_id=1, source_target_pairs={{0,224},{32,0},{64,32},{96,64},{128,96},{160,128},{192,160},{224,1... | collective-permute-start | bytes 786440 | tf_op jit(solution)/shard_map/ppermute | solution.py:111
  37.9 11.2 %collective-permute-start.1 = (bf16[1,128,1024]{2,1,0:T(8,128)(2,1)S(1)}, bf16[1,128,1024]{2,1,0:T(8,128)(2,1)S(1)}, u32[]{:S(2)}, u32[]{:S(2)}) collective-permute-start(bf16[1,128,1024]{2,1,0:T(8,128)(2,1)S(1)} %shard_map.94), channel_id=1, source_target_pairs={{0,32},{32,64},{64,96},{96,128},{128,160},{160,192},{192,224},{224... | collective-permute-start | bytes 786440 | tf_op jit(solution)/shard_map/ppermute | solution.py:111
  38.0 16.8 %collective-permute-start.16 = (bf16[1,128,1024]{2,1,0:T(8,128)(2,1)S(1)}, bf16[1,128,1024]{2,1,0:T(8,128)(2,1)S(1)}, u32[]{:S(2)}, u32[]{:S(2)}) collective-permute-start(bf16[1,128,1024]{2,1,0:T(8,128)(2,1)S(1)} %shard_map.105), channel_id=1, source_target_pairs={{0,32},{32,64},{64,96},{96,128},{128,160},{160,192},{192,224},{224... | collective-permute-start | bytes 786440 | tf_op jit(solution)/shard_map/ppermute | solution.py:111
  42.7 12.1 %collective-permute-start.12 = (bf16[1,128,1024]{2,1,0:T(8,128)(2,1)S(1)}, bf16[1,128,1024]{2,1,0:T(8,128)(2,1)S(1)}, u32[]{:S(2)}, u32[]{:S(2)}) collective-permute-start(bf16[1,128,1024]{2,1,0:T(8,128)(2,1)S(1)} %shard_map.102), channel_id=1, source_target_pairs={{0,224},{32,0},{64,32},{96,64},{128,96},{160,128},{192,160},{224,1... | collective-permute-start | bytes 786440 | tf_op jit(solution)/shard_map/ppermute | solution.py:111
  46.4 19.6 %collective-permute-start.20 = (bf16[1,128,1024]{2,1,0:T(8,128)(2,1)S(1)}, bf16[1,128,1024]{2,1,0:T(8,128)(2,1)S(1)}, u32[]{:S(2)}, u32[]{:S(2)}) collective-permute-start(bf16[1,128,1024]{2,1,0:T(8,128)(2,1)S(1)} %shard_map.108), channel_id=1, source_target_pairs={{0,224},{32,0},{64,32},{96,64},{128,96},{160,128},{192,160},{224,1... | collective-permute-start | bytes 786440 | tf_op jit(solution)/shard_map/ppermute | solution.py:111
  48.4 17.7 %collective-permute-start.9 = (bf16[1,128,1024]{2,1,0:T(8,128)(2,1)S(1)}, bf16[1,128,1024]{2,1,0:T(8,128)(2,1)S(1)}, u32[]{:S(2)}, u32[]{:S(2)}) collective-permute-start(bf16[1,128,1024]{2,1,0:T(8,128)(2,1)S(1)} %shard_map.100), channel_id=1, source_target_pairs={{0,32},{32,64},{64,96},{96,128},{128,160},{160,192},{192,224},{224... | collective-permute-start | bytes 786440 | tf_op jit(solution)/shard_map/ppermute | solution.py:111
  49.1 16.9 %collective-permute-start.6 = (bf16[1,128,1024]{2,1,0:T(8,128)(2,1)S(1)}, bf16[1,128,1024]{2,1,0:T(8,128)(2,1)S(1)}, u32[]{:S(2)}, u32[]{:S(2)}) collective-permute-start(bf16[1,128,1024]{2,1,0:T(8,128)(2,1)S(1)} %shard_map.98), channel_id=1, source_target_pairs={{0,224},{32,0},{64,32},{96,64},{128,96},{160,128},{192,160},{224,1... | collective-permute-start | bytes 786440 | tf_op jit(solution)/shard_map/ppermute | solution.py:111
  54.7 11.2 %collective-permute-start.2 = (bf16[1,128,1024]{2,1,0:T(8,128)(2,1)S(1)}, bf16[1,128,1024]{2,1,0:T(8,128)(2,1)S(1)}, u32[]{:S(2)}, u32[]{:S(2)}) collective-permute-start(bf16[1,128,1024]{2,1,0:T(8,128)(2,1)S(1)} %shard_map.95), channel_id=1, source_target_pairs={{0,32},{32,64},{64,96},{96,128},{128,160},{160,192},{192,224},{224... | collective-permute-start | bytes 786440 | tf_op jit(solution)/shard_map/ppermute | solution.py:111
  54.8 16.8 %collective-permute-start.17 = (bf16[1,128,1024]{2,1,0:T(8,128)(2,1)S(1)}, bf16[1,128,1024]{2,1,0:T(8,128)(2,1)S(1)}, u32[]{:S(2)}, u32[]{:S(2)}) collective-permute-start(bf16[1,128,1024]{2,1,0:T(8,128)(2,1)S(1)} %shard_map.106), channel_id=1, source_target_pairs={{0,32},{32,64},{64,96},{96,128},{128,160},{160,192},{192,224},{224... | collective-permute-start | bytes 786440 | tf_op jit(solution)/shard_map/ppermute | solution.py:111
  71.6 85.8 %copy-start = (bf16[2,128,1024]{2,1,0:T(8,128)(2,1)S(1)}, bf16[2,128,1024]{2,1,0:T(8,128)(2,1)}, u32[]{:S(2)}) copy-start(bf16[2,128,1024]{2,1,0:T(8,128)(2,1)} %root_ref.9) | copy-start | bytes 1572868
  72.5 6.5 %collective-permute-start.13 = (bf16[1,128,1024]{2,1,0:T(8,128)(2,1)S(1)}, bf16[1,128,1024]{2,1,0:T(8,128)(2,1)S(1)}, u32[]{:S(2)}, u32[]{:S(2)}) collective-permute-start(bf16[1,128,1024]{2,1,0:T(8,128)(2,1)S(1)} %shard_map.103.refs_1_), channel_id=1, source_target_pairs={{0,224},{32,0},{64,32},{96,64},{128,96},{160,128},{192,160},{224,1... | collective-permute-start | bytes 786440 | tf_op jit(solution)/shard_map/ppermute | solution.py:111
  73.9 7.2 %collective-permute-start.3 = (bf16[1,128,1024]{2,1,0:T(8,128)(2,1)S(1)}, bf16[1,128,1024]{2,1,0:T(8,128)(2,1)S(1)}, u32[]{:S(2)}, u32[]{:S(2)}) collective-permute-start(bf16[1,128,1024]{2,1,0:T(8,128)(2,1)S(1)} %shard_map.96.refs_0_), channel_id=1, source_target_pairs={{0,32},{32,64},{64,96},{96,128},{128,160},{160,192},{192,224},{224... | collective-permute-start | bytes 786440 | tf_op jit(solution)/shard_map/ppermute | solution.py:111
  121.2 12.0 %collective-permute-start.24 = (bf16[128,1024]{1,0:T(8,128)(2,1)S(1)}, bf16[128,1024]{1,0:T(8,128)(2,1)S(1)}, u32[]{:S(2)}, u32[]{:S(2)}) collective-permute-start(bf16[128,1024]{1,0:T(8,128)(2,1)S(1)} %get-tuple-element.37.rest_0_.rest_2_.rest_4_), channel_id=1, source_target_pairs={{0,32},{32,64},{64,96},{96,128},{128,160},{160,192},{192,224},{224... | collective-permute-start | bytes 786440 | tf_op jit(solution)/shard_map/ppermute | solution.py:111
  121.3 11.9 %collective-permute-start.21 = (bf16[128,1024]{1,0:T(8,128)(2,1)S(1)}, bf16[128,1024]{1,0:T(8,128)(2,1)S(1)}, u32[]{:S(2)}, u32[]{:S(2)}) collective-permute-start(bf16[128,1024]{1,0:T(8,128)(2,1)S(1)} %get-tuple-element.36.rest_1_.rest_3_.rest_5_), channel_id=1, source_target_pairs={{0,224},{32,0},{64,32},{96,64},{128,96},{160,128},{192,160},{224,1... | collective-permute-start | bytes 786440 | tf_op jit(solution)/shard_map/ppermute | solution.py:111
  124.0 13.1 %collective-permute-start.29 = (bf16[128,1024]{1,0:T(8,128)(2,1)S(1)}, bf16[128,1024]{1,0:T(8,128)(2,1)S(1)}, u32[]{:S(2)}, u32[]{:S(2)}) collective-permute-start(bf16[128,1024]{1,0:T(8,128)(2,1)S(1)} %get-tuple-element.37.rest_0_.rest_2_.rest_4_), channel_id=1, source_target_pairs={{0,224},{32,0},{64,32},{96,64},{128,96},{160,128},{192,160},{224,1... | collective-permute-start | bytes 786440 | tf_op jit(solution)/shard_map/ppermute | solution.py:111
  124.0 14.8 %collective-permute-start.32 = (bf16[128,1024]{1,0:T(8,128)(2,1)S(1)}, bf16[128,1024]{1,0:T(8,128)(2,1)S(1)}, u32[]{:S(2)}, u32[]{:S(2)}) collective-permute-start(bf16[128,1024]{1,0:T(8,128)(2,1)S(1)} %get-tuple-element.36.rest_1_.rest_3_.rest_5_), channel_id=1, source_target_pairs={{0,32},{32,64},{64,96},{96,128},{128,160},{160,192},{192,224},{224... | collective-permute-start | bytes 786440 | tf_op jit(solution)/shard_map/ppermute | solution.py:111
  133.2 11.2 %collective-permute-start.25 = (bf16[128,1024]{1,0:T(8,128)(2,1)S(1)}, bf16[128,1024]{1,0:T(8,128)(2,1)S(1)}, u32[]{:S(2)}, u32[]{:S(2)}) collective-permute-start(bf16[128,1024]{1,0:T(8,128)(2,1)S(1)} %collective-permute-done.24.rest_0_), channel_id=1, source_target_pairs={{0,32},{32,64},{64,96},{96,128},{128,160},{160,192},{192,224},{224... | collective-permute-start | bytes 786440 | tf_op jit(solution)/shard_map/ppermute | solution.py:111
  133.2 11.2 %collective-permute-start.22 = (bf16[128,1024]{1,0:T(8,128)(2,1)S(1)}, bf16[128,1024]{1,0:T(8,128)(2,1)S(1)}, u32[]{:S(2)}, u32[]{:S(2)}) collective-permute-start(bf16[128,1024]{1,0:T(8,128)(2,1)S(1)} %collective-permute-done.21.rest_1_), channel_id=1, source_target_pairs={{0,224},{32,0},{64,32},{96,64},{128,96},{160,128},{192,160},{224,1... | collective-permute-start | bytes 786440 | tf_op jit(solution)/shard_map/ppermute | solution.py:111
  137.1 25.7 %copy-start.4 = (bf16[128,1024]{1,0:T(8,128)(2,1)}, bf16[128,1024]{1,0:T(8,128)(2,1)S(1)}, u32[]{:S(2)}) copy-start(bf16[128,1024]{1,0:T(8,128)(2,1)S(1)} %collective-permute-done.29.rest_2_) | copy-start | bytes 786436
  137.1 11.3 %collective-permute-start.30 = (bf16[128,1024]{1,0:T(8,128)(2,1)S(1)}, bf16[128,1024]{1,0:T(8,128)(2,1)}, u32[]{:S(2)}, u32[]{:S(2)}) collective-permute-start(bf16[128,1024]{1,0:T(8,128)(2,1)S(1)} %collective-permute-done.29.rest_2_), channel_id=1, source_target_pairs={{0,224},{32,0},{64,32},{96,64},{128,96},{160,128},{192,160},{224,1... | collective-permute-start | bytes 786440 | tf_op jit(solution)/shard_map/ppermute | solution.py:111
  138.8 24.0 %copy-start.6 = (bf16[128,1024]{1,0:T(8,128)(2,1)}, bf16[128,1024]{1,0:T(8,128)(2,1)S(1)}, u32[]{:S(2)}) copy-start(bf16[128,1024]{1,0:T(8,128)(2,1)S(1)} %collective-permute-done.32.rest_3_) | copy-start | bytes 786436
  138.8 11.3 %collective-permute-start.33 = (bf16[128,1024]{1,0:T(8,128)(2,1)S(1)}, bf16[128,1024]{1,0:T(8,128)(2,1)}, u32[]{:S(2)}, u32[]{:S(2)}) collective-permute-start(bf16[128,1024]{1,0:T(8,128)(2,1)S(1)} %collective-permute-done.32.rest_3_), channel_id=1, source_target_pairs={{0,32},{32,64},{64,96},{96,128},{128,160},{160,192},{192,224},{224... | collective-permute-start | bytes 786440 | tf_op jit(solution)/shard_map/ppermute | solution.py:111
  144.4 11.3 %collective-permute-start.26 = (bf16[128,1024]{1,0:T(8,128)(2,1)S(1)}, bf16[128,1024]{1,0:T(8,128)(2,1)}, u32[]{:S(2)}, u32[]{:S(2)}) collective-permute-start(bf16[128,1024]{1,0:T(8,128)(2,1)S(1)} %collective-permute-done.25.rest_0_), channel_id=1, source_target_pairs={{0,32},{32,64},{64,96},{96,128},{128,160},{160,192},{192,224},{224... | collective-permute-start | bytes 786440 | tf_op jit(solution)/shard_map/ppermute | solution.py:111
  144.5 11.3 %collective-permute-start.23 = (bf16[128,1024]{1,0:T(8,128)(2,1)S(1)}, bf16[128,1024]{1,0:T(8,128)(2,1)}, u32[]{:S(2)}, u32[]{:S(2)}) collective-permute-start(bf16[128,1024]{1,0:T(8,128)(2,1)S(1)} %collective-permute-done.22.rest_1_), channel_id=1, source_target_pairs={{0,224},{32,0},{64,32},{96,64},{128,96},{160,128},{192,160},{224,1... | collective-permute-start | bytes 786440 | tf_op jit(solution)/shard_map/ppermute | solution.py:111
  148.4 11.4 %collective-permute-start.31 = (bf16[128,1024]{1,0:T(8,128)(2,1)}, bf16[128,1024]{1,0:T(8,128)(2,1)}, u32[]{:S(2)}, u32[]{:S(2)}) collective-permute-start(bf16[128,1024]{1,0:T(8,128)(2,1)} %collective-permute-done.30.rest_2_), channel_id=1, source_target_pairs={{0,224},{32,0},{64,32},{96,64},{128,96},{160,128},{192,160},{224,1... | collective-permute-start | bytes 786440 | tf_op jit(solution)/shard_map/ppermute | solution.py:111
  150.2 11.0 %collective-permute-start.34 = (bf16[128,1024]{1,0:T(8,128)(2,1)}, bf16[128,1024]{1,0:T(8,128)(2,1)}, u32[]{:S(2)}, u32[]{:S(2)}) collective-permute-start(bf16[128,1024]{1,0:T(8,128)(2,1)} %collective-permute-done.33.rest_3_), channel_id=1, source_target_pairs={{0,32},{32,64},{64,96},{96,128},{128,160},{160,192},{192,224},{224... | collective-permute-start | bytes 786440 | tf_op jit(solution)/shard_map/ppermute | solution.py:111
  155.8 9.3 %collective-permute-start.28 = (bf16[128,1024]{1,0:T(8,128)(2,1)}, bf16[128,1024]{1,0:T(8,128)(2,1)S(1)}, u32[]{:S(2)}, u32[]{:S(2)}) collective-permute-start(bf16[128,1024]{1,0:T(8,128)(2,1)} %collective-permute-done.23.rest_1_), channel_id=1, source_target_pairs={{0,224},{32,0},{64,32},{96,64},{128,96},{160,128},{192,160},{224,1... | collective-permute-start | bytes 786440 | tf_op jit(solution)/shard_map/ppermute | solution.py:111
  156.9 8.2 %collective-permute-start.27 = (bf16[128,1024]{1,0:T(8,128)(2,1)}, bf16[128,1024]{1,0:T(8,128)(2,1)S(1)}, u32[]{:S(2)}, u32[]{:S(2)}) collective-permute-start(bf16[128,1024]{1,0:T(8,128)(2,1)} %collective-permute-done.26.rest_0_), channel_id=1, source_target_pairs={{0,32},{32,64},{64,96},{96,128},{128,160},{160,192},{192,224},{224... | collective-permute-start | bytes 786440 | tf_op jit(solution)/shard_map/ppermute | solution.py:111
  159.8 33.0 %copy-start.2 = (f32[2,128,1024]{2,1,0:T(8,128)S(1)}, f32[2,128,1024]{2,1,0:T(8,128)}, u32[]{:S(2)}) copy-start(f32[2,128,1024]{2,1,0:T(8,128)} %rest_4_.1) | copy-start | bytes 3145732
  166.1 22.6 %copy-start.13 = (bf16[128,1024]{1,0:T(8,128)(2,1)}, bf16[128,1024]{1,0:T(8,128)(2,1)S(1)}, u32[]{:S(2)}) copy-start(bf16[128,1024]{1,0:T(8,128)(2,1)S(1)} %get-tuple-element.43.rest_0_) | copy-start | bytes 786436
  166.2 22.6 %copy-start.15 = (bf16[128,1024]{1,0:T(8,128)(2,1)}, bf16[128,1024]{1,0:T(8,128)(2,1)S(1)}, u32[]{:S(2)}) copy-start(bf16[128,1024]{1,0:T(8,128)(2,1)S(1)} %get-tuple-element.44.rest_1_) | copy-start | bytes 786436
  166.2 28.4 %copy-start.5 = (bf16[128,1024]{1,0:T(8,128)(2,1)S(1)}, bf16[128,1024]{1,0:T(8,128)(2,1)}, u32[]{:S(2)}) copy-start(bf16[128,1024]{1,0:T(8,128)(2,1)} %copy-done.4) | copy-start | bytes 786436
  166.2 28.4 %copy-start.7 = (bf16[128,1024]{1,0:T(8,128)(2,1)S(1)}, bf16[128,1024]{1,0:T(8,128)(2,1)}, u32[]{:S(2)}) copy-start(bf16[128,1024]{1,0:T(8,128)(2,1)} %copy-done.6) | copy-start | bytes 786436
  188.8 18.4 %all-to-all-start.3 = ((bf16[32,3,16,256]{3,2,1,0:T(8,128)(2,1)}), bf16[32,3,16,256]{3,2,1,0:T(8,128)(2,1)S(1)}, u32[]{:S(2)}, u32[]{:S(2)}) async-start(bf16[32,3,16,256]{3,2,1,0:T(8,128)(2,1)} %bitcast.27), calls=%async_computation.3 | async-start | bytes 1572864 | tf_op jit(solution)/shard_map/all_to_all | solution.py:242
  (8 other events, 52.5 us)
Sparse Core Ops, SparseCore 0:
  72.6 57.8 all-gather.2
